TPU v7x, 32 devices: a whole 2x2x4 slice. The times are simulated.
32 devices in a mesh: dp: 2 (over x), ctx: 4 (over z), exp: 4 (over y, core).
Axes of the slice: x: 2, y: 2, z: 4, core: 2. Of those that a mesh axis runs over, the one named last changes fastest.
Arguments:
- tokens: bfloat16 [8, 1024, 1024], P(('dp', 'exp'), 'ctx'), may hold values from -6 to 6
- qkv_weight: bfloat16 [1024, 3072], P(('dp', 'ctx', 'exp')), may hold values from -0.1875 to 0.1875
- out_weight: bfloat16 [1024, 1024], P(('dp', 'ctx', 'exp')), may hold values from -1 to 1
- norm1_gain: bfloat16 [1024], P(('dp', 'ctx', 'exp')), may hold values from 0.5 to 1.5
- norm1_shift: bfloat16 [1024], P(('dp', 'ctx', 'exp')), may hold values from -1.75 to 1.75
- norm2_gain: bfloat16 [1024], P(('dp', 'ctx', 'exp')), may hold values from 0.5 to 1.5
- norm2_shift: bfloat16 [1024], P(('dp', 'ctx', 'exp')), may hold values from -1.75 to 1.75
- inner_weight: bfloat16 [1024, 4096], P(('dp', 'ctx', 'exp')), may hold values from -0.1875 to 0.1875
- outer_weight: bfloat16 [4096, 1024], P(('dp', 'ctx', 'exp')), may hold values from -0.09375 to 0.09375
- router_weight: bfloat16 [1024, 4], P(('dp', 'ctx', 'exp')), may hold values from -0.09375 to 0.09375
- expert_inner: bfloat16 [4, 1024, 4096], P('exp', None, ('dp', 'ctx')), may hold values from -0.1875 to 0.1875
- expert_outer: bfloat16 [4, 4096, 1024], P('exp', ('dp', 'ctx')), may hold values from -0.375 to 0.375
- segments: int32 [8, 1024], P(('dp', 'exp')), may hold values from 0 to 2, as said below
- routes: int32 [8, 1024, 1], P(('dp', 'exp'), 'ctx'), may hold values from 0 to 3
- priority: int32 [8, 4, 256], P(('dp', 'exp'), 'ctx'), may hold values from 0 to 255, each once within a row
- cotangent: bfloat16 [8, 1024, 1024], P(('dp', 'exp'), 'ctx'), may hold values from -6 to 6
Outputs:
- output: bfloat16 [8, 1024, 1024], P(('dp', 'exp'), 'ctx')
- d_tokens: float32 [8, 1024, 1024], P(('dp', 'exp'), 'ctx')
- d_qkv_weight: float32 [1024, 3072], P(('dp', 'ctx', 'exp'))
- d_out_weight: float32 [1024, 1024], P(('dp', 'ctx', 'exp'))
- d_norm1_gain: float32 [1024], P(('dp', 'ctx', 'exp'))
- d_norm1_shift: float32 [1024], P(('dp', 'ctx', 'exp'))
- d_norm2_gain: float32 [1024], P(('dp', 'ctx', 'exp'))
- d_norm2_shift: float32 [1024], P(('dp', 'ctx', 'exp'))
- d_inner_weight: float32 [1024, 4096], P(('dp', 'ctx', 'exp'))
- d_outer_weight: float32 [4096, 1024], P(('dp', 'ctx', 'exp'))
- d_router_weight: float32 [1024, 4], P(('dp', 'ctx', 'exp'))
- d_expert_inner: float32 [4, 1024, 4096], P('exp', None, ('dp', 'ctx'))
- d_expert_outer: float32 [4, 4096, 1024], P('exp', ('dp', 'ctx'))
Inputs may be any that keep to these rules, and one draw needn't show every extreme that they name: `segments`: each sequence packs documents 0, 1 and 2 in order; document 1 starts at a position from 128 to 255 and document 2 at one from 769 to 896. `routes`: every expert is chosen by some token. `priority`: within each block of 256 positions of a sequence every number from 0 to 255 appears once.
All inputs are finite; a program needn't handle non-finite values.
Results may differ from a plain program's by a relative error of at most 0.028.
Values may be sent and summed in bfloat16 or wider, within the bound.
No kernel may reach another device: no remote copies, remote signals or barrier semaphores. Data moves between devices by JAX's collectives and lax.ppermute only.
A program may use at most 256 MiB of HBM per device.

v0:
```python
import math

import jax
import jax.numpy as jnp
from jax import lax
from jax.sharding import PartitionSpec as P

HEADS = 16
HEAD_DIM = 64


epsilon = 1e-05
neg_large = -1e30


def layer_norm(values, gain_vector, shift_vector):
    average = jnp.mean(values, axis=-1, keepdims=True)
    centred = values - average
    variance = jnp.mean(centred * centred, axis=-1, keepdims=True)
    return centred * lax.rsqrt(variance + epsilon) * gain_vector + shift_vector


def gelu_tanh(values):
    return (
        0.5
        * values
        * (1.0 + jnp.tanh(0.7978845608028654 * (values + 0.044715 * values * values * values)))
    )


def softmax_rows(values):
    highest = jnp.max(values, axis=-1, keepdims=True)
    raised = jnp.exp(values - highest)
    return raised / jnp.sum(raised, axis=-1, keepdims=True)


def low_product(left_side, right_side):
    return jnp.dot(left_side, right_side, preferred_element_type=jnp.float32)


def exact_product(left_side, right_side):
    return jnp.dot(
        left_side, right_side, preferred_element_type=jnp.float32, precision=lax.Precision.HIGHEST
    )


def per_device(
    tokens,
    qkv_weight,
    out_weight,
    norm1_gain,
    norm1_shift,
    norm2_gain,
    norm2_shift,
    inner_weight,
    outer_weight,
    router_weight,
    expert_inner,
    expert_outer,
    segments,
    routes,
    priority,
    cotangent,
):
    gathered = (
        lax.all_gather(qkv_weight, ("dp", "ctx", "exp"), axis=0, tiled=True),
        lax.all_gather(out_weight, ("dp", "ctx", "exp"), axis=0, tiled=True),
        lax.all_gather(inner_weight, ("dp", "ctx", "exp"), axis=0, tiled=True),
        lax.all_gather(outer_weight, ("dp", "ctx", "exp"), axis=0, tiled=True),
        lax.all_gather(router_weight, ("dp", "ctx", "exp"), axis=0, tiled=True),
        lax.all_gather(norm1_gain, ("dp", "ctx", "exp"), axis=0, tiled=True),
        lax.all_gather(norm1_shift, ("dp", "ctx", "exp"), axis=0, tiled=True),
        lax.all_gather(norm2_gain, ("dp", "ctx", "exp"), axis=0, tiled=True),
        lax.all_gather(norm2_shift, ("dp", "ctx", "exp"), axis=0, tiled=True),
    )
    (
        whole_qkv,
        whole_out,
        whole_inner,
        whole_outer,
        whole_router,
        gain_first,
        shift_first,
        gain_second,
        shift_second,
    ) = gathered
    local_inner, local_outer = (
        lax.all_gather(expert_inner, ("dp", "ctx"), axis=2, tiled=True),
        lax.all_gather(expert_outer, ("dp", "ctx"), axis=1, tiled=True),
    )
    token_rows = tokens.shape[1]
    model_width = tokens.shape[2]
    sequence_length = segments.shape[1]
    hidden_size = local_inner.shape[2]
    experts_here = local_inner.shape[0]
    scale_factor = 1.0 / math.sqrt(HEAD_DIM)
    block_start = lax.axis_index("ctx") * token_rows
    segment_row = segments[0]
    query_positions = block_start + jnp.arange(token_rows, dtype=jnp.int32)
    query_segments = lax.dynamic_slice_in_dim(segment_row, block_start, token_rows)
    inputs_wide = tokens[0].astype(jnp.float32)
    first_normed, first_back = jax.vjp(
        layer_norm, inputs_wide, gain_first.astype(jnp.float32), shift_first.astype(jnp.float32)
    )
    first_low = first_normed.astype(jnp.bfloat16)
    projected = low_product(first_low, whole_qkv).astype(jnp.bfloat16)
    queries_low = projected[:, :model_width]
    keys_low = projected[:, model_width : 2 * model_width]
    values_low = projected[:, 2 * model_width :]
    queries_heads = queries_low.reshape(token_rows, HEADS, HEAD_DIM)

    def block_scores(key_block, key_start):
        key_count = key_block.shape[0]
        key_positions = key_start + jnp.arange(key_count, dtype=jnp.int32)
        key_segments = lax.dynamic_slice_in_dim(segment_row, key_start, key_count)
        visible = jnp.logical_and(
            key_positions[None, :] <= query_positions[:, None],
            key_segments[None, :] == query_segments[:, None],
        )
        keys_heads = key_block.reshape(key_count, HEADS, HEAD_DIM)
        scores = (
            jnp.einsum(
                "qhd,khd->hqk", queries_heads, keys_heads, preferred_element_type=jnp.float32
            )
            * scale_factor
        )
        return (scores, visible[None], keys_heads)

    forward_start = (
        jnp.full((HEADS, token_rows), neg_large, jnp.float32),
        jnp.zeros((HEADS, token_rows), jnp.float32),
        jnp.zeros((token_rows, HEADS, HEAD_DIM), jnp.float32),
    )
    piece_pair = (
        lax.all_gather(keys_low, "ctx", axis=0, tiled=True),
        lax.all_gather(values_low, "ctx", axis=0, tiled=True),
    )
    piece_rows = piece_pair[0].shape[0]
    block_size = math.gcd(piece_rows, 256)

    def forward_step(state_now, block_number):
        best_now, total_now, accum_now = state_now
        offset_rows = block_number * block_size
        key_block = lax.dynamic_slice_in_dim(piece_pair[0], offset_rows, block_size)
        value_block = lax.dynamic_slice_in_dim(piece_pair[1], offset_rows, block_size)
        scores, visible, keys_heads = block_scores(key_block, offset_rows)
        block_best = jnp.max(jnp.where(visible, scores, neg_large), axis=2)
        best_next = jnp.maximum(best_now, block_best)
        factor = jnp.exp(best_now - best_next)
        weights = jnp.where(visible, jnp.exp(scores - best_next[:, :, None]), 0.0)
        total_next = total_now * factor + jnp.sum(weights, axis=2)
        values_heads = value_block.reshape(block_size, HEADS, HEAD_DIM)
        accum_next = accum_now * factor.T[:, :, None] + jnp.einsum(
            "hqk,khd->qhd",
            weights.astype(jnp.bfloat16),
            values_heads,
            preferred_element_type=jnp.float32,
        )
        return ((best_next, total_next, accum_next), None)

    result_state, unused_output = lax.scan(
        forward_step, forward_start, jnp.arange(piece_rows // block_size, dtype=jnp.int32)
    )
    best_final, total_final, accum_final = result_state
    attended_wide = accum_final / total_final.T[:, :, None]
    log_total = best_final + jnp.log(total_final)
    attended_low = attended_wide.reshape(token_rows, model_width).astype(jnp.bfloat16)
    residual = inputs_wide + low_product(attended_low, whole_out)
    second_normed, second_back = jax.vjp(
        layer_norm, residual, gain_second.astype(jnp.float32), shift_second.astype(jnp.float32)
    )
    second_low = second_normed.astype(jnp.bfloat16)
    hidden_dense = low_product(second_low, whole_inner)
    active_wide, gelu_back = jax.vjp(gelu_tanh, hidden_dense)
    active_low = active_wide.astype(jnp.bfloat16)
    dense_out = low_product(active_low, whole_outer)
    probabilities = softmax_rows(low_product(second_low, whole_router))
    expert_count = whole_router.shape[1]
    route_ids = routes[0, :, 0]
    order_ids = priority[0, 0]
    chosen = (route_ids[:, None] == jnp.arange(expert_count, dtype=jnp.int32)[None, :]).astype(
        jnp.float32
    )
    gate_value = jnp.sum(probabilities * chosen, axis=1)
    capacity = (9 * token_rows + 8 * expert_count - 1) // (8 * expert_count)
    same_expert = route_ids[:, None] == route_ids[None, :]
    earlier = order_ids[None, :] < order_ids[:, None]
    slot_index = jnp.sum(jnp.logical_and(same_expert, earlier).astype(jnp.int32), axis=1)
    kept_mask = slot_index < capacity
    placement_index = jnp.where(kept_mask, route_ids * capacity + slot_index, -1)
    dispatch_table = (
        jnp.arange(expert_count * capacity, dtype=jnp.int32)[:, None] == placement_index[None, :]
    ).astype(jnp.bfloat16)
    outgoing = (
        low_product(dispatch_table, second_low)
        .astype(jnp.bfloat16)
        .reshape(expert_count, capacity, model_width)
    )
    received = lax.all_to_all(outgoing, "exp", split_axis=0, concat_axis=0, tiled=True)
    item_count = received.shape[1]
    rows_total = received.shape[0]
    grouped = received.reshape(-1, experts_here, item_count, model_width)
    expert_hidden = jnp.einsum(
        "necd,edf->necf", grouped, local_inner, preferred_element_type=jnp.float32
    )
    expert_active = gelu_tanh(expert_hidden).astype(jnp.bfloat16)
    expert_result = jnp.einsum(
        "necf,efd->necd", expert_active, local_outer, preferred_element_type=jnp.float32
    ).astype(jnp.bfloat16)
    expert_result, expert_hidden, expert_active, arrived = (
        expert_result.reshape(rows_total, item_count, model_width),
        expert_hidden.reshape(rows_total, item_count, hidden_size),
        expert_active.reshape(rows_total, item_count, hidden_size),
        received,
    )
    returned = lax.all_to_all(expert_result, "exp", split_axis=0, concat_axis=0, tiled=True)
    picked = jnp.einsum(
        "st,sd->td",
        dispatch_table,
        returned.reshape(-1, model_width),
        preferred_element_type=jnp.float32,
    )
    output = residual + dense_out + gate_value[:, None] * picked
    cotangent_low = cotangent[0]
    cotangent_wide = cotangent_low.astype(jnp.float32)
    d_outer = jnp.einsum("tf,td->fd", active_low, cotangent_low, preferred_element_type=jnp.float32)
    d_active_dense = jnp.einsum(
        "td,fd->tf", cotangent_low, whole_outer, preferred_element_type=jnp.float32
    )
    d_hidden_low = gelu_back(d_active_dense)[0].astype(jnp.bfloat16)
    d_inner = jnp.einsum("td,tf->df", second_low, d_hidden_low, preferred_element_type=jnp.float32)
    d_second = jnp.einsum(
        "tf,df->td", d_hidden_low, whole_inner, preferred_element_type=jnp.float32
    )
    d_result_low = (gate_value[:, None] * cotangent_wide).astype(jnp.bfloat16)
    gradient_out = (
        low_product(dispatch_table, d_result_low)
        .astype(jnp.bfloat16)
        .reshape(expert_count, capacity, model_width)
    )
    incoming = lax.all_to_all(gradient_out, "exp", split_axis=0, concat_axis=0, tiled=True)
    grad_grouped = incoming.reshape(-1, experts_here, capacity, model_width)
    hidden_grouped = expert_hidden.reshape(-1, experts_here, capacity, hidden_size)
    active_grouped = expert_active.reshape(-1, experts_here, capacity, hidden_size)
    arrived_grouped = arrived.reshape(-1, experts_here, capacity, model_width)
    d_expert_active = jnp.einsum(
        "necd,efd->necf", grad_grouped, local_outer, preferred_element_type=jnp.float32
    )
    d_expert_hidden = jax.vjp(gelu_tanh, hidden_grouped)[1](d_expert_active)[0].astype(jnp.bfloat16)
    d_local_outer = jnp.einsum(
        "necf,necd->efd", active_grouped, grad_grouped, preferred_element_type=jnp.float32
    )
    d_local_inner = jnp.einsum(
        "necd,necf->edf", arrived_grouped, d_expert_hidden, preferred_element_type=jnp.float32
    )
    d_arrived = (
        jnp.einsum(
            "necf,edf->necd", d_expert_hidden, local_inner, preferred_element_type=jnp.float32
        )
        .astype(jnp.bfloat16)
        .reshape(arrived.shape)
    )
    sent_back = lax.all_to_all(d_arrived, "exp", split_axis=0, concat_axis=0, tiled=True)
    d_second = d_second + jnp.einsum(
        "st,sd->td",
        dispatch_table,
        sent_back.reshape(-1, model_width),
        preferred_element_type=jnp.float32,
    )
    expert_sums = (
        lax.psum_scatter(
            d_local_inner.astype(jnp.bfloat16), ("dp", "ctx"), scatter_dimension=2, tiled=True
        ).astype(jnp.float32),
        lax.psum_scatter(
            d_local_outer.astype(jnp.bfloat16), ("dp", "ctx"), scatter_dimension=1, tiled=True
        ).astype(jnp.float32),
    )
    d_gate = jnp.sum(cotangent_wide * picked, axis=1)
    d_logits = d_gate[:, None] * probabilities * (chosen - gate_value[:, None])
    d_router = exact_product(second_low.astype(jnp.float32).T, d_logits)
    d_second = d_second + exact_product(d_logits, whole_router.astype(jnp.float32).T)
    d_residual_part, d_gain_second, d_shift_second = second_back(d_second)
    d_residual = cotangent_wide + d_residual_part
    d_branch_low = d_residual.astype(jnp.bfloat16)
    d_out = jnp.einsum("td,te->de", attended_low, d_branch_low, preferred_element_type=jnp.float32)
    d_attended_low = jnp.einsum(
        "te,de->td", d_branch_low, whole_out, preferred_element_type=jnp.float32
    ).astype(jnp.bfloat16)
    grads_heads = d_attended_low.reshape(token_rows, HEADS, HEAD_DIM)
    delta_rows = jnp.sum(grads_heads.astype(jnp.float32) * attended_wide, axis=2).T
    backward_start = (
        jnp.zeros((token_rows, HEADS, HEAD_DIM), jnp.float32),
        jnp.zeros((sequence_length, 2 * model_width), jnp.float32),
    )
    backward_piece_pair = (
        lax.all_gather(keys_low, "ctx", axis=0, tiled=True),
        lax.all_gather(values_low, "ctx", axis=0, tiled=True),
    )
    piece_rows = backward_piece_pair[0].shape[0]
    backward_block_size = math.gcd(piece_rows, 256)

    def backward_step(state_now, block_number):
        d_query_now, d_keys_now = state_now
        offset_rows = block_number * backward_block_size
        key_block = lax.dynamic_slice_in_dim(
            backward_piece_pair[0], offset_rows, backward_block_size
        )
        value_block = lax.dynamic_slice_in_dim(
            backward_piece_pair[1], offset_rows, backward_block_size
        )
        scores, visible, keys_heads = block_scores(key_block, offset_rows)
        weights = jnp.where(visible, jnp.exp(scores - log_total[:, :, None]), 0.0)
        values_heads = value_block.reshape(backward_block_size, HEADS, HEAD_DIM)
        d_weights = jnp.einsum(
            "qhd,khd->hqk", grads_heads, values_heads, preferred_element_type=jnp.float32
        )
        d_scores = (weights * (d_weights - delta_rows[:, :, None])).astype(jnp.bfloat16)
        d_query_next = d_query_now + scale_factor * jnp.einsum(
            "hqk,khd->qhd", d_scores, keys_heads, preferred_element_type=jnp.float32
        )
        d_key_block = scale_factor * jnp.einsum(
            "hqk,qhd->khd", d_scores, queries_heads, preferred_element_type=jnp.float32
        )
        d_value_block = jnp.einsum(
            "hqk,qhd->khd",
            weights.astype(jnp.bfloat16),
            grads_heads,
            preferred_element_type=jnp.float32,
        )
        joined = jnp.concatenate(
            [
                d_key_block.reshape(backward_block_size, model_width),
                d_value_block.reshape(backward_block_size, model_width),
            ],
            axis=1,
        )
        current = lax.dynamic_slice_in_dim(d_keys_now, offset_rows, backward_block_size)
        d_keys_next = lax.dynamic_update_slice_in_dim(d_keys_now, current + joined, offset_rows, 0)
        return ((d_query_next, d_keys_next), None)

    result_state, unused_output = lax.scan(
        backward_step,
        backward_start,
        jnp.arange(piece_rows // backward_block_size, dtype=jnp.int32),
    )
    d_query_total, d_keys_total = result_state
    d_key_value = lax.psum_scatter(
        d_keys_total.astype(jnp.bfloat16), "ctx", scatter_dimension=0, tiled=True
    ).astype(jnp.float32)
    d_projected = jnp.concatenate(
        [d_query_total.reshape(token_rows, model_width), d_key_value], axis=1
    ).astype(jnp.bfloat16)
    d_qkv = jnp.einsum("td,te->de", first_low, d_projected, preferred_element_type=jnp.float32)
    d_first = jnp.einsum("te,de->td", d_projected, whole_qkv, preferred_element_type=jnp.float32)
    d_inputs_part, d_gain_first, d_shift_first = first_back(d_first)
    d_tokens = d_residual + d_inputs_part
    layer_sums = (
        lax.psum_scatter(d_qkv, ("dp", "ctx", "exp"), scatter_dimension=0, tiled=True),
        lax.psum_scatter(d_out, ("dp", "ctx", "exp"), scatter_dimension=0, tiled=True),
        lax.psum_scatter(d_inner, ("dp", "ctx", "exp"), scatter_dimension=0, tiled=True),
        lax.psum_scatter(d_outer, ("dp", "ctx", "exp"), scatter_dimension=0, tiled=True),
        lax.psum_scatter(d_router, ("dp", "ctx", "exp"), scatter_dimension=0, tiled=True),
        lax.psum_scatter(d_gain_first, ("dp", "ctx", "exp"), scatter_dimension=0, tiled=True),
        lax.psum_scatter(d_shift_first, ("dp", "ctx", "exp"), scatter_dimension=0, tiled=True),
        lax.psum_scatter(d_gain_second, ("dp", "ctx", "exp"), scatter_dimension=0, tiled=True),
        lax.psum_scatter(d_shift_second, ("dp", "ctx", "exp"), scatter_dimension=0, tiled=True),
    )
    return (
        output.astype(jnp.bfloat16)[None],
        d_tokens[None],
        layer_sums[0],
        layer_sums[1],
        layer_sums[5],
        layer_sums[6],
        layer_sums[7],
        layer_sums[8],
        layer_sums[2],
        layer_sums[3],
        layer_sums[4],
        expert_sums[0],
        expert_sums[1],
    )


def solution(mesh):
    in_specs = (
        P(("dp", "exp"), "ctx", None),
        P(("dp", "ctx", "exp"), None),
        P(("dp", "ctx", "exp"), None),
        P(("dp", "ctx", "exp")),
        P(("dp", "ctx", "exp")),
        P(("dp", "ctx", "exp")),
        P(("dp", "ctx", "exp")),
        P(("dp", "ctx", "exp"), None),
        P(("dp", "ctx", "exp"), None),
        P(("dp", "ctx", "exp"), None),
        P("exp", None, ("dp", "ctx")),
        P("exp", ("dp", "ctx"), None),
        P(("dp", "exp"), None),
        P(("dp", "exp"), "ctx", None),
        P(("dp", "exp"), "ctx", None),
        P(("dp", "exp"), "ctx", None),
    )
    out_specs = (
        P(("dp", "exp"), "ctx", None),
        P(("dp", "exp"), "ctx", None),
        P(("dp", "ctx", "exp"), None),
        P(("dp", "ctx", "exp"), None),
        P(("dp", "ctx", "exp")),
        P(("dp", "ctx", "exp")),
        P(("dp", "ctx", "exp")),
        P(("dp", "ctx", "exp")),
        P(("dp", "ctx", "exp"), None),
        P(("dp", "ctx", "exp"), None),
        P(("dp", "ctx", "exp"), None),
        P("exp", None, ("dp", "ctx")),
        P("exp", ("dp", "ctx"), None),
    )
    return jax.shard_map(
        per_device, mesh=mesh, in_specs=in_specs, out_specs=out_specs, check_vma=False
    )
```

profile of v0, /device:TPU:4, one launch (start us, length us, event | category | flops | bytes accessed | tf_op | source)
XLA Modules:
  0.0 1919.1 jit_solution(6907193899459035575)
XLA Ops:
  11.3 41.7 %all-reduce.9 = (bf16[1024]{0:T(1024)(128)(2,1)S(1)}, bf16[1024]{0:T(1024)(128)(2,1)S(1)}, bf16[1024]{0:T(1024)(128)(2,1)S(1)}, bf16[1024]{0:T(1024)(128)(2,1)S(1)}) all-reduce(bf16[1024]{0:T(1024)(128)(2,1)S(1)} %dynamic-update-slice.1, ...), channel_id=1, replica_groups=mesh['dp'=2,'ctx'=4,'exp'=4] {'dp','ctx','exp'}, use_global_device_ids=true, to_apply=%add.1 | all-reduce | flops 4096 | bytes 16384
  55.7 26.1 %all-gather.10.cloned.1.call-done = bf16[1024,3072]{1,0:T(8,128)(2,1)} async-done(((bf16[32,3072]{1,0:T(8,128)(2,1)}), bf16[1024,3072]{1,0:T(8,128)(2,1)}) %all-gather.10.cloned.1.call-update) | async-done | bytes 6291472 | tf_op jit(solution)/shard_map/all_gather | solution.py:66
  81.8 4.9 convolution_convert_fusion
  92.2 37.4 %all-gather = bf16[32,32,4]{1,2,0:T(4,128)(2,1)S(1)} all-gather(bf16[1,32,4]{1,2,0:T(4,128)(2,1)S(1)} %bitcast.310), channel_id=1, replica_groups=mesh['dp'=2,'ctx'=4,'exp'=4] {'dp','ctx','exp'}, dimensions={0}, use_global_device_ids=true | all-gather | bytes 8448 | tf_op jit(solution)/shard_map/all_gather | solution.py:70
  132.7 3.9 copy.69
  136.7 42.9 %all-gather.12.cloned.1.call-done = bf16[1024,1024]{1,0:T(8,128)(2,1)} async-done(((bf16[256,1024]{1,0:T(8,128)(2,1)}), bf16[1024,1024]{1,0:T(8,128)(2,1)}) %all-gather.12.cloned.1.call-update) | async-done | bytes 2097168 | tf_op jit(solution)/shard_map/all_gather | solution.py:135
  179.6 3.9 copy.68
  183.5 22.3 %while.28 = (s32[]{:T(128)}, f32[16,256]{1,0:T(8,128)S(1)}, f32[16,256]{1,0:T(8,128)S(1)}, f32[256,16,64]{0,2,1:T(8,128)S(1)}, s32[4]{0:T(128)S(1)}, /*index=5*/...) while((s32[]{:T(128)}, f32[16,256]{1,0:T(8,128)S(1)}, ...), condition=%wide.region_5.6_spmd.clone, body=%wide.region_2.5_spmd.clone.sunk | while | flops 280977920 | bytes 18882796 | solution.py:161
  206.8 30.7 %all-gather.16.cloned.1.call-done = bf16[1024,1024]{1,0:T(8,128)(2,1)} async-done(((bf16[32,1024]{1,0:T(8,128)(2,1)}), bf16[1024,1024]{1,0:T(8,128)(2,1)}) %all-gather.16.cloned.1.call-update) | async-done | bytes 2097168 | tf_op jit(solution)/shard_map/all_gather | solution.py:67
  241.8 4.7 all-to-all-start
  249.1 5.3 all-to-all-done
  254.5 6.0 all-to-all-start.2
  260.5 103.2 %all-gather.22.cloned.1.call-done = bf16[1,1024,4096]{2,1,0:T(8,128)(2,1)} async-done(((bf16[1,1024,512]{2,1,0:T(8,128)(2,1)}), bf16[1,1024,4096]{2,1,0:T(8,128)(2,1)}) %all-gather.22.cloned.1.call-update) | async-done | bytes 8388624 | tf_op jit(solution)/shard_map/all_gather | solution.py:88
  363.7 8.3 fusion.48
  372.0 116.8 %all-gather.24.cloned.1.call-done = bf16[1,4096,1024]{2,1,0:T(8,128)(2,1)} async-done(((bf16[1,512,1024]{2,1,0:T(8,128)(2,1)}), bf16[1,4096,1024]{2,1,0:T(8,128)(2,1)}) %all-gather.24.cloned.1.call-update) | async-done | bytes 8388624 | tf_op jit(solution)/shard_map/all_gather | solution.py:89
  488.8 8.9 fusion.76
  497.7 4.7 all-to-all-start.1
  502.4 9.1 fusion.68
  512.9 6.8 fusion.73
  519.8 4.2 all-to-all-start.3
  527.1 41.6 %all-gather.18.cloned.1.call-done = bf16[1024,4096]{1,0:T(8,128)(2,1)} async-done(((bf16[32,4096]{1,0:T(8,128)(2,1)}), bf16[1024,4096]{1,0:T(8,128)(2,1)}) %all-gather.18.cloned.1.call-update) | async-done | bytes 8388624 | tf_op jit(solution)/shard_map/all_gather | solution.py:68
  568.7 7.9 fusion.139
  576.6 71.2 %all-gather.20.cloned.1.call-done = bf16[4096,1024]{1,0:T(8,128)(2,1)} async-done(((bf16[128,1024]{1,0:T(8,128)(2,1)}), bf16[4096,1024]{1,0:T(8,128)(2,1)}) %all-gather.20.cloned.1.call-update) | async-done | bytes 8388624 | tf_op jit(solution)/shard_map/all_gather | solution.py:69
  647.8 8.6 fusion.63
  657.8 3.3 fusion.140
  671.7 4.3 broadcast_in_dim.95
  676.0 41.9 %while.29 = (s32[]{:T(128)}, f32[256,16,64]{0,2,1:T(8,128)S(1)}, f32[1024,2048]{0,1:T(8,128)}, s32[4]{0:T(128)S(1)}, bf16[1024,1024]{0,1:T(8,128)(2,1)}, /*index...) while((s32[]{:T(128)}, f32[256,16,64]{0,2,1:T(8,128)S(1)}, ...), condition=%wide.region_17.18_spmd.clone, body=%wide.region_16.17_spmd.clone.sunk | while | flops 683868672 | bytes 37478680 | solution.py:341
  683.3 3.3 fusion.231
  693.8 3.3 fusion.231
  704.2 3.3 fusion.231
  717.9 6.0 convert_element_type.149
  725.5 10.7 fusion.47
  736.5 9.7 fusion.46
  747.3 3.7 fusion.141
  752.0 47.4 %reduce-scatter.11.cloned.1.call-done = bf16[256,2048]{0,1:T(8,128)(2,1)} async-done(((bf16[1024,2048]{0,1:T(8,128)(2,1)}), bf16[256,2048]{0,1:T(8,128)(2,1)}) %reduce-scatter.11.cloned.1.call-update) | async-done | bytes 1048592 | tf_op jit(solution)/shard_map/reduce_scatter | solution.py:347
  799.4 7.9 fusion.98
  808.3 10.8 fusion.102
  819.4 9.7 fusion.142
  829.2 8.6 fusion.88
  837.8 93.3 %reduce-scatter.25.cloned.1.call-done = f32[32,4]{1,0:T(8,128)} async-done(((f32[1024,4]{1,0:T(8,128)}), f32[32,4]{1,0:T(8,128)}) %reduce-scatter.25.cloned.1.call-update) | async-done | bytes 528
  932.5 5.2 fusion.132
  939.2 46.4 %all-reduce.8 = (f32[1024]{0:T(1024)S(1)}, f32[1024]{0:T(1024)S(1)}, f32[1024]{0:T(1024)S(1)}, f32[1024]{0:T(1024)S(1)}) all-reduce(f32[1024]{0:T(1024)S(1)} %get-tuple-element.327, f32[1024]{0:T(1024)S(1)} %get-tuple-element.330, f32[1024]{0:T(1024)S(1)} %get-tuple-element.325, ...), channel_id=5, replica_groups=mesh['dp'=2,'ctx'=4,'exp'=4] {'dp','ctx','exp'}, use_global_device_ids=true, to_apply=%region_24.25.clone | all-reduce | flops 4096 | bytes 32768
  990.6 96.1 %reduce-scatter.23.cloned.1.call-done = bf16[1,512,1024]{2,1,0:T(8,128)(2,1)} async-done(((bf16[1,4096,1024]{2,1,0:T(8,128)(2,1)}), bf16[1,512,1024]{2,1,0:T(8,128)(2,1)}) %reduce-scatter.23.cloned.1.call-update) | async-done | bytes 1048592 | tf_op jit(solution)/shard_map/reduce_scatter | solution.py:274
  1089.5 149.6 %reduce-scatter.21.cloned.1.call-done = bf16[1,1024,512]{2,1,0:T(8,128)(2,1)} async-done(((bf16[1,1024,4096]{2,1,0:T(8,128)(2,1)}), bf16[1,1024,512]{2,1,0:T(8,128)(2,1)}) %reduce-scatter.21.cloned.1.call-update) | async-done | bytes 1048592 | tf_op jit(solution)/shard_map/reduce_scatter | solution.py:271
  1241.9 135.3 %reduce-scatter.15.cloned.1.call-done = f32[32,1024]{1,0:T(8,128)} async-done(((f32[1024,1024]{1,0:T(8,128)}), f32[32,1024]{1,0:T(8,128)}) %reduce-scatter.15.cloned.1.call-update) | async-done | bytes 131088 | tf_op jit(solution)/shard_map/reduce_scatter | solution.py:359
  1377.2 163.2 %reduce-scatter.13.cloned.1.call-done = f32[32,3072]{1,0:T(8,128)} async-done(((f32[1024,3072]{1,0:T(8,128)}), f32[32,3072]{1,0:T(8,128)}) %reduce-scatter.13.cloned.1.call-update) | async-done | bytes 393232 | tf_op jit(solution)/shard_map/reduce_scatter | solution.py:358
  1540.4 184.3 %reduce-scatter.19.cloned.1.call-done = f32[128,1024]{1,0:T(8,128)} async-done(((f32[4096,1024]{1,0:T(8,128)}), f32[128,1024]{1,0:T(8,128)}) %reduce-scatter.19.cloned.1.call-update) | async-done | bytes 524304 | tf_op jit(solution)/shard_map/reduce_scatter | solution.py:361
  1724.7 187.4 %reduce-scatter.17.cloned.1.call-done = f32[32,4096]{1,0:T(8,128)} async-done(((f32[1024,4096]{1,0:T(8,128)}), f32[32,4096]{1,0:T(8,128)}) %reduce-scatter.17.cloned.1.call-update) | async-done | bytes 524304 | tf_op jit(solution)/shard_map/reduce_scatter | solution.py:360
  (251 shorter events, 106.5 us)
Async XLA Ops:
  7.2 74.6 %all-gather.10.cloned.1.call-start = ((), (), s32[]{:S(2)}) async-start(), calls=%async_computation.12 | async-start | bytes 6488064 | tf_op jit(solution)/shard_map/all_gather | solution.py:66
  7.9 124.8 %all-gather.14.cloned.1.call-start = ((), (), s32[]{:S(2)}) async-start(), calls=%async_computation.14 | async-start | bytes 2621440 | tf_op jit(solution)/shard_map/all_gather | solution.py:136
  53.1 33.6 %copy-start.16 = (f32[1024]{0:T(1024)}, f32[1024]{0:T(1024)S(1)}, u32[]{:S(2)}) copy-start(f32[1024]{0:T(1024)S(1)} %convert_element_type.125) | copy-start | bytes 12292
  53.1 33.6 %copy-start.14 = (f32[1024]{0:T(1024)}, f32[1024]{0:T(1024)S(1)}, u32[]{:S(2)}) copy-start(f32[1024]{0:T(1024)S(1)} %convert_element_type.124) | copy-start | bytes 12292
  54.3 32.4 %copy-start.18 = (f32[256]{0:T(256)}, f32[256]{0:T(256)S(1)}, u32[]{:S(2)}) copy-start(f32[256]{0:T(256)S(1)} %broadcast_multiply_fusion.1) | copy-start | bytes 3076
  55.7 31.1 %copy-start.24 = (f32[256]{0:T(256)}, f32[256]{0:T(256)S(1)}, u32[]{:S(2)}) copy-start(f32[256]{0:T(256)S(1)} %fusion.94) | copy-start | bytes 3076
  55.7 31.1 %copy-start.22 = (f32[256]{0:T(256)}, f32[256]{0:T(256)S(1)}, u32[]{:S(2)}) copy-start(f32[256]{0:T(256)S(1)} %fusion.125) | copy-start | bytes 3076
  86.7 5.2 copy-start.20
  86.8 5.2 copy-start.26
  86.8 5.4 copy-start.27
  86.8 43.0 %copy-start.21 = (s32[1,1024]{1,0:T(1,128)S(1)}, s32[1,1024]{1,0:T(1,128)}, u32[]{:S(2)}) copy-start(s32[1,1024]{1,0:T(1,128)} %param.32) | copy-start | bytes 12292
  87.9 91.6 %all-gather.12.cloned.1.call-start = ((), (), s32[]{:S(2)}) async-start(), calls=%async_computation.13 | async-start | bytes 2621440 | tf_op jit(solution)/shard_map/all_gather | solution.py:135
  88.7 148.9 %all-gather.16.cloned.1.call-start = ((), (), s32[]{:S(2)}) async-start(), calls=%async_computation.15 | async-start | bytes 2162688 | tf_op jit(solution)/shard_map/all_gather | solution.py:67
  89.2 274.4 %all-gather.22.cloned.1.call-start = ((), (), s32[]{:S(2)}) async-start(), calls=%async_computation.18 | async-start | bytes 9437184 | tf_op jit(solution)/shard_map/all_gather | solution.py:88
  89.8 399.0 %all-gather.24.cloned.1.call-start = ((), (), s32[]{:S(2)}) async-start(), calls=%async_computation.19 | async-start | bytes 9437184 | tf_op jit(solution)/shard_map/all_gather | solution.py:89
  90.4 478.3 %all-gather.18.cloned.1.call-start = ((), (), s32[]{:S(2)}) async-start(), calls=%async_computation.16 | async-start | bytes 8650752 | tf_op jit(solution)/shard_map/all_gather | solution.py:68
  91.2 556.6 %all-gather.20.cloned.1.call-start = ((), (), s32[]{:S(2)}) async-start(), calls=%async_computation.17 | async-start | bytes 8650752 | tf_op jit(solution)/shard_map/all_gather | solution.py:69
  183.5 54.0 %copy-start = (bf16[1,256,1024]{2,1,0:T(8,128)(2,1)S(1)}, bf16[1,256,1024]{2,1,0:T(8,128)(2,1)}, u32[]{:S(2)}) copy-start(bf16[1,256,1024]{2,1,0:T(8,128)(2,1)} %param.20) | copy-start | bytes 1572868
  205.8 31.7 %copy-start.8 = (f32[256,16,64]{0,2,1:T(8,128)}, f32[256,16,64]{0,2,1:T(8,128)S(1)}, u32[]{:S(2)}) copy-start(f32[256,16,64]{0,2,1:T(8,128)S(1)} %get-tuple-element.140) | copy-start | bytes 3145732
  241.8 12.7 all-to-all-start
  254.5 243.2 %all-to-all-start.2 = ((bf16[4,72,1024]{2,1,0:T(8,128)(2,1)}), bf16[4,72,1024]{2,1,0:T(8,128)(2,1)}, u32[]{:S(2)}, u32[]{:S(2)}) async-start(bf16[4,72,1024]{2,1,0:T(8,128)(2,1)} %bitcast.295), calls=%async_computation.2 | async-start | bytes 1179648 | tf_op jit(solution)/shard_map/all_to_all | solution.py:241
  497.7 22.1 %all-to-all-start.1 = ((bf16[4,72,1024]{2,1,0:T(8,128)(2,1)}), bf16[4,72,1024]{2,1,0:T(8,128)(2,1)}, u32[]{:S(2)}, u32[]{:S(2)}) async-start(bf16[4,72,1024]{2,1,0:T(8,128)(2,1)} %fusion.76), calls=%async_computation.1 | async-start | bytes 1179648 | tf_op jit(solution)/shard_map/all_to_all | solution.py:216
  511.5 1.4 copy-start.29
  519.8 141.4 %all-to-all-start.3 = ((bf16[4,72,1024]{2,1,0:T(8,128)(2,1)}), bf16[4,72,1024]{2,1,0:T(8,128)(2,1)}, u32[]{:S(2)}, u32[]{:S(2)}) async-start(bf16[4,72,1024]{2,1,0:T(8,128)(2,1)} %fusion.73), calls=%async_computation.3 | async-start | bytes 1179648 | tf_op jit(solution)/shard_map/all_to_all | solution.py:263
  524.0 275.4 %reduce-scatter.11.cloned.1.call-start = ((), (), s32[]{:S(2)}) async-start(), calls=%async_computation.20 | async-start | bytes 5242880 | tf_op jit(solution)/shard_map/reduce_scatter | solution.py:347
  647.8 10.0 copy-start.28
  656.4 1.4 copy-start.13
  661.1 4.4 copy-start.2
  663.1 3.5 copy-start.10
  677.4 2.3 copy-start.11
  687.9 2.3 copy-start.11
  698.3 2.3 copy-start.11
  708.7 2.3 copy-start.11
  723.9 207.2 %reduce-scatter.25.cloned.1.call-start = ((), (), s32[]{:S(2)}) async-start(), calls=%async_computation.27 | async-start | bytes 540672
  725.5 361.2 %reduce-scatter.23.cloned.1.call-start = ((), (), s32[]{:S(2)}) async-start(), calls=%async_computation.26 | async-start | bytes 9437184 | tf_op jit(solution)/shard_map/reduce_scatter | solution.py:274
  736.2 502.8 %reduce-scatter.21.cloned.1.call-start = ((), (), s32[]{:S(2)}) async-start(), calls=%async_computation.25 | async-start | bytes 9437184 | tf_op jit(solution)/shard_map/reduce_scatter | solution.py:271
  746.3 631.0 %reduce-scatter.15.cloned.1.call-start = ((), (), s32[]{:S(2)}) async-start(), calls=%async_computation.22 | async-start | bytes 4325376 | tf_op jit(solution)/shard_map/reduce_scatter | solution.py:359
  751.0 48.4 %copy-start.1 = (bf16[1,256,1024]{2,1,0:T(8,128)(2,1)S(1)}, bf16[1,256,1024]{2,1,0:T(8,128)(2,1)}, u32[]{:S(2)}) copy-start(bf16[1,256,1024]{2,1,0:T(8,128)(2,1)} %param.20) | copy-start | bytes 1572868
  751.0 48.4 %copy-start.15 = (f32[1024]{0:T(1024)S(1)}, f32[1024]{0:T(1024)}, u32[]{:S(2)}) copy-start(f32[1024]{0:T(1024)} %copy-done.14) | copy-start | bytes 12292
  751.0 48.4 %copy-start.17 = (f32[1024]{0:T(1024)S(1)}, f32[1024]{0:T(1024)}, u32[]{:S(2)}) copy-start(f32[1024]{0:T(1024)} %copy-done.16) | copy-start | bytes 12292
  751.0 48.4 %copy-start.19 = (f32[256]{0:T(256)S(1)}, f32[256]{0:T(256)}, u32[]{:S(2)}) copy-start(f32[256]{0:T(256)} %copy-done.18) | copy-start | bytes 3076
  751.0 48.4 %copy-start.23 = (f32[256]{0:T(256)S(1)}, f32[256]{0:T(256)}, u32[]{:S(2)}) copy-start(f32[256]{0:T(256)} %copy-done.22) | copy-start | bytes 3076
  751.0 789.4 %reduce-scatter.13.cloned.1.call-start = ((), (), s32[]{:S(2)}) async-start(), calls=%async_computation.21 | async-start | bytes 12976128 | tf_op jit(solution)/shard_map/reduce_scatter | solution.py:358
  807.3 917.4 %reduce-scatter.19.cloned.1.call-start = ((), (), s32[]{:S(2)}) async-start(), calls=%async_computation.24 | async-start | bytes 17301504 | tf_op jit(solution)/shard_map/reduce_scatter | solution.py:361
  819.1 1093.0 %reduce-scatter.17.cloned.1.call-start = ((), (), s32[]{:S(2)}) async-start(), calls=%async_computation.23 | async-start | bytes 17301504 | tf_op jit(solution)/shard_map/reduce_scatter | solution.py:360
  829.2 103.3 %copy-start.9 = (bf16[256,16,64]{0,2,1:T(8,128)(2,1)S(1)}, bf16[256,16,64]{0,2,1:T(8,128)(2,1)}, u32[]{:S(2)}) copy-start(bf16[256,16,64]{0,2,1:T(8,128)(2,1)} %convert.5) | copy-start | bytes 1572868
  932.5 5.2 copy-start.25
  932.5 55.4 %copy-start.5 = (f32[256,1024]{1,0:T(8,128)S(1)}, f32[256,1024]{1,0:T(8,128)}, u32[]{:S(2)}) copy-start(f32[256,1024]{1,0:T(8,128)} %copy-done.4) | copy-start | bytes 3145732
  (5 other events, 4.9 us)
Sparse Core Ops, SparseCore 0:
  10.9 70.8 all-gather.9
  88.0 44.6 all-gather.13
  134.9 44.6 all-gather.11
  182.3 55.1 all-gather.15
  239.4 124.2 all-gather.21
  365.7 123.1 all-gather.23
  491.7 76.9 all-gather.17
  571.6 76.1 all-gather.19
  724.0 75.3 reduce-scatter.10
  802.1 128.9 reduce-scatter.24
  934.8 151.8 reduce-scatter.22
  1090.6 148.4 reduce-scatter.20
  1241.9 135.2 reduce-scatter.14
  1383.7 156.6 reduce-scatter.12
  1543.2 181.4 reduce-scatter.18
  1727.5 184.5 reduce-scatter.16
where the time goes:
time: 1930 us; the launch traced here: 1920 us
  waiting for transfers between devices  1500 us (78%)
  matrix products  164 us (8%)
  blocking collectives  126 us (7%)
  local copies, waits for them, and re-layouts  45.8 us (2%)
  other arithmetic  40.1 us (2%)
  starting transfers between devices  21 us (1%)
    reduce_scatter x1, waiting for transfers between devices, per_device(): lax.psum_scatter(d_inner, ('dp', 'ctx', 'exp'), scatter_dimension=0, tile...  187 us
    reduce_scatter x1, waiting for transfers between devices, per_device(): lax.psum_scatter(d_outer, ('dp', 'ctx', 'exp'), scatter_dimension=0, tile...  184 us
    reduce_scatter x1, waiting for transfers between devices, per_device(): lax.psum_scatter(d_qkv, ('dp', 'ctx', 'exp'), scatter_dimension=0, tiled=...  163 us
    reduce_scatter x1, waiting for transfers between devices, per_device(): lax.psum_scatter(d_local_inner.astype(jnp.bfloat16), ('dp', 'ctx'), scatt...  150 us
    reduce_scatter x1, waiting for transfers between devices, per_device(): lax.psum_scatter(d_out, ('dp', 'ctx', 'exp'), scatter_dimension=0, tiled=...  135 us
    all_gather x1, waiting for transfers between devices, per_device(): lax.all_gather(expert_outer, ('dp', 'ctx'), axis=1, tiled=True)  117 us
    all_gather x1, waiting for transfers between devices, per_device(): lax.all_gather(expert_inner, ('dp', 'ctx'), axis=2, tiled=True)  103 us
    unnamed x17, waiting for transfers between devices  97.8 us
  transfers between devices with their start and end apart: 20, of which 17 were waited for; matrix products, arithmetic and copies ran while one was open for 9% of the time, Pallas kernels for 0%

commit v1 on v0

v1 whole, which is shorter than its diff:
```python
import functools
import math

import jax
import jax.numpy as jnp
from jax import lax
from jax.experimental import pallas as pl
from jax.experimental.pallas import tpu as pltpu
from jax.sharding import PartitionSpec as P

HEADS = 16
HEAD_DIM = 64
AXES = ("dp", "ctx", "exp")
EPS = 1e-05
NEG = -1e30
GELU_A = 0.7978845608028654
GELU_B = 0.044715
F32 = jnp.float32
BF16 = jnp.bfloat16


def dot(a, b):
    return jnp.dot(a, b, preferred_element_type=F32)


def dot_nt(a, b):
    return lax.dot_general(a, b, (((1,), (1,)), ((), ())), preferred_element_type=F32)


def dot_tn(a, b):
    return lax.dot_general(a, b, (((0,), (0,)), ((), ())), preferred_element_type=F32)


def norm_parts(z):
    average = jnp.mean(z, axis=-1, keepdims=True)
    centred = z - average
    scale = lax.rsqrt(jnp.mean(centred * centred, axis=-1, keepdims=True) + EPS)
    return centred * scale, scale


def norm_back(grad, unit, scale, gain):
    w = grad * gain
    return scale * (
        w
        - jnp.mean(w, axis=-1, keepdims=True)
        - unit * jnp.mean(w * unit, axis=-1, keepdims=True)
    )


def gelu_pair(u):
    t = jnp.tanh(GELU_A * (u + GELU_B * u * u * u))
    value = 0.5 * u * (1.0 + t)
    slope = 0.5 * (1.0 + t) + 0.5 * u * (1.0 - t * t) * GELU_A * (1.0 + 3.0 * GELU_B * u * u)
    return value, slope


def softmax_rows(v):
    raised = jnp.exp(v - jnp.max(v, axis=-1, keepdims=True))
    return raised / jnp.sum(raised, axis=-1, keepdims=True)


def attention_fwd_kernel(block, q_ref, k_ref, v_ref, segrow_ref, segcol_ref, o_ref):
    length = q_ref.shape[0]
    scale = 1.0 / math.sqrt(HEAD_DIM)
    first_half = lax.broadcasted_iota(jnp.int32, (block, 2 * HEAD_DIM), 1) < HEAD_DIM
    for i in range(length // block):
        ext = (i + 1) * block
        rows = pl.ds(i * block, block)
        q = q_ref[rows, :]
        k = k_ref[pl.ds(0, ext), :]
        v = v_ref[pl.ds(0, ext), :]
        qpos = lax.broadcasted_iota(jnp.int32, (block, ext), 0) + i * block
        kpos = lax.broadcasted_iota(jnp.int32, (block, ext), 1)
        visible = jnp.logical_and(
            kpos <= qpos, segcol_ref[rows, :] == segrow_ref[:, pl.ds(0, ext)]
        )
        outs = []
        for half in range(2):
            mine = first_half if half == 0 else jnp.logical_not(first_half)
            qh = jnp.where(mine, q, jnp.zeros_like(q))
            s = jnp.where(visible, dot_nt(qh, k) * scale, NEG)
            p = jnp.exp(s - jnp.max(s, axis=1, keepdims=True))
            total = jnp.sum(p, axis=1, keepdims=True)
            outs.append(dot(p.astype(BF16), v) / total)
        o_ref[rows, :] = jnp.where(first_half, outs[0], outs[1]).astype(o_ref.dtype)


def attention_bwd_kernel(
    block, q_ref, k_ref, v_ref, do_ref, segrow_ref, segcol_ref, dq_ref, dk_ref, dv_ref, dk_acc, dv_acc
):
    length = q_ref.shape[0]
    scale = 1.0 / math.sqrt(HEAD_DIM)
    first_half = lax.broadcasted_iota(jnp.int32, (block, 2 * HEAD_DIM), 1) < HEAD_DIM
    dk_acc[...] = jnp.zeros_like(dk_acc)
    dv_acc[...] = jnp.zeros_like(dv_acc)
    for i in range(length // block):
        ext = (i + 1) * block
        rows = pl.ds(i * block, block)
        keys = pl.ds(0, ext)
        q = q_ref[rows, :]
        do = do_ref[rows, :]
        k = k_ref[keys, :]
        v = v_ref[keys, :]
        qpos = lax.broadcasted_iota(jnp.int32, (ext, block), 1) + i * block
        kpos = lax.broadcasted_iota(jnp.int32, (ext, block), 0)
        visible = jnp.logical_and(kpos <= qpos, segcol_ref[keys, :] == segrow_ref[:, rows])
        dq = []
        for half in range(2):
            mine = first_half if half == 0 else jnp.logical_not(first_half)
            qh = jnp.where(mine, q, jnp.zeros_like(q))
            doh = jnp.where(mine, do, jnp.zeros_like(do))
            s = jnp.where(visible, dot_nt(k, qh) * scale, NEG)
            p = jnp.exp(s - jnp.max(s, axis=0, keepdims=True))
            p = p * (1.0 / jnp.sum(p, axis=0, keepdims=True))
            dp = dot_nt(v, doh)
            delta = jnp.sum(p * dp, axis=0, keepdims=True)
            ds = (p * (dp - delta)).astype(BF16)
            dv_acc[keys, :] += dot(p.astype(BF16), doh)
            dk_acc[keys, :] += dot(ds, qh)
            dq.append(dot_tn(ds, k))
        dq_ref[rows, :] = (jnp.where(first_half, dq[0], dq[1]) * scale).astype(dq_ref.dtype)
    dk_ref[...] = (dk_acc[...] * scale).astype(dk_ref.dtype)
    dv_ref[...] = dv_acc[...].astype(dv_ref.dtype)


def attention_fwd(qkv, segs, block):
    length, width3 = qkv.shape
    width = width3 // 3
    pair = 2 * HEAD_DIM
    steps = width // pair
    return pl.pallas_call(
        functools.partial(attention_fwd_kernel, block),
        grid=(steps,),
        in_specs=[
            pl.BlockSpec((length, pair), lambda p: (0, p)),
            pl.BlockSpec((length, pair), lambda p: (0, steps + p)),
            pl.BlockSpec((length, pair), lambda p: (0, 2 * steps + p)),
            pl.BlockSpec((1, length), lambda p: (0, 0)),
            pl.BlockSpec((length, 1), lambda p: (0, 0)),
        ],
        out_specs=pl.BlockSpec((length, pair), lambda p: (0, p)),
        out_shape=jax.ShapeDtypeStruct((length, width), BF16),
        compiler_params=pltpu.CompilerParams(vmem_limit_bytes=48 * 1024 * 1024),
        cost_estimate=pl.CostEstimate(
            flops=8 * length * length * width, bytes_accessed=8 * length * width,
            transcendentals=length * length * width // HEAD_DIM // 2,
        ),
    )(qkv, qkv, qkv, segs[None, :], segs[:, None])


def attention_bwd(qkv, d_out, segs, block):
    length, width3 = qkv.shape
    width = width3 // 3
    pair = 2 * HEAD_DIM
    steps = width // pair
    out = jax.ShapeDtypeStruct((length, width), BF16)
    spec = pl.BlockSpec((length, pair), lambda p: (0, p))
    return pl.pallas_call(
        functools.partial(attention_bwd_kernel, block),
        grid=(steps,),
        in_specs=[
            spec,
            pl.BlockSpec((length, pair), lambda p: (0, steps + p)),
            pl.BlockSpec((length, pair), lambda p: (0, 2 * steps + p)),
            spec,
            pl.BlockSpec((1, length), lambda p: (0, 0)),
            pl.BlockSpec((length, 1), lambda p: (0, 0)),
        ],
        out_specs=[spec, spec, spec],
        out_shape=[out, out, out],
        scratch_shapes=[pltpu.VMEM((length, pair), F32), pltpu.VMEM((length, pair), F32)],
        compiler_params=pltpu.CompilerParams(vmem_limit_bytes=48 * 1024 * 1024),
        cost_estimate=pl.CostEstimate(
            flops=20 * length * length * width, bytes_accessed=14 * length * width,
            transcendentals=length * length * width // HEAD_DIM // 2,
        ),
    )(qkv, qkv, qkv, d_out, segs[None, :], segs[:, None])


def solution(mesh):
    nd, nc, ne = (mesh.shape[a] for a in AXES)
    ndev = nd * nc * ne
    bits_of = lambda n: [1 << b for b in range(n.bit_length() - 1)]
    low_bits, all_bits = bits_of(nc), bits_of(ne)
    high_bits = [b for b in all_bits if b not in low_bits]


    def send(x, target):
        pairs = []
        for d in range(nd):
            for c in range(nc):
                for e in range(ne):
                    to = target(d, c, e)
                    if to is not None:
                        pairs.append(((d * nc + c) * ne + e, (to[0] * nc + to[1]) * ne + to[2]))
        return lax.ppermute(x, AXES, pairs)

    def swap_exp(x, bit):
        return send(x, lambda d, c, e: (d, c, e ^ bit))

    def swap_dp(x):
        return send(x, lambda d, c, e: (d ^ 1, c, e))

    def swap_seq(x):
        return send(x, lambda d, c, e: (d, e % nc, e - e % nc + c))

    def my_bit(bit):
        return (lax.axis_index("exp") // bit) % 2

    def ordered(mine, other, index, axis):
        return jnp.where(
            index == 0, jnp.stack([mine, other], axis), jnp.stack([other, mine], axis)
        )

    def gather_exp(x, bits):
        out = x[None]
        for bit in reversed(bits):
            out = ordered(out, swap_exp(out, bit), my_bit(bit), 1)
            out = out.reshape((-1,) + x.shape)
        return out

    def gather_exp_rel(x, bits):
        out = x[None]
        for bit in reversed(bits):
            out = jnp.stack([out, swap_exp(out, bit)], 1).reshape((-1,) + x.shape)
        return out

    def split_bit(x, position, count):
        shape = x.shape
        return x.reshape((shape[0] >> (position + 1), 2, 1 << position) + shape[1:])

    def scatter_exp_rel(parts, bits):
        for bit in bits:
            pairs = parts.reshape((-1, 2) + parts.shape[1:])
            parts = pairs[:, 0].astype(F32) + swap_exp(pairs[:, 1].astype(BF16), bit).astype(F32)
        return parts[0]

    def scatter_exp(parts, bits):
        for bit in bits:
            pairs = parts.reshape((-1, 2) + parts.shape[1:])
            mine = my_bit(bit)
            keep = lax.dynamic_index_in_dim(pairs, mine, 1, keepdims=False)
            away = lax.dynamic_index_in_dim(pairs, 1 - mine, 1, keepdims=False)
            parts = keep.astype(F32) + swap_exp(away.astype(BF16), bit).astype(F32)
        return parts[0]

    def trade_exp_rel(parts, bits):
        for position, bit in enumerate(bits):
            pairs = split_bit(parts, position, len(bits))
            parts = jnp.stack([pairs[:, 0], swap_exp(pairs[:, 1], bit)], 1).reshape(parts.shape)
        return parts

    def trade_exp(parts, bits):
        for position, bit in enumerate(bits):
            pairs = split_bit(parts, position, len(bits))
            mine = my_bit(bit)
            keep = lax.dynamic_index_in_dim(pairs, mine, 1, keepdims=False)
            away = lax.dynamic_index_in_dim(pairs, 1 - mine, 1, keepdims=False)
            parts = ordered(keep, swap_exp(away, bit), mine, 1).reshape(parts.shape)
        return parts

    def line_steps(x):
        below, above, up, down = [], [], x, x
        for k in range(1, nc):
            up = send(up, lambda d, c, e: (d, c + 1, e) if k - 1 <= c < nc - 1 else None)
            down = send(down, lambda d, c, e: (d, c - 1, e) if 0 < c <= nc - k else None)
            below.append(up)
            above.append(down)
        return below, above

    def line_order(own, below, above):
        stack = jnp.stack(below[::-1] + [own] + above)
        return lax.dynamic_slice_in_dim(stack, nc - 1 - lax.axis_index("ctx"), nc)

    def gather_line(x):
        below, above = line_steps(x)
        return line_order(x, below, above)

    def gather_plane(x):
        below, above = line_steps(x)
        mine = line_order(x, below, above)
        other = line_order(
            swap_dp(x),
            [send(v, lambda d, c, e: (d ^ 1, c, e) if c >= k + 1 else None) for k, v in enumerate(below)],
            [send(v, lambda d, c, e: (d ^ 1, c, e) if c < nc - 1 - k else None) for k, v in enumerate(above)],
        )
        return ordered(mine, other, lax.axis_index("dp"), 0)

    def scatter_line(parts):
        c_here = lax.axis_index("ctx")

        def part(j):
            return lax.dynamic_index_in_dim(parts, jnp.clip(j, 0, nc - 1), 0, keepdims=False)

        up = down = None
        for t in range(1, nc):
            away = nc - t
            high, low = part(c_here + away), part(c_here - away)
            if up is not None:
                high = high.astype(F32) + up.astype(F32)
                low = low.astype(F32) + down.astype(F32)
            up = send(high.astype(BF16), lambda d, c, e: (d, c + 1, e) if c + away < nc else None)
            down = send(low.astype(BF16), lambda d, c, e: (d, c - 1, e) if c - away >= 0 else None)
        return part(c_here).astype(F32) + up.astype(F32) + down.astype(F32)

    def scatter_plane(parts):
        d_here = lax.axis_index("dp")
        keep = lax.dynamic_index_in_dim(parts, d_here, 0, keepdims=False)
        away = lax.dynamic_index_in_dim(parts, 1 - d_here, 0, keepdims=False)
        return scatter_line(keep.astype(F32) + swap_dp(away.astype(BF16)).astype(F32))

    def per_device(
        tokens, qkv_weight, out_weight, norm1_gain, norm1_shift, norm2_gain, norm2_shift,
        inner_weight, outer_weight, router_weight, expert_inner, expert_outer,
        segments, routes, priority, cotangent,
    ):
        rows, width = tokens.shape[1:]
        length = segments.shape[1]
        rw = qkv_weight.shape[0]
        ff_rows = outer_weight.shape[0]
        nplane = nd * nc
        e_here = lax.axis_index("exp")
        group = width // nc

        x_low = swap_seq(tokens[0])
        ints = jnp.concatenate([segments[0], routes[0, :, 0], priority[0, 0]])
        ints = swap_seq(ints.reshape(-1, 128)).reshape(-1)
        segs, route, order = ints[:length], ints[length : length + rows], ints[length + rows :]

        small = jnp.concatenate(
            [norm1_gain, norm1_shift, norm2_gain, norm2_shift, router_weight.reshape(-1)]
        )
        small = lax.all_to_all(
            jnp.broadcast_to(small[None], (ndev,) + small.shape), AXES, 0, 0, tiled=True
        )
        gain1, shift1, gain2, shift2 = (
            small[:, i * rw : (i + 1) * rw].reshape(width).astype(F32) for i in range(4)
        )
        router = small[:, 4 * rw :].reshape(width, ne)

        qkv_part = jnp.moveaxis(qkv_weight.reshape(rw, 3, nc, group), 2, 0)
        qkv_part = trade_exp(qkv_part.reshape(nc, rw, 3 * group), low_bits)
        qkv_part = gather_exp(qkv_part.reshape(nc * rw, 3 * group), high_bits)
        qkv_rows = width // nplane
        qkv_flat = qkv_part.reshape(-1, width)
        bundle = gather_plane(jnp.concatenate([qkv_flat, out_weight]))
        w_qkv = bundle[:, :, : qkv_flat.shape[0]].reshape(width, 3 * group)
        w_out = gather_exp(bundle[:, :, qkv_flat.shape[0] :], all_bits)
        w_out = jnp.moveaxis(w_out, 0, 2).reshape(width, width)

        inner_part = jnp.moveaxis(inner_weight.reshape(rw, nplane, ne, ff_rows), 2, 0)
        inner_part = trade_exp(inner_part.reshape(ne, rw, nplane * ff_rows), all_bits)
        inner_flat = inner_part.reshape(-1, width)
        bundle = gather_plane(jnp.concatenate([inner_flat, outer_weight]))
        ff = nplane * ff_rows
        w_inner = bundle[:, :, : inner_flat.shape[0]].reshape(width, ff)
        w_outer = bundle[:, :, inner_flat.shape[0] :].reshape(ff, width)

        e_in_own, e_out_own = expert_inner[0], expert_outer[0]
        e_in = jnp.concatenate([e_in_own, swap_dp(e_in_own)], axis=1)
        e_out = jnp.concatenate([e_out_own, swap_dp(e_out_own)], axis=0)
        half = e_out_own.shape[0]

        x = x_low.astype(F32)
        unit1, scale1 = norm_parts(x)
        normed = (unit1 * gain1 + shift1).astype(BF16)
        normed_all = gather_exp(normed, low_bits).reshape(length, width)
        qkv = dot(normed_all, w_qkv).astype(BF16)
        mixed = attention_fwd(qkv, segs, rows)
        attended = trade_exp(mixed.reshape(nc, rows, group), low_bits)
        attended = jnp.moveaxis(attended, 0, 1).reshape(rows, width)
        residual = x + dot(attended, w_out)
        unit2, scale2 = norm_parts(residual)
        normed2 = (unit2 * gain2 + shift2).astype(BF16)

        cot_low = swap_seq(cotangent[0])
        cot = cot_low.astype(F32)
        capacity = (9 * rows + 8 * ne - 1) // (8 * ne)
        same = route[:, None] == route[None, :]
        earlier = order[None, :] < order[:, None]
        slot = jnp.sum(jnp.logical_and(same, earlier).astype(jnp.int32), axis=1)
        place = jnp.where(slot < capacity, (route ^ e_here) * capacity + slot, -1)
        slots = ne * capacity
        table = (jnp.arange(slots, dtype=jnp.int32)[:, None] == place[None, :]).astype(BF16)

        def to_experts(v):
            out = dot(table, v).astype(BF16).reshape(ne, capacity, width)
            out = trade_exp_rel(out, all_bits).reshape(slots, width)
            return gather_line(out).reshape(nc * slots, width)

        def from_experts(v):
            back = scatter_line(v.reshape(nc, slots, width)).astype(BF16)
            back = trade_exp_rel(back.reshape(ne, capacity, width), all_bits)
            return dot_tn(table, back.reshape(slots, width))

        e_cot = to_experts(cot_low)
        e_x = to_experts(normed2)

        cot_all = gather_exp_rel(cot_low, all_bits).reshape(ne * rows, width)
        n2_all = gather_exp_rel(normed2, all_bits).reshape(ne * rows, width)
        act, slope = gelu_pair(dot(n2_all, w_inner))
        act = act.astype(BF16)
        d_hidden = (dot_nt(cot_all, w_outer) * slope).astype(BF16)
        dense_part = dot(act, w_outer).reshape(ne, rows, width)
        d_n2_part = dot_nt(d_hidden, w_inner).reshape(ne, rows, width)
        dense = scatter_exp_rel(dense_part, all_bits)
        d_n2_dense = scatter_exp_rel(d_n2_part, all_bits)
        d_outer = dot_tn(act, cot_all)
        d_inner = dot_tn(n2_all, d_hidden)

        e_probs = softmax_rows(dot(e_x, router))
        mine = (jnp.arange(ne, dtype=jnp.int32) == e_here).astype(F32)[None, :]
        e_gate = jnp.sum(e_probs * mine, axis=1, keepdims=True)
        e_grad = (e_gate * e_cot.astype(F32)).astype(BF16)
        e_act, e_slope = gelu_pair(dot(e_x, e_in))
        e_act = e_act.astype(BF16)
        e_result = dot(e_act, e_out)
        d_e_hidden = (dot_nt(e_grad, e_out) * e_slope).astype(BF16)
        d_gate = jnp.sum(e_cot.astype(F32) * e_result, axis=1, keepdims=True)
        d_logits = d_gate * e_probs * (mine - e_gate)
        d_e_x = dot_nt(d_e_hidden, e_in) + dot_nt(d_logits, router.astype(F32))
        d_router = dot_tn(e_x.astype(F32), d_logits)
        d_e_out = dot_tn(e_act, e_grad)
        d_e_in = dot_tn(e_x, d_e_hidden)
        g_e_in = d_e_in[:, :half] + swap_dp(d_e_in[:, half:].astype(BF16)).astype(F32)
        g_e_out = d_e_out[:half] + swap_dp(d_e_out[half:].astype(BF16)).astype(F32)

        d_n2 = d_n2_dense + from_experts(d_e_x)
        picked = from_experts(e_result)
        probs = softmax_rows(dot(normed2, router))
        chosen = (route[:, None] == jnp.arange(ne, dtype=jnp.int32)[None, :]).astype(F32)
        gate = jnp.sum(probs * chosen, axis=1, keepdims=True)
        output = swap_seq((residual + dense + gate * picked).astype(BF16))

        d_gain2 = jnp.sum(d_n2 * unit2, axis=0)
        d_shift2 = jnp.sum(d_n2, axis=0)
        d_residual = cot + norm_back(d_n2, unit2, scale2, gain2)
        d_branch = d_residual.astype(BF16)
        d_out = dot_tn(attended, d_branch)
        d_att = dot_nt(d_branch, w_out).astype(BF16)
        d_att = jnp.moveaxis(d_att.reshape(rows, nc, group), 1, 0)
        d_mixed = trade_exp(d_att, low_bits).reshape(length, group)
        d_qkv = jnp.concatenate(attention_bwd(qkv, d_mixed, segs, rows), axis=1)
        d_normed = dot_nt(d_qkv, w_qkv).reshape(nc, rows, width)
        d_normed = scatter_exp(d_normed, low_bits)
        d_w_qkv = dot_tn(normed_all, d_qkv)
        d_gain1 = jnp.sum(d_normed * unit1, axis=0)
        d_shift1 = jnp.sum(d_normed, axis=0)
        d_tokens = d_residual + norm_back(d_normed, unit1, scale1, gain1)
        d_tokens = swap_seq(d_tokens.astype(BF16)).astype(F32)

        bundle = jnp.concatenate(
            [d_inner.reshape(nd, nc, -1, width), d_outer.reshape(nd, nc, -1, width)], axis=2
        )
        bundle = scatter_plane(bundle)
        g_outer = bundle[inner_flat.shape[0] :]
        g_inner = bundle[: inner_flat.shape[0]].astype(BF16).reshape(ne, rw, ff)
        g_inner = trade_exp(g_inner, all_bits).reshape(ne, rw, nplane, ff_rows)
        g_inner = jnp.transpose(g_inner, (1, 2, 0, 3)).reshape(rw, -1).astype(F32)

        d_out = jnp.moveaxis(d_out.reshape(nplane, ne, rw, width), 1, 0)
        d_out = scatter_exp(d_out, all_bits).reshape(nd, nc, rw, width)
        bundle = jnp.concatenate([d_w_qkv.reshape(nd, nc, -1, width), d_out], axis=2)
        bundle = scatter_plane(bundle)
        g_out = bundle[qkv_flat.shape[0] :]
        g_qkv = bundle[: qkv_flat.shape[0]].reshape(-1, nc * rw, 3 * group)
        g_qkv = scatter_exp(g_qkv, high_bits).astype(BF16).reshape(nc, rw, 3 * group)
        g_qkv = trade_exp(g_qkv, low_bits).reshape(nc, rw, 3, group)
        g_qkv = jnp.transpose(g_qkv, (1, 2, 0, 3)).reshape(rw, 3 * width).astype(F32)

        small = jnp.concatenate([jnp.stack([d_gain1, d_shift1, d_gain2, d_shift2], 1), d_router], 1)
        small = lax.all_to_all(small.reshape(ndev, -1), AXES, 0, 0, tiled=True)
        small = jnp.sum(small, axis=0).reshape(rw, 4 + ne)

        return (
            output[None], d_tokens[None], g_qkv, g_out,
            small[:, 0], small[:, 1], small[:, 2], small[:, 3],
            g_inner, g_outer, small[:, 4:], g_e_in[None], g_e_out[None],
        )

    rest = ("dp", "ctx", "exp")
    seq = P(("dp", "exp"), "ctx", None)
    in_specs = (
        seq, P(rest, None), P(rest, None), P(rest), P(rest), P(rest), P(rest),
        P(rest, None), P(rest, None), P(rest, None),
        P("exp", None, ("dp", "ctx")), P("exp", ("dp", "ctx"), None),
        P(("dp", "exp"), None), seq, seq, seq,
    )
    out_specs = (
        seq, seq, P(rest, None), P(rest, None), P(rest), P(rest), P(rest), P(rest),
        P(rest, None), P(rest, None), P(rest, None),
        P("exp", None, ("dp", "ctx")), P("exp", ("dp", "ctx"), None),
    )
    return jax.shard_map(
        per_device, mesh=mesh, in_specs=in_specs, out_specs=out_specs, check_vma=False
    )
```

time: 1930 us -> 743 us (0.38)
  waiting for transfers between devices: 1500 us -> 251 us
  starting transfers between devices: 21 us -> 218 us
  blocking collectives: 126 us -> 0 us
  matrix products: 164 us -> 77 us
  local copies, waits for them, and re-layouts: 45.8 us -> 101 us
  Pallas kernels: 0 us -> 21.3 us
    reduce_scatter x7 -> x0, waiting for transfers between devices: 963 us -> none  [the longest x1 187 us: per_device(): lax.psum_scatter(d_inner, ('dp', 'ctx', 'exp'), scatter_dimension=0, tile...]
    all_gather x8 -> x0, waiting for transfers between devices: 435 us -> none  [the longest x1 117 us: per_device(): lax.all_gather(expert_outer, ('dp', 'ctx'), axis=1, tiled=True)]
    ppermute x0 -> x109, waiting for transfers between devices: none -> 251 us  [send(): return lax.ppermute(x, AXES, pairs)]
    ppermute x0 -> x109, starting transfers between devices: none -> 207 us  [send(): return lax.ppermute(x, AXES, pairs)]
    unnamed x17 -> x0, waiting for transfers between devices: 97.8 us -> none
    unnamed x2 -> x0, blocking collectives: 88.1 us -> none
    dot_general x52 -> x26, matrix products: 163 us -> 77 us  [the longest x9 27.9 us: dot_tn(): lax.dot_general(a, b, (((0,), (0,)), ((), ())), preferred_element_type=F32)]
    all_gather x1 -> x0, blocking collectives: 37.4 us -> none  [per_device(): lax.all_gather(router_weight, ('dp', 'ctx', 'exp'), axis=0, tiled=True)]
  transfers between devices with their start and end apart: 20 -> 111, of which waited for: 17 -> 36; matrix products, arithmetic and copies ran while one was open for 9% -> 30% of each run, Pallas kernels for 0% -> 3%
where the time goes in v1:
time: 743 us; the launch traced here: 731 us
  waiting for transfers between devices  251 us (34%)
  starting transfers between devices  218 us (29%)
  local copies, waits for them, and re-layouts  101 us (14%)
  matrix products  77 us (10%)
  other arithmetic  58.6 us (8%)
  Pallas kernels  21.3 us (3%)
    ppermute x109, waiting for transfers between devices, send(): return lax.ppermute(x, AXES, pairs)  251 us
    ppermute x109, starting transfers between devices, send(): return lax.ppermute(x, AXES, pairs)  207 us
    unnamed x191, local copies, waits for them, and re-layouts  31.5 us
    dot_general x9, matrix products, dot_tn(): lax.dot_general(a, b, (((0,), (0,)), ((), ())), preferred_element_type=F32)  27.9 us
    dot_general x10, matrix products, dot(): return jnp.dot(a, b, preferred_element_type=F32)  26 us
    dot_general x7, matrix products, dot_nt(): lax.dot_general(a, b, (((1,), (1,)), ((), ())), preferred_element_type=F32)  23 us
  transfers between devices with their start and end apart: 111, of which 36 were waited for; matrix products, arithmetic and copies ran while one was open for 30% of the time, Pallas kernels for 3%

profile of v1, /device:TPU:4, one launch (start us, length us, event | category | flops | bytes accessed | tf_op | source)
XLA Modules:
  0.0 731.4 jit_solution(4258223208192007626)
XLA Ops:
  29.2 5.6 collective-permute-done.4
  41.9 10.1 %collective-permute-done.5 = bf16[128,1024]{1,0:T(8,128)(2,1)} collective-permute-done((bf16[128,1024]{1,0:T(8,128)(2,1)S(1)}, bf16[128,1024]{1,0:T(8,128)(2,1)}, u32[]{:S(2)}, u32[]{:S(2)}) %collective-permute-start.5) | collective-permute-done | bytes 262176 | tf_op jit(solution)/shard_map/ppermute | solution.py:196
  53.3 6.4 collective-permute-done
  60.6 10.4 %collective-permute-done.61 = bf16[256,1024]{1,0:T(8,128)(2,1)S(1)} collective-permute-done((bf16[256,1024]{1,0:T(8,128)(2,1)}, bf16[256,1024]{1,0:T(8,128)(2,1)S(1)}, u32[]{:S(2)}, u32[]{:S(2)}) %collective-permute-start.61) | collective-permute-done | bytes 524320 | tf_op jit(solution)/shard_map/ppermute | solution.py:196
  72.1 13.2 %collective-permute-start.27 = (bf16[256,1024]{1,0:T(8,128)(2,1)S(1)}, bf16[256,1024]{1,0:T(8,128)(2,1)}, u32[]{:S(2)}, u32[]{:S(2)}) collective-permute-start(bf16[256,1024]{1,0:T(8,128)(2,1)S(1)} %pad_maximum_fusion.14), channel_id=1, source_target_pairs={{0,4},{1,5},{2,6},{3,7},{4,8},{5,9},{6,10},{7,11},{8,12},{9,13},{1... | collective-permute-start | bytes 1572872 | tf_op jit(solution)/shard_map/ppermute | solution.py:196
  87.4 8.4 %collective-permute-done.9 = bf16[128,1024]{1,0:T(8,128)(2,1)S(1)} collective-permute-done((bf16[128,1024]{1,0:T(8,128)(2,1)S(1)}, bf16[128,1024]{1,0:T(8,128)(2,1)S(1)}, u32[]{:S(2)}, u32[]{:S(2)}) %collective-permute-start.9) | collective-permute-done | bytes 262176 | tf_op jit(solution)/shard_map/ppermute | solution.py:196
  98.9 7.2 collective-permute-done.10
  113.7 5.1 collective-permute-done.15
  129.0 8.2 %collective-permute-done.1 = bf16[1,256,1024]{2,1,0:T(8,128)(2,1)S(1)} collective-permute-done((bf16[1,256,1024]{2,1,0:T(8,128)(2,1)S(1)}, bf16[1,256,1024]{2,1,0:T(8,128)(2,1)S(1)}, u32[]{:S(2)}, u32[]{:S(2)}) %collective-permute-start.1) | collective-permute-done | bytes 524320 | tf_op jit(solution)/shard_map/ppermute | solution.py:196
  165.4 24.6 %collective-permute-done.32 = bf16[256,1024]{1,0:T(8,128)(2,1)S(1)} collective-permute-done((bf16[256,1024]{1,0:T(8,128)(2,1)}, bf16[256,1024]{1,0:T(8,128)(2,1)S(1)}, u32[]{:S(2)}, u32[]{:S(2)}) %collective-permute-start.32) | collective-permute-done | bytes 524320 | tf_op jit(solution)/shard_map/ppermute | solution.py:196
  197.0 7.3 %shard_map.255 = bf16[1024,256]{1,0:T(8,128)(2,1)S(1)} custom-call(bf16[1024,768]{1,0:T(8,128)(2,1)S(1)} %convolution_convert_fusion.q_ref.k_ref.v_ref, bf16[1024,768]{1,0:T(8,128)(2,1)S(1)} %convolution_convert_fusion.q_ref.k_ref.v_ref, bf16[1024,768]{1,0:T(8,128)(2,1)S(1)} %convolution_convert_fusion.q_ref.k_ref.v_ref, s32[1,1024]{1,0:T(1,128)S(1)} %bitcast.571, ...), custom_call_target="tpu_custom_call" | custom-call | flops 2147483648 | bytes 2097152 | tf_op jit(solution)/shard_map/pallas_call | solution.py:131
  217.0 4.9 collective-permute-done.68
  227.1 8.0 %collective-permute-done.37 = bf16[256,1024]{1,0:T(8,128)(2,1)S(1)} collective-permute-done((bf16[256,1024]{1,0:T(8,128)(2,1)}, bf16[256,1024]{1,0:T(8,128)(2,1)S(1)}, u32[]{:S(2)}, u32[]{:S(2)}) %collective-permute-start.37) | collective-permute-done | bytes 524320 | tf_op jit(solution)/shard_map/ppermute | solution.py:196
  235.8 10.6 %collective-permute-done.38 = bf16[256,1024]{1,0:T(8,128)(2,1)S(1)} collective-permute-done((bf16[256,1024]{1,0:T(8,128)(2,1)}, bf16[256,1024]{1,0:T(8,128)(2,1)S(1)}, u32[]{:S(2)}, u32[]{:S(2)}) %collective-permute-start.38) | collective-permute-done | bytes 524320 | tf_op jit(solution)/shard_map/ppermute | solution.py:196
  249.2 8.4 %collective-permute-done.39 = bf16[256,1024]{1,0:T(8,128)(2,1)S(1)} collective-permute-done((bf16[256,1024]{1,0:T(8,128)(2,1)S(1)}, bf16[256,1024]{1,0:T(8,128)(2,1)S(1)}, u32[]{:S(2)}, u32[]{:S(2)}) %collective-permute-start.39) | collective-permute-done | bytes 524320 | tf_op jit(solution)/shard_map/ppermute | solution.py:196
  277.8 9.9 %collective-permute-done.23 = bf16[1,256,1024]{2,1,0:T(8,128)(2,1)S(1)} collective-permute-done((bf16[1,256,1024]{2,1,0:T(8,128)(2,1)S(1)}, bf16[1,256,1024]{2,1,0:T(8,128)(2,1)S(1)}, u32[]{:S(2)}, u32[]{:S(2)}) %collective-permute-start.23) | collective-permute-done | bytes 524320 | tf_op jit(solution)/shard_map/ppermute | solution.py:196
  288.1 5.5 collective-permute-done.43
  295.0 5.4 collective-permute-start.44
  303.3 7.4 %collective-permute-done.47 = bf16[288,1024]{1,0:T(8,128)(2,1)} collective-permute-done((bf16[288,1024]{1,0:T(8,128)(2,1)S(1)}, bf16[288,1024]{1,0:T(8,128)(2,1)}, u32[]{:S(2)}, u32[]{:S(2)}) %collective-permute-start.47) | collective-permute-done | bytes 589856 | tf_op jit(solution)/shard_map/ppermute | solution.py:196
  319.3 7.9 %fusion.18 = (bf16[1024,1024]{0,1:T(8,128)(2,1)}, f32[1024,1024]{1,0:T(8,128)}) fusion(bf16[1024,1024]{1,0:T(8,128)(2,1)} %bitcast.594, bf16[1024,1024]{1,0:T(8,128)(2,1)} %bitcast.630), kind=kOutput, calls=%fused_computation.36 | convolution fusion | flops 2156920832 | bytes 10485760 | tf_op jit(solution)/shard_map/dot_general | solution.py:23
  327.2 5.4 copy.189
  332.6 4.8 multiply_convert_fusion.1
  341.3 4.7 fusion.41
  349.2 5.5 fusion.13
  358.7 6.6 fusion.37
  369.4 4.7 fusion.149
  387.6 13.0 %collective-permute-done.49 = bf16[288,1024]{1,0:T(8,128)(2,1)S(1)} collective-permute-done((bf16[288,1024]{1,0:T(8,128)(2,1)}, bf16[288,1024]{1,0:T(8,128)(2,1)S(1)}, u32[]{:S(2)}, u32[]{:S(2)}) %collective-permute-start.49) | collective-permute-done | bytes 589856 | tf_op jit(solution)/shard_map/ppermute | solution.py:196
  407.1 5.0 fusion
  414.6 5.1 fusion.141
  419.7 6.7 fusion.24
  426.3 4.6 fusion.150
  447.3 9.2 %collective-permute-done.74 = bf16[288,1024]{1,0:T(8,128)(2,1)S(1)} collective-permute-done((bf16[288,1024]{1,0:T(8,128)(2,1)S(1)}, bf16[288,1024]{1,0:T(8,128)(2,1)S(1)}, u32[]{:S(2)}, u32[]{:S(2)}) %collective-permute-start.74) | collective-permute-done | bytes 589856 | tf_op jit(solution)/shard_map/ppermute | solution.py:196
  464.4 4.8 collective-permute-done.53
  472.1 5.2 collective-permute-start.54
  477.3 4.5 collective-permute-done.75
  489.2 15.4 %collective-permute-start.99 = (bf16[256,1024]{1,0:T(8,128)(2,1)S(1)}, bf16[256,1024]{1,0:T(8,128)(2,1)S(1)}, u32[]{:S(2)}, u32[]{:S(2)}) collective-permute-start(bf16[256,1024]{1,0:T(8,128)(2,1)S(1)} %get-tuple-element.96), channel_id=1, source_target_pairs={{0,4},{1,5},{2,6},{3,7},{16,20},{17,21},{18,22},{19,23}} | collective-permute-start | bytes 1572872 | tf_op jit(solution)/shard_map/ppermute | solution.py:196
  509.0 8.3 %collective-permute-start.76 = (bf16[288,1024]{1,0:T(8,128)(2,1)S(1)}, bf16[288,1024]{1,0:T(8,128)(2,1)S(1)}, u32[]{:S(2)}, u32[]{:S(2)}) collective-permute-start(bf16[288,1024]{1,0:T(8,128)(2,1)S(1)} %copy-done.51), channel_id=1, source_target_pairs={{0,4},{1,5},{2,6},{3,7},{4,8},{5,9},{6,10},{7,11},{8,12},{9,13},{1... | collective-permute-start | bytes 1769480 | tf_op jit(solution)/shard_map/ppermute | solution.py:196
  521.8 8.0 %collective-permute-start.100 = (bf16[256,1024]{1,0:T(8,128)(2,1)S(1)}, bf16[256,1024]{1,0:T(8,128)(2,1)S(1)}, u32[]{:S(2)}, u32[]{:S(2)}) collective-permute-start(bf16[256,1024]{1,0:T(8,128)(2,1)S(1)} %fusion.89), channel_id=1, source_target_pairs={{0,4},{1,5},{2,6},{3,7},{4,8},{5,9},{6,10},{7,11},{16,20},{17,21},... | collective-permute-start | bytes 1572872 | tf_op jit(solution)/shard_map/ppermute | solution.py:196
  540.5 19.7 %collective-permute-start.101 = (bf16[256,1024]{1,0:T(8,128)(2,1)}, bf16[256,1024]{1,0:T(8,128)(2,1)}, u32[]{:S(2)}, u32[]{:S(2)}) collective-permute-start(bf16[256,1024]{1,0:T(8,128)(2,1)} %get-tuple-element.94), channel_id=1, source_target_pairs={{0,4},{1,5},{2,6},{3,7},{4,8},{5,9},{6,10},{7,11},{8,12},{9,13},{1... | collective-permute-start | bytes 1572872 | tf_op jit(solution)/shard_map/ppermute | solution.py:196
  564.6 5.2 collective-permute-done.81
  588.2 9.9 %collective-permute-done.83 = bf16[1,2,256,256]{3,2,1,0:T(8,128)(2,1)S(1)} collective-permute-done((bf16[1,2,256,256]{3,2,1,0:T(8,128)(2,1)S(1)}, bf16[1,2,256,256]{3,2,1,0:T(8,128)(2,1)S(1)}, u32[]{:S(2)}, u32[]{:S(2)}) %collective-permute-start.83) | collective-permute-done | bytes 262176 | tf_op jit(solution)/shard_map/ppermute | solution.py:196
  598.1 14.0 %shard_map.256 = (bf16[1024,256]{1,0:T(8,128)(2,1)S(1)}, bf16[1024,256]{1,0:T(8,128)(2,1)S(1)}, bf16[1024,256]{1,0:T(8,128)(2,1)S(1)}) custom-call(bf16[1024,768]{1,0:T(8,128)(2,1)S(1)} %convolution_convert_fusion.q_ref.k_ref.v_ref, bf16[1024,768]{1,0:T(8,128)(2,1)S(1)} %convolution_convert_fusion.q_ref.k_ref.v_ref, ...), custom_call_target="tpu_custom_call" | custom-call | flops 5368709120 | bytes 3670016 | tf_op jit(solution)/shard_map/pallas_call | solution.py:158
  626.0 11.1 %collective-permute-done.88 = bf16[1,8,32,1024]{3,2,0,1:T(8,128)(2,1)S(1)} collective-permute-done((bf16[1,8,32,1024]{3,2,0,1:T(8,128)(2,1)S(1)}, bf16[1,8,32,1024]{3,2,0,1:T(8,128)(2,1)S(1)}, u32[]{:S(2)}, u32[]{:S(2)}) %collective-permute-start.88) | collective-permute-done | bytes 524320 | tf_op jit(solution)/shard_map/ppermute | solution.py:196
  646.7 14.6 %collective-permute-done.89 = bf16[4,128,1024]{2,1,0:T(8,128)(2,1)S(1)} collective-permute-done((bf16[4,128,1024]{2,1,0:T(8,128)(2,1)S(1)}, bf16[4,128,1024]{2,1,0:T(8,128)(2,1)S(1)}, u32[]{:S(2)}, u32[]{:S(2)}) %collective-permute-start.89) | collective-permute-done | bytes 1048608 | tf_op jit(solution)/shard_map/ppermute | solution.py:196
  668.1 4.5 collective-permute-start.91
  679.9 7.1 all-to-all-start.1
  694.0 5.4 collective-permute-start.86
  706.1 19.8 %collective-permute-done.86 = bf16[256,1024]{1,0:T(8,128)(2,1)S(1)} collective-permute-done((bf16[256,1024]{1,0:T(8,128)(2,1)S(1)}, bf16[256,1024]{1,0:T(8,128)(2,1)S(1)}, u32[]{:S(2)}, u32[]{:S(2)}) %collective-permute-start.86) | collective-permute-done | bytes 524320 | tf_op jit(solution)/shard_map/ppermute | solution.py:196
  (580 shorter events, 319.8 us)
Async XLA Ops:
  1.4 25.0 %collective-permute-start.18 = (s32[12,128]{1,0:T(8,128)S(1)}, s32[12,128]{1,0:T(8,128)S(1)}, u32[]{:S(2)}, u32[]{:S(2)}) collective-permute-start(s32[12,128]{1,0:T(8,128)S(1)} %add_bitcast_fusion), channel_id=1, source_target_pairs={{0,0},{1,4},{2,8},{3,12},{4,1},{5,5},{6,9},{7,13},{8,2},{9,6},{10,... | collective-permute-start | bytes 18440 | tf_op jit(solution)/shard_map/ppermute | solution.py:196
  18.7 41.1 %collective-permute-start = (bf16[256,1024]{1,0:T(8,128)(2,1)}, bf16[256,1024]{1,0:T(8,128)(2,1)S(1)}, u32[]{:S(2)}, u32[]{:S(2)}) collective-permute-start(bf16[256,1024]{1,0:T(8,128)(2,1)} %bitcast), channel_id=1, source_target_pairs={{0,0},{1,4},{2,8},{3,12},{4,1},{5,5},{6,9},{7,13},{8,2},{9,6},{10,... | collective-permute-start | bytes 1572872 | tf_op jit(solution)/shard_map/ppermute | solution.py:196
  22.9 48.1 %collective-permute-start.61 = (bf16[256,1024]{1,0:T(8,128)(2,1)}, bf16[256,1024]{1,0:T(8,128)(2,1)S(1)}, u32[]{:S(2)}, u32[]{:S(2)}) collective-permute-start(bf16[256,1024]{1,0:T(8,128)(2,1)} %bitcast.125), channel_id=1, source_target_pairs={{0,0},{1,4},{2,8},{3,12},{4,1},{5,5},{6,9},{7,13},{8,2},{9,6},{10,... | collective-permute-start | bytes 1572872 | tf_op jit(solution)/shard_map/ppermute | solution.py:196
  39.0 72.2 %collective-permute-start.14 = (bf16[128,1024]{1,0:T(8,128)(2,1)S(1)}, bf16[128,1024]{1,0:T(8,128)(2,1)S(1)}, u32[]{:S(2)}, u32[]{:S(2)}) collective-permute-start(bf16[128,1024]{1,0:T(8,128)(2,1)S(1)} %constant_dynamic-update-slice_fusion), channel_id=1, source_target_pairs={{0,16},{1,17},{2,18},{3,19},{4,20},{5,21},{6,22},{7,23},{8,24},{9,... | collective-permute-start | bytes 786440 | tf_op jit(solution)/shard_map/ppermute | solution.py:196
  40.5 31.6 %collective-permute-start.8 = (bf16[128,1024]{1,0:T(8,128)(2,1)S(1)}, bf16[128,1024]{1,0:T(8,128)(2,1)S(1)}, u32[]{:S(2)}, u32[]{:S(2)}) collective-permute-start(bf16[128,1024]{1,0:T(8,128)(2,1)S(1)} %constant_dynamic-update-slice_fusion), channel_id=1, source_target_pairs={{4,0},{5,1},{6,2},{7,3},{8,4},{9,5},{10,6},{11,7},{12,8},{13,9},{1... | collective-permute-start | bytes 786440 | tf_op jit(solution)/shard_map/ppermute | solution.py:196
  52.0 86.3 %collective-permute-start.30 = (bf16[256,1024]{1,0:T(8,128)(2,1)S(1)}, bf16[256,1024]{1,0:T(8,128)(2,1)}, u32[]{:S(2)}, u32[]{:S(2)}) collective-permute-start(bf16[256,1024]{1,0:T(8,128)(2,1)S(1)} %pad_maximum_fusion.14), channel_id=1, source_target_pairs={{4,0},{5,1},{6,2},{7,3},{8,4},{9,5},{10,6},{11,7},{12,8},{13,9},{1... | collective-permute-start | bytes 1572872 | tf_op jit(solution)/shard_map/ppermute | solution.py:196
  59.8 25.5 %collective-permute-start.6 = (bf16[128,1024]{1,0:T(8,128)(2,1)}, bf16[128,1024]{1,0:T(8,128)(2,1)S(1)}, u32[]{:S(2)}, u32[]{:S(2)}) collective-permute-start(bf16[128,1024]{1,0:T(8,128)(2,1)} %collective-permute-done.5), channel_id=1, source_target_pairs={{4,8},{5,9},{6,10},{7,11},{8,12},{9,13},{10,14},{11,15},{20,24},{2... | collective-permute-start | bytes 786440 | tf_op jit(solution)/shard_map/ppermute | solution.py:196
  72.1 50.1 %collective-permute-start.27 = (bf16[256,1024]{1,0:T(8,128)(2,1)S(1)}, bf16[256,1024]{1,0:T(8,128)(2,1)}, u32[]{:S(2)}, u32[]{:S(2)}) collective-permute-start(bf16[256,1024]{1,0:T(8,128)(2,1)S(1)} %pad_maximum_fusion.14), channel_id=1, source_target_pairs={{0,4},{1,5},{2,6},{3,7},{4,8},{5,9},{6,10},{7,11},{8,12},{9,13},{1... | collective-permute-start | bytes 1572872 | tf_op jit(solution)/shard_map/ppermute | solution.py:196
  111.1 28.8 %collective-permute-start.62 = (bf16[1,256,1024]{2,1,0:T(8,128)(2,1)S(1)}, bf16[1,256,1024]{2,1,0:T(8,128)(2,1)S(1)}, u32[]{:S(2)}, u32[]{:S(2)}) collective-permute-start(bf16[1,256,1024]{2,1,0:T(8,128)(2,1)S(1)} %bitcast.596), channel_id=1, source_target_pairs={{0,2},{1,3},{2,0},{3,1},{4,6},{5,7},{6,4},{7,5},{8,10},{9,11},{10,... | collective-permute-start | bytes 1572872 | tf_op jit(solution)/shard_map/ppermute | solution.py:196
  138.4 74.8 %collective-permute-start.35 = (bf16[256,1024]{1,0:T(8,128)(2,1)}, bf16[256,1024]{1,0:T(8,128)(2,1)}, u32[]{:S(2)}, u32[]{:S(2)}) collective-permute-start(bf16[256,1024]{1,0:T(8,128)(2,1)} %collective-permute-done.27), channel_id=1, source_target_pairs={{4,20},{5,21},{6,22},{7,23},{8,24},{9,25},{10,26},{11,27},{12,28},... | collective-permute-start | bytes 1572872 | tf_op jit(solution)/shard_map/ppermute | solution.py:196
  145.2 46.0 %collective-permute-start.2 = (bf16[2,256,1024]{2,1,0:T(8,128)(2,1)}, bf16[2,256,1024]{2,1,0:T(8,128)(2,1)}, u32[]{:S(2)}, u32[]{:S(2)}) collective-permute-start(bf16[2,256,1024]{2,1,0:T(8,128)(2,1)} %maximum_select_fusion.5), channel_id=1, source_target_pairs={{0,1},{1,0},{2,3},{3,2},{4,5},{5,4},{6,7},{7,6},{8,9},{9,8},{10,11... | collective-permute-start | bytes 3145736 | tf_op jit(solution)/shard_map/ppermute | solution.py:196
  152.1 52.6 %collective-permute-start.63 = (bf16[2,256,1024]{2,1,0:T(8,128)(2,1)}, bf16[2,256,1024]{2,1,0:T(8,128)(2,1)S(1)}, u32[]{:S(2)}, u32[]{:S(2)}) collective-permute-start(bf16[2,256,1024]{2,1,0:T(8,128)(2,1)} %get-tuple-element.109), channel_id=1, source_target_pairs={{0,1},{1,0},{2,3},{3,2},{4,5},{5,4},{6,7},{7,6},{8,9},{9,8},{10,11... | collective-permute-start | bytes 3145736 | tf_op jit(solution)/shard_map/ppermute | solution.py:196
  157.2 58.5 %collective-permute-start.71 = (bf16[288,1024]{1,0:T(8,128)(2,1)S(1)}, bf16[288,1024]{1,0:T(8,128)(2,1)S(1)}, u32[]{:S(2)}, u32[]{:S(2)}) collective-permute-start(bf16[288,1024]{1,0:T(8,128)(2,1)S(1)} %bitcast.604), channel_id=1, source_target_pairs={{4,0},{5,1},{6,2},{7,3},{8,4},{9,5},{10,6},{11,7},{12,8},{13,9},{1... | collective-permute-start | bytes 1769480 | tf_op jit(solution)/shard_map/ppermute | solution.py:196
  158.5 31.5 %collective-permute-start.32 = (bf16[256,1024]{1,0:T(8,128)(2,1)}, bf16[256,1024]{1,0:T(8,128)(2,1)S(1)}, u32[]{:S(2)}, u32[]{:S(2)}) collective-permute-start(bf16[256,1024]{1,0:T(8,128)(2,1)} %collective-permute-done.31), channel_id=1, source_target_pairs={{4,0},{5,1},{6,2},{7,3},{20,16},{21,17},{22,18},{23,19}} | collective-permute-start | bytes 1572872 | tf_op jit(solution)/shard_map/ppermute | solution.py:196
  209.8 25.4 %collective-permute-start.37 = (bf16[256,1024]{1,0:T(8,128)(2,1)}, bf16[256,1024]{1,0:T(8,128)(2,1)S(1)}, u32[]{:S(2)}, u32[]{:S(2)}) collective-permute-start(bf16[256,1024]{1,0:T(8,128)(2,1)} %collective-permute-done.30), channel_id=1, source_target_pairs={{0,16},{1,17},{2,18},{3,19},{4,20},{5,21},{6,22},{7,23},{8,24},{9,... | collective-permute-start | bytes 1572872 | tf_op jit(solution)/shard_map/ppermute | solution.py:196
  213.1 33.2 %collective-permute-start.38 = (bf16[256,1024]{1,0:T(8,128)(2,1)}, bf16[256,1024]{1,0:T(8,128)(2,1)S(1)}, u32[]{:S(2)}, u32[]{:S(2)}) collective-permute-start(bf16[256,1024]{1,0:T(8,128)(2,1)} %collective-permute-done.31), channel_id=1, source_target_pairs={{0,16},{1,17},{2,18},{3,19},{4,20},{5,21},{6,22},{7,23},{16,0},{17... | collective-permute-start | bytes 1572872 | tf_op jit(solution)/shard_map/ppermute | solution.py:196
  215.7 30.7 %collective-permute-start.72 = (bf16[288,1024]{1,0:T(8,128)(2,1)S(1)}, bf16[288,1024]{1,0:T(8,128)(2,1)}, u32[]{:S(2)}, u32[]{:S(2)}) collective-permute-start(bf16[288,1024]{1,0:T(8,128)(2,1)S(1)} %collective-permute-done.71), channel_id=1, source_target_pairs={{4,0},{5,1},{6,2},{7,3},{8,4},{9,5},{10,6},{11,7},{20,16},{21,17},... | collective-permute-start | bytes 1769480 | tf_op jit(solution)/shard_map/ppermute | solution.py:196
  221.9 25.7 %collective-permute-start.69 = (bf16[288,1024]{1,0:T(8,128)(2,1)S(1)}, bf16[288,1024]{1,0:T(8,128)(2,1)}, u32[]{:S(2)}, u32[]{:S(2)}) collective-permute-start(bf16[288,1024]{1,0:T(8,128)(2,1)S(1)} %collective-permute-done.68), channel_id=1, source_target_pairs={{4,8},{5,9},{6,10},{7,11},{8,12},{9,13},{10,14},{11,15},{20,24},{2... | collective-permute-start | bytes 1769480 | tf_op jit(solution)/shard_map/ppermute | solution.py:196
  224.5 33.1 %collective-permute-start.39 = (bf16[256,1024]{1,0:T(8,128)(2,1)S(1)}, bf16[256,1024]{1,0:T(8,128)(2,1)S(1)}, u32[]{:S(2)}, u32[]{:S(2)}) collective-permute-start(bf16[256,1024]{1,0:T(8,128)(2,1)S(1)} %collective-permute-done.32), channel_id=1, source_target_pairs={{0,16},{1,17},{2,18},{3,19},{16,0},{17,1},{18,2},{19,3}} | collective-permute-start | bytes 1572872 | tf_op jit(solution)/shard_map/ppermute | solution.py:196
  235.1 167.8 %collective-permute-start.50 = (bf16[1024,512]{1,0:T(8,128)(2,1)}, bf16[1024,512]{1,0:T(8,128)(2,1)}, u32[]{:S(2)}, u32[]{:S(2)}) collective-permute-start(bf16[1024,512]{1,0:T(8,128)(2,1)} %bitcast.107), channel_id=1, source_target_pairs={{0,16},{1,17},{2,18},{3,19},{4,20},{5,21},{6,22},{7,23},{8,24},{9,... | collective-permute-start | bytes 3145736 | tf_op jit(solution)/shard_map/ppermute | solution.py:196
  246.4 55.2 %collective-permute-start.73 = (bf16[288,1024]{1,0:T(8,128)(2,1)}, bf16[288,1024]{1,0:T(8,128)(2,1)}, u32[]{:S(2)}, u32[]{:S(2)}) collective-permute-start(bf16[288,1024]{1,0:T(8,128)(2,1)} %collective-permute-done.72), channel_id=1, source_target_pairs={{4,0},{5,1},{6,2},{7,3},{20,16},{21,17},{22,18},{23,19}} | collective-permute-start | bytes 1769480 | tf_op jit(solution)/shard_map/ppermute | solution.py:196
  247.7 27.5 %collective-permute-start.70 = (bf16[288,1024]{1,0:T(8,128)(2,1)}, bf16[288,1024]{1,0:T(8,128)(2,1)}, u32[]{:S(2)}, u32[]{:S(2)}) collective-permute-start(bf16[288,1024]{1,0:T(8,128)(2,1)} %collective-permute-done.69), channel_id=1, source_target_pairs={{8,12},{9,13},{10,14},{11,15},{24,28},{25,29},{26,30},{27,31}} | collective-permute-start | bytes 1769480 | tf_op jit(solution)/shard_map/ppermute | solution.py:196
  287.9 25.7 %collective-permute-start.24 = (bf16[2,256,1024]{2,1,0:T(8,128)(2,1)S(1)}, bf16[2,256,1024]{2,1,0:T(8,128)(2,1)S(1)}, u32[]{:S(2)}, u32[]{:S(2)}) collective-permute-start(bf16[2,256,1024]{2,1,0:T(8,128)(2,1)S(1)} %get-tuple-element.111), channel_id=1, source_target_pairs={{0,1},{1,0},{2,3},{3,2},{4,5},{5,4},{6,7},{7,6},{8,9},{9,8},{10,11... | collective-permute-start | bytes 3145736 | tf_op jit(solution)/shard_map/ppermute | solution.py:196
  301.6 105.5 %collective-permute-start.51 = (bf16[512,1024]{1,0:T(8,128)(2,1)}, bf16[512,1024]{1,0:T(8,128)(2,1)}, u32[]{:S(2)}, u32[]{:S(2)}) collective-permute-start(bf16[512,1024]{1,0:T(8,128)(2,1)} %bitcast.108), channel_id=1, source_target_pairs={{0,16},{1,17},{2,18},{3,19},{4,20},{5,21},{6,22},{7,23},{8,24},{9,... | collective-permute-start | bytes 3145736 | tf_op jit(solution)/shard_map/ppermute | solution.py:196
  310.6 70.3 %collective-permute-start.48 = (bf16[288,1024]{1,0:T(8,128)(2,1)}, bf16[288,1024]{1,0:T(8,128)(2,1)}, u32[]{:S(2)}, u32[]{:S(2)}) collective-permute-start(bf16[288,1024]{1,0:T(8,128)(2,1)} %collective-permute-done.47), channel_id=1, source_target_pairs={{4,0},{5,1},{6,2},{7,3},{8,4},{9,5},{10,6},{11,7},{20,16},{21,17},... | collective-permute-start | bytes 1769480 | tf_op jit(solution)/shard_map/ppermute | solution.py:196
  311.9 62.2 %collective-permute-start.45 = (bf16[288,1024]{1,0:T(8,128)(2,1)}, bf16[288,1024]{1,0:T(8,128)(2,1)}, u32[]{:S(2)}, u32[]{:S(2)}) collective-permute-start(bf16[288,1024]{1,0:T(8,128)(2,1)} %collective-permute-done.44), channel_id=1, source_target_pairs={{4,8},{5,9},{6,10},{7,11},{8,12},{9,13},{10,14},{11,15},{20,24},{2... | collective-permute-start | bytes 1769480 | tf_op jit(solution)/shard_map/ppermute | solution.py:196
  349.2 91.9 %collective-permute-start.40 = (bf16[2,256,1024]{2,1,0:T(8,128)(2,1)}, bf16[2,256,1024]{2,1,0:T(8,128)(2,1)}, u32[]{:S(2)}, u32[]{:S(2)}) collective-permute-start(bf16[2,256,1024]{2,1,0:T(8,128)(2,1)} %fusion.76), channel_id=1, source_target_pairs={{0,1},{1,0},{2,3},{3,2},{4,5},{5,4},{6,7},{7,6},{8,9},{9,8},{10,11... | collective-permute-start | bytes 3145736 | tf_op jit(solution)/shard_map/ppermute | solution.py:196
  381.0 63.6 %collective-permute-start.64 = (bf16[2,256,1024]{2,1,0:T(8,128)(2,1)}, bf16[2,256,1024]{2,1,0:T(8,128)(2,1)S(1)}, u32[]{:S(2)}, u32[]{:S(2)}) collective-permute-start(bf16[2,256,1024]{2,1,0:T(8,128)(2,1)} %fusion.77), channel_id=1, source_target_pairs={{0,1},{1,0},{2,3},{3,2},{4,5},{5,4},{6,7},{7,6},{8,9},{9,8},{10,11... | collective-permute-start | bytes 3145736 | tf_op jit(solution)/shard_map/ppermute | solution.py:196
  400.6 84.1 %collective-permute-start.98 = (bf16[4,256,1024]{2,1,0:T(8,128)(2,1)}, bf16[4,256,1024]{2,1,0:T(8,128)(2,1)}, u32[]{:S(2)}, u32[]{:S(2)}) collective-permute-start(bf16[4,256,1024]{2,1,0:T(8,128)(2,1)} %fusion.25), channel_id=1, source_target_pairs={{0,16},{1,17},{2,18},{3,19},{4,20},{5,21},{6,22},{7,23},{8,24},{9,... | collective-permute-start | bytes 6291464 | tf_op jit(solution)/shard_map/ppermute | solution.py:196
  412.3 33.5 %collective-permute-start.52 = (bf16[288,1024]{1,0:T(8,128)(2,1)S(1)}, bf16[288,1024]{1,0:T(8,128)(2,1)S(1)}, u32[]{:S(2)}, u32[]{:S(2)}) collective-permute-start(bf16[288,1024]{1,0:T(8,128)(2,1)S(1)} %get-tuple-element.92), channel_id=1, source_target_pairs={{0,4},{1,5},{2,6},{3,7},{16,20},{17,21},{18,22},{19,23}} | collective-permute-start | bytes 1769480 | tf_op jit(solution)/shard_map/ppermute | solution.py:196
  413.9 49.0 %collective-permute-start.55 = (bf16[288,1024]{1,0:T(8,128)(2,1)S(1)}, bf16[288,1024]{1,0:T(8,128)(2,1)S(1)}, u32[]{:S(2)}, u32[]{:S(2)}) collective-permute-start(bf16[288,1024]{1,0:T(8,128)(2,1)S(1)} %get-tuple-element.93), channel_id=1, source_target_pairs={{12,8},{13,9},{14,10},{15,11},{28,24},{29,25},{30,26},{31,27}} | collective-permute-start | bytes 1769480 | tf_op jit(solution)/shard_map/ppermute | solution.py:196
  444.6 27.5 %collective-permute-start.77 = (bf16[288,1024]{1,0:T(8,128)(2,1)S(1)}, bf16[288,1024]{1,0:T(8,128)(2,1)S(1)}, u32[]{:S(2)}, u32[]{:S(2)}) collective-permute-start(bf16[288,1024]{1,0:T(8,128)(2,1)S(1)} %get-tuple-element.89), channel_id=1, source_target_pairs={{12,8},{13,9},{14,10},{15,11},{28,24},{29,25},{30,26},{31,27}} | collective-permute-start | bytes 1769480 | tf_op jit(solution)/shard_map/ppermute | solution.py:196
  446.0 23.2 %collective-permute-start.53 = (bf16[288,1024]{1,0:T(8,128)(2,1)S(1)}, bf16[288,1024]{1,0:T(8,128)(2,1)S(1)}, u32[]{:S(2)}, u32[]{:S(2)}) collective-permute-start(bf16[288,1024]{1,0:T(8,128)(2,1)S(1)} %fusion.61), channel_id=1, source_target_pairs={{0,4},{1,5},{2,6},{3,7},{4,8},{5,9},{6,10},{7,11},{16,20},{17,21},... | collective-permute-start | bytes 1769480 | tf_op jit(solution)/shard_map/ppermute | solution.py:196
  456.7 25.1 %collective-permute-start.75 = (bf16[288,1024]{1,0:T(8,128)(2,1)S(1)}, bf16[288,1024]{1,0:T(8,128)(2,1)S(1)}, u32[]{:S(2)}, u32[]{:S(2)}) collective-permute-start(bf16[288,1024]{1,0:T(8,128)(2,1)S(1)} %fusion.55), channel_id=1, source_target_pairs={{0,4},{1,5},{2,6},{3,7},{4,8},{5,9},{6,10},{7,11},{16,20},{17,21},... | collective-permute-start | bytes 1769480 | tf_op jit(solution)/shard_map/ppermute | solution.py:196
  462.9 43.1 %collective-permute-start.108 = (bf16[512,1024]{1,0:T(8,128)(2,1)S(1)}, bf16[512,1024]{1,0:T(8,128)(2,1)S(1)}, u32[]{:S(2)}, u32[]{:S(2)}) collective-permute-start(bf16[512,1024]{1,0:T(8,128)(2,1)S(1)} %slice.336), channel_id=1, source_target_pairs={{0,16},{1,17},{2,18},{3,19},{4,20},{5,21},{6,22},{7,23},{8,24},{9,... | collective-permute-start | bytes 3145736 | tf_op jit(solution)/shard_map/ppermute | solution.py:196
  469.2 169.9 %collective-permute-start.107 = (bf16[1024,512]{1,0:T(8,128)(2,1)}, bf16[1024,512]{1,0:T(8,128)(2,1)}, u32[]{:S(2)}, u32[]{:S(2)}) collective-permute-start(bf16[1024,512]{1,0:T(8,128)(2,1)} %slice.337), channel_id=1, source_target_pairs={{0,16},{1,17},{2,18},{3,19},{4,20},{5,21},{6,22},{7,23},{8,24},{9,... | collective-permute-start | bytes 3145736 | tf_op jit(solution)/shard_map/ppermute | solution.py:196
  472.1 48.0 %collective-permute-start.54 = (bf16[288,1024]{1,0:T(8,128)(2,1)}, bf16[288,1024]{1,0:T(8,128)(2,1)}, u32[]{:S(2)}, u32[]{:S(2)}) collective-permute-start(bf16[288,1024]{1,0:T(8,128)(2,1)} %get-tuple-element.90), channel_id=1, source_target_pairs={{0,4},{1,5},{2,6},{3,7},{4,8},{5,9},{6,10},{7,11},{8,12},{9,13},{1... | collective-permute-start | bytes 1769480 | tf_op jit(solution)/shard_map/ppermute | solution.py:196
  484.7 24.3 %collective-permute-start.78 = (bf16[288,1024]{1,0:T(8,128)(2,1)}, bf16[288,1024]{1,0:T(8,128)(2,1)}, u32[]{:S(2)}, u32[]{:S(2)}) collective-permute-start(bf16[288,1024]{1,0:T(8,128)(2,1)} %get-tuple-element.87), channel_id=1, source_target_pairs={{8,4},{9,5},{10,6},{11,7},{12,8},{13,9},{14,10},{15,11},{24,20},{2... | collective-permute-start | bytes 1769480 | tf_op jit(solution)/shard_map/ppermute | solution.py:196
  489.2 29.4 %collective-permute-start.99 = (bf16[256,1024]{1,0:T(8,128)(2,1)S(1)}, bf16[256,1024]{1,0:T(8,128)(2,1)S(1)}, u32[]{:S(2)}, u32[]{:S(2)}) collective-permute-start(bf16[256,1024]{1,0:T(8,128)(2,1)S(1)} %get-tuple-element.96), channel_id=1, source_target_pairs={{0,4},{1,5},{2,6},{3,7},{16,20},{17,21},{18,22},{19,23}} | collective-permute-start | bytes 1572872 | tf_op jit(solution)/shard_map/ppermute | solution.py:196
  531.3 30.6 %collective-permute-start.41 = (bf16[1,256,1024]{2,1,0:T(8,128)(2,1)S(1)}, bf16[1,256,1024]{2,1,0:T(8,128)(2,1)S(1)}, u32[]{:S(2)}, u32[]{:S(2)}) collective-permute-start(bf16[1,256,1024]{2,1,0:T(8,128)(2,1)S(1)} %copy-done.59), channel_id=1, source_target_pairs={{0,2},{1,3},{2,0},{3,1},{4,6},{5,7},{6,4},{7,5},{8,10},{9,11},{10,... | collective-permute-start | bytes 1572872 | tf_op jit(solution)/shard_map/ppermute | solution.py:196
  533.5 38.5 %collective-permute-start.65 = (bf16[1,256,1024]{2,1,0:T(8,128)(2,1)S(1)}, bf16[1,256,1024]{2,1,0:T(8,128)(2,1)S(1)}, u32[]{:S(2)}, u32[]{:S(2)}) collective-permute-start(bf16[1,256,1024]{2,1,0:T(8,128)(2,1)S(1)} %copy-done.58), channel_id=1, source_target_pairs={{0,2},{1,3},{2,0},{3,1},{4,6},{5,7},{6,4},{7,5},{8,10},{9,11},{10,... | collective-permute-start | bytes 1572872 | tf_op jit(solution)/shard_map/ppermute | solution.py:196
  540.5 42.1 %collective-permute-start.101 = (bf16[256,1024]{1,0:T(8,128)(2,1)}, bf16[256,1024]{1,0:T(8,128)(2,1)}, u32[]{:S(2)}, u32[]{:S(2)}) collective-permute-start(bf16[256,1024]{1,0:T(8,128)(2,1)} %get-tuple-element.94), channel_id=1, source_target_pairs={{0,4},{1,5},{2,6},{3,7},{4,8},{5,9},{6,10},{7,11},{8,12},{9,13},{1... | collective-permute-start | bytes 1572872 | tf_op jit(solution)/shard_map/ppermute | solution.py:196
  561.9 24.5 %collective-permute-start.104 = (bf16[256,1024]{1,0:T(8,128)(2,1)}, bf16[256,1024]{1,0:T(8,128)(2,1)}, u32[]{:S(2)}, u32[]{:S(2)}) collective-permute-start(bf16[256,1024]{1,0:T(8,128)(2,1)} %fusion.88), channel_id=1, source_target_pairs={{4,0},{5,1},{6,2},{7,3},{8,4},{9,5},{10,6},{11,7},{12,8},{13,9},{1... | collective-permute-start | bytes 1572872 | tf_op jit(solution)/shard_map/ppermute | solution.py:196
  569.7 73.4 %collective-permute-start.60 = (bf16[256,1024]{1,0:T(8,128)(2,1)}, bf16[256,1024]{1,0:T(8,128)(2,1)}, u32[]{:S(2)}, u32[]{:S(2)}) collective-permute-start(bf16[256,1024]{1,0:T(8,128)(2,1)} %fusion.86), channel_id=1, source_target_pairs={{0,0},{1,4},{2,8},{3,12},{4,1},{5,5},{6,9},{7,13},{8,2},{9,6},{10,... | collective-permute-start | bytes 1572872 | tf_op jit(solution)/shard_map/ppermute | solution.py:196
  582.0 39.1 %collective-permute-start.87 = (bf16[2,8,32,1024]{3,2,0,1:T(8,128)(2,1)}, bf16[2,8,32,1024]{3,2,0,1:T(8,128)(2,1)}, u32[]{:S(2)}, u32[]{:S(2)}) collective-permute-start(bf16[2,8,32,1024]{3,2,0,1:T(8,128)(2,1)} %fusion.74), channel_id=1, source_target_pairs={{0,1},{1,0},{2,3},{3,2},{4,5},{5,4},{6,7},{7,6},{8,9},{9,8},{10,11... | collective-permute-start | bytes 3145736 | tf_op jit(solution)/shard_map/ppermute | solution.py:196
  637.4 23.8 %collective-permute-start.89 = (bf16[4,128,1024]{2,1,0:T(8,128)(2,1)S(1)}, bf16[4,128,1024]{2,1,0:T(8,128)(2,1)S(1)}, u32[]{:S(2)}, u32[]{:S(2)}) collective-permute-start(bf16[4,128,1024]{2,1,0:T(8,128)(2,1)S(1)} %fusion.78), channel_id=1, source_target_pairs={{0,16},{1,17},{2,18},{3,19},{4,20},{5,21},{6,22},{7,23},{8,24},{9,... | collective-permute-start | bytes 3145736 | tf_op jit(solution)/shard_map/ppermute | solution.py:196
  645.0 27.7 %collective-permute-start.85 = (bf16[1,256,1024]{2,1,0:T(8,128)(2,1)}, bf16[1,256,1024]{2,1,0:T(8,128)(2,1)}, u32[]{:S(2)}, u32[]{:S(2)}) collective-permute-start(bf16[1,256,1024]{2,1,0:T(8,128)(2,1)} %dynamic-slice_convert_fusion.8), channel_id=1, source_target_pairs={{0,2},{1,3},{2,0},{3,1},{4,6},{5,7},{6,4},{7,5},{8,10},{9,11},{10,... | collective-permute-start | bytes 1572872 | tf_op jit(solution)/shard_map/ppermute | solution.py:196
  694.0 31.8 %collective-permute-start.86 = (bf16[256,1024]{1,0:T(8,128)(2,1)S(1)}, bf16[256,1024]{1,0:T(8,128)(2,1)S(1)}, u32[]{:S(2)}, u32[]{:S(2)}) collective-permute-start(bf16[256,1024]{1,0:T(8,128)(2,1)S(1)} %fusion.71), channel_id=1, source_target_pairs={{0,0},{1,4},{2,8},{3,12},{4,1},{5,5},{6,9},{7,13},{8,2},{9,6},{10,... | collective-permute-start | bytes 1572872 | tf_op jit(solution)/shard_map/ppermute | solution.py:196
  (132 other events, 1549.5 us)

commit v2 on v1

--- a/solution.py
+++ b/solution.py
@@ -177,6 +177,124 @@
     )(qkv, qkv, qkv, d_out, segs[None, :], segs[:, None])
 
 
+def dense_kernel(
+    rows, step, x_ref, g_ref, wi_ref, wo_ref, both_ref, dwi_ref, dwo_ref, act_ref, dh_ref
+):
+    @pl.loop(0, x_ref.shape[0] // rows)
+    def _(t):
+        r = pl.ds(pl.multiple_of(t * rows, rows), rows)
+        act, slope = gelu_pair(dot(x_ref[r, :], wi_ref[...]))
+        act = act.astype(BF16)
+        dh = (dot_nt(g_ref[r, :], wo_ref[...]) * slope).astype(BF16)
+        act_ref[r, :] = act
+        dh_ref[r, :] = dh
+        both_ref[t % 2, 0, t // 2] = dot(act, wo_ref[...]).astype(BF16)
+        both_ref[t % 2, 1, t // 2] = dot_nt(dh, wi_ref[...]).astype(BF16)
+
+    @pl.loop(0, act_ref.shape[1] // min(step, act_ref.shape[1]))
+    def _(f):
+        size = min(step, act_ref.shape[1])
+        c = pl.ds(pl.multiple_of(f * size, size), size)
+        dwo_ref[c, :] = dot_tn(act_ref[:, c], g_ref[...]).astype(BF16)
+
+    @pl.loop(0, x_ref.shape[1] // step)
+    def _(d):
+        c = pl.ds(pl.multiple_of(d * step, step), step)
+        dwi_ref[c, :] = dot_tn(x_ref[:, c], dh_ref[...]).astype(BF16)
+
+
+def dense_block(x, g, w_inner, w_outer, rows):
+    tokens, width = x.shape
+    ff = w_inner.shape[1]
+    return pl.pallas_call(
+        functools.partial(dense_kernel, rows, 512),
+        out_shape=[
+            jax.ShapeDtypeStruct((2, 2, tokens // rows // 2, rows, width), BF16),
+            jax.ShapeDtypeStruct((width, ff), BF16),
+            jax.ShapeDtypeStruct((ff, width), BF16),
+        ],
+        scratch_shapes=[pltpu.VMEM((tokens, ff), BF16), pltpu.VMEM((tokens, ff), BF16)],
+        compiler_params=pltpu.CompilerParams(vmem_limit_bytes=56 * 1024 * 1024),
+        cost_estimate=pl.CostEstimate(
+            flops=12 * tokens * width * ff,
+            bytes_accessed=8 * tokens * width + 8 * width * ff,
+            transcendentals=tokens * ff,
+        ),
+    )(x, g, w_inner, w_outer)
+
+
+def expert_kernel(
+    rows, step, ne, x_ref, c_ref, wi_ref, wo_ref, mine_ref,
+    y_ref, dx_ref, dwi_own_ref, dwi_other_ref, dwo_own_ref, dwo_other_ref, drouter_ref,
+    act_ref, dh_ref, g_ref,
+):
+    ff = wo_ref.shape[0]
+    half = ff // 2
+    mine = mine_ref[...]
+    lanes = lax.broadcasted_iota(jnp.int32, (rows, mine.shape[1]), 1)
+
+    @pl.loop(0, x_ref.shape[0] // rows)
+    def _(t):
+        r = pl.ds(pl.multiple_of(t * rows, rows), rows)
+        hidden = dot(x_ref[r, :], wi_ref[...])
+        logits = jnp.where(lanes < ne, hidden[:, ff:], NEG)
+        raised = jnp.exp(logits - jnp.max(logits, axis=1, keepdims=True))
+        probs = raised / jnp.sum(raised, axis=1, keepdims=True)
+        gate = jnp.sum(probs * mine, axis=1, keepdims=True)
+        act, slope = gelu_pair(hidden[:, :ff])
+        act = act.astype(BF16)
+        cot = c_ref[r, :].astype(F32)
+        grad = (gate * cot).astype(BF16)
+        dh = (dot_nt(grad, wo_ref[...]) * slope).astype(BF16)
+        result = dot(act, wo_ref[...])
+        d_gate = jnp.sum(cot * result, axis=1, keepdims=True)
+        act_ref[r, :] = act
+        g_ref[r, :] = grad
+        dh_ref[r, :ff] = dh
+        dh_ref[r, ff:] = (d_gate * probs * (mine - gate)).astype(BF16)
+        y_ref[r, :] = result.astype(BF16)
+        dx_ref[r, :] = dot_nt(dh_ref[r, :], wi_ref[...]).astype(BF16)
+
+    dwo_own_ref[...] = dot_tn(act_ref[:, :half], g_ref[...])
+    dwo_other_ref[...] = dot_tn(act_ref[:, half:], g_ref[...]).astype(BF16)
+
+    @pl.loop(0, x_ref.shape[1] // step)
+    def _(d):
+        c = pl.ds(pl.multiple_of(d * step, step), step)
+        grad = dot_tn(x_ref[:, c], dh_ref[...])
+        dwi_own_ref[c, :] = grad[:, :half]
+        dwi_other_ref[c, :] = grad[:, half:ff].astype(BF16)
+        drouter_ref[c, :] = grad[:, ff:]
+
+
+def expert_block(x, cot, w_in, w_out, mine, rows, ne):
+    tokens, width = x.shape
+    ff = w_out.shape[0]
+    pad = w_in.shape[1] - ff
+    half = ff // 2
+    s = jax.ShapeDtypeStruct
+    return pl.pallas_call(
+        functools.partial(expert_kernel, rows, 256, ne),
+        out_shape=[
+            s((tokens, width), BF16), s((tokens, width), BF16),
+            s((width, half), F32), s((width, half), BF16),
+            s((half, width), F32), s((half, width), BF16),
+            s((width, pad), F32),
+        ],
+        scratch_shapes=[
+            pltpu.VMEM((tokens, ff), BF16),
+            pltpu.VMEM((tokens, ff + pad), BF16),
+            pltpu.VMEM((tokens, width), BF16),
+        ],
+        compiler_params=pltpu.CompilerParams(vmem_limit_bytes=56 * 1024 * 1024),
+        cost_estimate=pl.CostEstimate(
+            flops=12 * tokens * width * ff,
+            bytes_accessed=8 * tokens * width + 10 * width * ff,
+            transcendentals=tokens * ff,
+        ),
+    )(x, cot, w_in, w_out, mine)
+
+
 def solution(mesh):
     nd, nc, ne = (mesh.shape[a] for a in AXES)
     ndev = nd * nc * ne
@@ -201,8 +319,14 @@
     def swap_dp(x):
         return send(x, lambda d, c, e: (d ^ 1, c, e))
 
-    def swap_seq(x):
-        return send(x, lambda d, c, e: (d, e % nc, e - e % nc + c))
+    def reverse(i):
+        return int(format(i, "b").zfill(len(low_bits))[::-1], 2)
+
+    def to_seq(x):
+        return send(x, lambda d, c, e: (d, reverse(e % nc), e - e % nc + c))
+
+    def from_seq(x):
+        return send(x, lambda d, c, e: (d, e % nc, e - e % nc + reverse(c)))
 
     def my_bit(bit):
         return (lax.axis_index("exp") // bit) % 2
@@ -259,55 +383,24 @@
             parts = ordered(keep, swap_exp(away, bit), mine, 1).reshape(parts.shape)
         return parts
 
-    def line_steps(x):
-        below, above, up, down = [], [], x, x
-        for k in range(1, nc):
-            up = send(up, lambda d, c, e: (d, c + 1, e) if k - 1 <= c < nc - 1 else None)
-            down = send(down, lambda d, c, e: (d, c - 1, e) if 0 < c <= nc - k else None)
-            below.append(up)
-            above.append(down)
-        return below, above
-
-    def line_order(own, below, above):
-        stack = jnp.stack(below[::-1] + [own] + above)
-        return lax.dynamic_slice_in_dim(stack, nc - 1 - lax.axis_index("ctx"), nc)
-
-    def gather_line(x):
-        below, above = line_steps(x)
-        return line_order(x, below, above)
+    def gather_ctx(x):
+        return lax.all_to_all(
+            jnp.broadcast_to(x[None], (nc,) + x.shape), "ctx", 0, 0, tiled=True
+        )
 
     def gather_plane(x):
-        below, above = line_steps(x)
-        mine = line_order(x, below, above)
-        other = line_order(
-            swap_dp(x),
-            [send(v, lambda d, c, e: (d ^ 1, c, e) if c >= k + 1 else None) for k, v in enumerate(below)],
-            [send(v, lambda d, c, e: (d ^ 1, c, e) if c < nc - 1 - k else None) for k, v in enumerate(above)],
-        )
-        return ordered(mine, other, lax.axis_index("dp"), 0)
-
-    def scatter_line(parts):
-        c_here = lax.axis_index("ctx")
-
-        def part(j):
-            return lax.dynamic_index_in_dim(parts, jnp.clip(j, 0, nc - 1), 0, keepdims=False)
-
-        up = down = None
-        for t in range(1, nc):
-            away = nc - t
-            high, low = part(c_here + away), part(c_here - away)
-            if up is not None:
-                high = high.astype(F32) + up.astype(F32)
-                low = low.astype(F32) + down.astype(F32)
-            up = send(high.astype(BF16), lambda d, c, e: (d, c + 1, e) if c + away < nc else None)
-            down = send(low.astype(BF16), lambda d, c, e: (d, c - 1, e) if c - away >= 0 else None)
-        return part(c_here).astype(F32) + up.astype(F32) + down.astype(F32)
+        mine = gather_ctx(x)
+        return ordered(mine, swap_dp(mine), lax.axis_index("dp"), 0)
+
+    def scatter_ctx(parts):
+        parts = lax.all_to_all(parts.astype(BF16), "ctx", 0, 0, tiled=True)
+        return jnp.sum(parts.astype(F32), axis=0)
 
     def scatter_plane(parts):
         d_here = lax.axis_index("dp")
         keep = lax.dynamic_index_in_dim(parts, d_here, 0, keepdims=False)
         away = lax.dynamic_index_in_dim(parts, 1 - d_here, 0, keepdims=False)
-        return scatter_line(keep.astype(F32) + swap_dp(away.astype(BF16)).astype(F32))
+        return scatter_ctx(keep.astype(F32) + swap_dp(away.astype(BF16)).astype(F32))
 
     def per_device(
         tokens, qkv_weight, out_weight, norm1_gain, norm1_shift, norm2_gain, norm2_shift,
@@ -322,9 +415,9 @@
         e_here = lax.axis_index("exp")
         group = width // nc
 
-        x_low = swap_seq(tokens[0])
+        x_low = to_seq(tokens[0])
         ints = jnp.concatenate([segments[0], routes[0, :, 0], priority[0, 0]])
-        ints = swap_seq(ints.reshape(-1, 128)).reshape(-1)
+        ints = to_seq(ints.reshape(-1, 128)).reshape(-1)
         segs, route, order = ints[:length], ints[length : length + rows], ints[length + rows :]
 
         small = jnp.concatenate(
@@ -338,28 +431,28 @@
         )
         router = small[:, 4 * rw :].reshape(width, ne)
 
+        ff = nplane * ff_rows
         qkv_part = jnp.moveaxis(qkv_weight.reshape(rw, 3, nc, group), 2, 0)
-        qkv_part = trade_exp(qkv_part.reshape(nc, rw, 3 * group), low_bits)
-        qkv_part = gather_exp(qkv_part.reshape(nc * rw, 3 * group), high_bits)
-        qkv_rows = width // nplane
-        qkv_flat = qkv_part.reshape(-1, width)
-        bundle = gather_plane(jnp.concatenate([qkv_flat, out_weight]))
-        w_qkv = bundle[:, :, : qkv_flat.shape[0]].reshape(width, 3 * group)
-        w_out = gather_exp(bundle[:, :, qkv_flat.shape[0] :], all_bits)
-        w_out = jnp.moveaxis(w_out, 0, 2).reshape(width, width)
-
+        qkv_part = jnp.tile(qkv_part.reshape(nc, rw, 3 * group), (ne // nc, 1, 1))
         inner_part = jnp.moveaxis(inner_weight.reshape(rw, nplane, ne, ff_rows), 2, 0)
-        inner_part = trade_exp(inner_part.reshape(ne, rw, nplane * ff_rows), all_bits)
-        inner_flat = inner_part.reshape(-1, width)
+        columns = jnp.concatenate([qkv_part, inner_part.reshape(ne, rw, ff)], axis=2)
+        columns = lax.all_to_all(columns, "exp", 0, 0, tiled=True).reshape(ne * rw, -1)
+        out_part = jnp.concatenate(jnp.split(out_weight, nc, axis=1), axis=0)
+        out_part = jnp.pad(out_part, ((0, ne * rw - nc * rw), (0, 0)))
+        bundle = gather_plane(jnp.concatenate([columns[:, : 3 * group], out_part], axis=1))
+        w_qkv = bundle[..., : 3 * group].reshape(width, 3 * group)
+        w_out = bundle[:, :, : nc * rw, 3 * group :].reshape(nplane, nc, rw, group)
+        w_out = gather_exp(w_out, all_bits)
+        w_out = jnp.transpose(w_out, (1, 0, 3, 2, 4)).reshape(width, width)
+        inner_flat = columns[:, 3 * group :].reshape(-1, width)
         bundle = gather_plane(jnp.concatenate([inner_flat, outer_weight]))
-        ff = nplane * ff_rows
         w_inner = bundle[:, :, : inner_flat.shape[0]].reshape(width, ff)
         w_outer = bundle[:, :, inner_flat.shape[0] :].reshape(ff, width)
 
         e_in_own, e_out_own = expert_inner[0], expert_outer[0]
-        e_in = jnp.concatenate([e_in_own, swap_dp(e_in_own)], axis=1)
+        lanes = jnp.pad(router, ((0, 0), (0, 128 - ne)))
+        e_in = jnp.concatenate([e_in_own, swap_dp(e_in_own), lanes], axis=1)
         e_out = jnp.concatenate([e_out_own, swap_dp(e_out_own)], axis=0)
-        half = e_out_own.shape[0]
 
         x = x_low.astype(F32)
         unit1, scale1 = norm_parts(x)
@@ -373,7 +466,7 @@
         unit2, scale2 = norm_parts(residual)
         normed2 = (unit2 * gain2 + shift2).astype(BF16)
 
-        cot_low = swap_seq(cotangent[0])
+        cot_low = to_seq(cotangent[0])
         cot = cot_low.astype(F32)
         capacity = (9 * rows + 8 * ne - 1) // (8 * ne)
         same = route[:, None] == route[None, :]
@@ -386,10 +479,10 @@
         def to_experts(v):
             out = dot(table, v).astype(BF16).reshape(ne, capacity, width)
             out = trade_exp_rel(out, all_bits).reshape(slots, width)
-            return gather_line(out).reshape(nc * slots, width)
+            return gather_ctx(out).reshape(nc * slots, width)
 
         def from_experts(v):
-            back = scatter_line(v.reshape(nc, slots, width)).astype(BF16)
+            back = scatter_ctx(v.reshape(nc, slots, width)).astype(BF16)
             back = trade_exp_rel(back.reshape(ne, capacity, width), all_bits)
             return dot_tn(table, back.reshape(slots, width))
 
@@ -403,34 +496,25 @@
         d_hidden = (dot_nt(cot_all, w_outer) * slope).astype(BF16)
         dense_part = dot(act, w_outer).reshape(ne, rows, width)
         d_n2_part = dot_nt(d_hidden, w_inner).reshape(ne, rows, width)
-        dense = scatter_exp_rel(dense_part, all_bits)
-        d_n2_dense = scatter_exp_rel(d_n2_part, all_bits)
+        both = scatter_exp_rel(jnp.stack([dense_part, d_n2_part], 1), all_bits)
+        dense, d_n2_dense = both[0], both[1]
         d_outer = dot_tn(act, cot_all)
         d_inner = dot_tn(n2_all, d_hidden)
 
-        e_probs = softmax_rows(dot(e_x, router))
-        mine = (jnp.arange(ne, dtype=jnp.int32) == e_here).astype(F32)[None, :]
-        e_gate = jnp.sum(e_probs * mine, axis=1, keepdims=True)
-        e_grad = (e_gate * e_cot.astype(F32)).astype(BF16)
-        e_act, e_slope = gelu_pair(dot(e_x, e_in))
-        e_act = e_act.astype(BF16)
-        e_result = dot(e_act, e_out)
-        d_e_hidden = (dot_nt(e_grad, e_out) * e_slope).astype(BF16)
-        d_gate = jnp.sum(e_cot.astype(F32) * e_result, axis=1, keepdims=True)
-        d_logits = d_gate * e_probs * (mine - e_gate)
-        d_e_x = dot_nt(d_e_hidden, e_in) + dot_nt(d_logits, router.astype(F32))
-        d_router = dot_tn(e_x.astype(F32), d_logits)
-        d_e_out = dot_tn(e_act, e_grad)
-        d_e_in = dot_tn(e_x, d_e_hidden)
-        g_e_in = d_e_in[:, :half] + swap_dp(d_e_in[:, half:].astype(BF16)).astype(F32)
-        g_e_out = d_e_out[:half] + swap_dp(d_e_out[half:].astype(BF16)).astype(F32)
+        mine = (jnp.arange(128, dtype=jnp.int32) == e_here).astype(F32)[None, :]
+        e_result, d_e_x, own_in, other_in, own_out, other_out, d_router = expert_block(
+            e_x, e_cot, e_in, e_out, mine, nc * slots // 3, ne
+        )
+        d_router = d_router[:, :ne]
+        g_e_in = own_in + swap_dp(other_in).astype(F32)
+        g_e_out = own_out + swap_dp(other_out).astype(F32)
 
         d_n2 = d_n2_dense + from_experts(d_e_x)
         picked = from_experts(e_result)
         probs = softmax_rows(dot(normed2, router))
         chosen = (route[:, None] == jnp.arange(ne, dtype=jnp.int32)[None, :]).astype(F32)
         gate = jnp.sum(probs * chosen, axis=1, keepdims=True)
-        output = swap_seq((residual + dense + gate * picked).astype(BF16))
+        output = from_seq((residual + dense + gate * picked).astype(BF16))
 
         d_gain2 = jnp.sum(d_n2 * unit2, axis=0)
         d_shift2 = jnp.sum(d_n2, axis=0)
@@ -447,26 +531,31 @@
         d_gain1 = jnp.sum(d_normed * unit1, axis=0)
         d_shift1 = jnp.sum(d_normed, axis=0)
         d_tokens = d_residual + norm_back(d_normed, unit1, scale1, gain1)
-        d_tokens = swap_seq(d_tokens.astype(BF16)).astype(F32)
+        d_tokens = from_seq(d_tokens.astype(BF16)).astype(F32)
 
         bundle = jnp.concatenate(
             [d_inner.reshape(nd, nc, -1, width), d_outer.reshape(nd, nc, -1, width)], axis=2
         )
         bundle = scatter_plane(bundle)
         g_outer = bundle[inner_flat.shape[0] :]
-        g_inner = bundle[: inner_flat.shape[0]].astype(BF16).reshape(ne, rw, ff)
-        g_inner = trade_exp(g_inner, all_bits).reshape(ne, rw, nplane, ff_rows)
+        g_inner = bundle[: inner_flat.shape[0]].reshape(ne, rw, ff)
+
+        d_out = jnp.moveaxis(d_out.reshape(nplane, ne, rw, width), 1, 0)
+        d_out = scatter_exp(d_out, all_bits).reshape(nd, nc, rw, nc, group)
+        d_out = jnp.moveaxis(d_out, 3, 2).reshape(nd, nc, nc * rw, group)
+        d_out = jnp.pad(d_out, ((0, 0), (0, 0), (0, ne * rw - nc * rw), (0, 0)))
+        bundle = jnp.concatenate([d_w_qkv.reshape(nd, nc, ne * rw, -1), d_out], axis=3)
+        bundle = scatter_plane(bundle)
+        g_out = bundle[: nc * rw, 3 * group :].reshape(nc, rw, group)
+        g_out = jnp.moveaxis(g_out, 0, 1).reshape(rw, width)
+        g_qkv = bundle[:, : 3 * group].reshape(ne, rw, 3 * group)
+        columns = jnp.concatenate([g_qkv, g_inner], axis=2).astype(BF16)
+        columns = lax.all_to_all(columns, "exp", 0, 0, tiled=True)
+        g_inner = columns[:, :, 3 * group :].reshape(ne, rw, nplane, ff_rows)
         g_inner = jnp.transpose(g_inner, (1, 2, 0, 3)).reshape(rw, -1).astype(F32)
-
-        d_out = jnp.moveaxis(d_out.reshape(nplane, ne, rw, width), 1, 0)
-        d_out = scatter_exp(d_out, all_bits).reshape(nd, nc, rw, width)
-        bundle = jnp.concatenate([d_w_qkv.reshape(nd, nc, -1, width), d_out], axis=2)
-        bundle = scatter_plane(bundle)
-        g_out = bundle[qkv_flat.shape[0] :]
-        g_qkv = bundle[: qkv_flat.shape[0]].reshape(-1, nc * rw, 3 * group)
-        g_qkv = scatter_exp(g_qkv, high_bits).astype(BF16).reshape(nc, rw, 3 * group)
-        g_qkv = trade_exp(g_qkv, low_bits).reshape(nc, rw, 3, group)
-        g_qkv = jnp.transpose(g_qkv, (1, 2, 0, 3)).reshape(rw, 3 * width).astype(F32)
+        g_qkv = columns[:, :, : 3 * group].reshape(ne // nc, nc, rw, 3, group)
+        g_qkv = jnp.sum(g_qkv.astype(F32), axis=0)
+        g_qkv = jnp.transpose(g_qkv, (1, 2, 0, 3)).reshape(rw, 3 * width)
 
         small = jnp.concatenate([jnp.stack([d_gain1, d_shift1, d_gain2, d_shift2], 1), d_router], 1)
         small = lax.all_to_all(small.reshape(ndev, -1), AXES, 0, 0, tiled=True)

time: 743 us -> 601 us (0.81)
  starting transfers between devices: 218 us -> 126 us
  waiting for transfers between devices: 251 us -> 188 us
  other arithmetic: 58.6 us -> 89.6 us
  matrix products: 77 us -> 47.7 us
  Pallas kernels: 21.3 us -> 49.3 us
  local copies, waits for them, and re-layouts: 101 us -> 87.5 us
    ppermute x109 -> x39, starting transfers between devices: 207 us -> 38.4 us  [send(): return lax.ppermute(x, AXES, pairs)]
    ppermute x109 -> x39, waiting for transfers between devices: 251 us -> 114 us  [send(): return lax.ppermute(x, AXES, pairs)]
    all_to_all x0 -> x10, starting transfers between devices: none -> 78.1 us  [the longest x1 34 us: per_device(): columns = lax.all_to_all(columns, 'exp', 0, 0, tiled=True)]
    all_to_all x0 -> x10, waiting for transfers between devices: none -> 73.3 us  [the longest x4 31 us: gather_ctx(): lax.all_to_all(jnp.broadcast_to(x[None], (nc,) + x.shape), 'ctx', 0, 0, t...]
    pallas_call x0 -> x1, Pallas kernels: none -> 27.8 us  [expert_block(): pl.pallas_call(functools.partial(expert_kernel, rows, 256, ne), out_shape...]
    unnamed x191 -> x106, local copies, waits for them, and re-layouts: 31.5 us -> 13.9 us
    another operation x8, local copies, waits for them, and re-layouts: 1.59 us -> 12.9 us  [the longest x6 1.25 us: line_order(): stack = jnp.stack(below[::-1] + [own] + above)]
    dot_general x9 -> x6, matrix products: 27.9 us -> 16.9 us  [dot_tn(): lax.dot_general(a, b, (((0,), (0,)), ((), ())), preferred_element_type=F32)]
  transfers between devices with their start and end apart: 111 -> 51, of which waited for: 36 -> 20; matrix products, arithmetic and copies ran while one was open for 30% -> 36% of each run, Pallas kernels for 3% -> 4%
where the time goes in v2:
time: 601 us; the launch traced here: 591 us
  waiting for transfers between devices  188 us (31%)
  starting transfers between devices  126 us (21%)
  other arithmetic  89.6 us (15%)
  local copies, waits for them, and re-layouts  87.5 us (15%)
  Pallas kernels  49.3 us (8%)
  matrix products  47.7 us (8%)
    ppermute x39, waiting for transfers between devices, send(): return lax.ppermute(x, AXES, pairs)  114 us
    ppermute x39, starting transfers between devices, send(): return lax.ppermute(x, AXES, pairs)  38.4 us
    all_to_all x1, starting transfers between devices, per_device(): columns = lax.all_to_all(columns, 'exp', 0, 0, tiled=True)  34 us
    all_to_all x4, waiting for transfers between devices, gather_ctx(): lax.all_to_all(jnp.broadcast_to(x[None], (nc,) + x.shape), 'ctx', 0, 0, t...  31 us
    pallas_call x1, Pallas kernels, expert_block(): pl.pallas_call(functools.partial(expert_kernel, rows, 256, ne), out_shape...  27.8 us
    all_to_all x1, waiting for transfers between devices, per_device(): lax.all_to_all(columns, 'exp', 0, 0, tiled=True).reshape(ne * rw, -1)  19.9 us
    all_to_all x4, waiting for transfers between devices, scatter_ctx(): parts = lax.all_to_all(parts.astype(BF16), 'ctx', 0, 0, tiled=True)  19.2 us
    all_to_all x4, starting transfers between devices, gather_ctx(): lax.all_to_all(jnp.broadcast_to(x[None], (nc,) + x.shape), 'ctx', 0, 0, t...  19.1 us
  transfers between devices with their start and end apart: 51, of which 20 were waited for; matrix products, arithmetic and copies ran while one was open for 36% of the time, Pallas kernels for 4%

profile of v2, /device:TPU:4, one launch (start us, length us, event | category | flops | bytes accessed | tf_op | source)
XLA Modules:
  0.0 591.0 jit_solution(17959399736245221189)
XLA Ops:
  10.3 4.9 all-to-all-start
  24.1 5.9 %all-to-all-start.1 = ((bf16[4,32,1792]{2,1,0:T(8,128)(2,1)}), bf16[4,32,1792]{2,1,0:T(8,128)(2,1)S(1)}, u32[]{:S(2)}, u32[]{:S(2)}) async-start(bf16[4,32,1792]{2,1,0:T(8,128)(2,1)} %pad_maximum_fusion.11), calls=%async_computation.1 | async-start | bytes 917504 | tf_op jit(solution)/shard_map/all_to_all | solution.py:439
  30.3 19.9 %all-to-all-done.1 = bf16[4,32,1792]{2,1,0:T(8,128)(2,1)S(1)} async-done(((bf16[4,32,1792]{2,1,0:T(8,128)(2,1)}), bf16[4,32,1792]{2,1,0:T(8,128)(2,1)S(1)}, u32[]{:S(2)}, u32[]{:S(2)}) %all-to-all-start.1) | async-done | bytes 458784 | tf_op jit(solution)/shard_map/all_to_all | solution.py:439
  51.3 4.3 all-to-all-start.2
  56.8 13.6 %collective-permute-done.1 = bf16[1,256,1024]{2,1,0:T(8,128)(2,1)S(1)} collective-permute-done((bf16[1,256,1024]{2,1,0:T(8,128)(2,1)S(1)}, bf16[1,256,1024]{2,1,0:T(8,128)(2,1)S(1)}, u32[]{:S(2)}, u32[]{:S(2)}) %collective-permute-start.1) | collective-permute-done | bytes 524320 | tf_op jit(solution)/shard_map/ppermute | solution.py:314
  71.5 10.4 %all-to-all-done.2 = bf16[4,128,1024]{2,1,0:T(8,128)(2,1)} async-done(((bf16[4,128,1024]{2,1,0:T(8,128)(2,1)}), bf16[4,128,1024]{2,1,0:T(8,128)(2,1)}, u32[]{:S(2)}, u32[]{:S(2)}) %all-to-all-start.2) | async-done | bytes 1048608 | tf_op jit(solution)/shard_map/all_to_all | solution.py:387
  83.5 4.7 all-to-all-start.3
  97.3 17.3 %collective-permute-done.3 = bf16[4,128,1024]{2,1,0:T(8,128)(2,1)} collective-permute-done((bf16[4,128,1024]{2,1,0:T(8,128)(2,1)}, bf16[4,128,1024]{2,1,0:T(8,128)(2,1)}, u32[]{:S(2)}, u32[]{:S(2)}) %collective-permute-start.3) | collective-permute-done | bytes 1048608 | tf_op jit(solution)/shard_map/ppermute | solution.py:314
  119.4 7.4 %shard_map.255 = bf16[1024,256]{1,0:T(8,128)(2,1)S(1)} custom-call(bf16[1024,768]{1,0:T(8,128)(2,1)S(1)} %convolution_convert_fusion.q_ref.k_ref.v_ref, bf16[1024,768]{1,0:T(8,128)(2,1)S(1)} %convolution_convert_fusion.q_ref.k_ref.v_ref, bf16[1024,768]{1,0:T(8,128)(2,1)S(1)} %convolution_convert_fusion.q_ref.k_ref.v_ref, s32[1,1024]{1,0:T(1,128)S(1)} %bitcast.330, ...), custom_call_target="tpu_custom_call" | custom-call | flops 2147483648 | bytes 2097152 | tf_op jit(solution)/shard_map/pallas_call | solution.py:131
  134.0 4.7 collective-permute-done.20
  143.5 5.3 all-to-all-start.5
  168.3 12.3 %collective-permute-done.9 = bf16[1,256,1024]{2,1,0:T(8,128)(2,1)S(1)} collective-permute-done((bf16[1,256,1024]{2,1,0:T(8,128)(2,1)S(1)}, bf16[1,256,1024]{2,1,0:T(8,128)(2,1)S(1)}, u32[]{:S(2)}, u32[]{:S(2)}) %collective-permute-start.9) | collective-permute-done | bytes 524320 | tf_op jit(solution)/shard_map/ppermute | solution.py:314
  182.0 4.5 collective-permute-done.18
  187.4 14.5 %all-to-all-done.5 = bf16[4,288,1024]{2,1,0:T(8,128)(2,1)} async-done(((bf16[4,288,1024]{2,1,0:T(8,128)(2,1)}), bf16[4,288,1024]{2,1,0:T(8,128)(2,1)}, u32[]{:S(2)}, u32[]{:S(2)}) %all-to-all-start.5) | async-done | bytes 2359328 | tf_op jit(solution)/shard_map/all_to_all | solution.py:387
  204.8 4.8 all-to-all-start.4
  215.7 4.3 maximum_select_fusion
  224.2 5.7 fusion.12
  229.9 5.3 copy.253
  235.2 4.8 multiply_convert_fusion
  240.1 3.9 copy.303
  244.0 9.0 %fusion.7 = bf16[1024,1024]{0,1:T(8,128)(2,1)} fusion(f32[1024,1024]{0,1:T(8,128)} %copy.253, bf16[1024,1024]{1,0:T(8,128)(2,1)} %bitcast.365, bf16[1024,1024]{1,0:T(8,128)(2,1)} %bitcast.378), kind=kOutput, calls=%fused_computation.21 | convolution fusion | flops 2167406592 | bytes 10485760 | tf_op jit(solution)/shard_map/dot_general | solution.py:27
  253.0 3.9 copy.304
  257.0 6.0 %all-to-all-done.4 = bf16[4,288,1024]{2,1,0:T(8,128)(2,1)} async-done(((bf16[4,288,1024]{2,1,0:T(8,128)(2,1)}), bf16[4,288,1024]{2,1,0:T(8,128)(2,1)}, u32[]{:S(2)}, u32[]{:S(2)}) %all-to-all-start.4) | async-done | bytes 2359328 | tf_op jit(solution)/shard_map/all_to_all | solution.py:387
  263.0 27.8 %shard_map.256 = (bf16[1152,1024]{1,0:T(8,128)(2,1)}, bf16[1152,1024]{1,0:T(8,128)(2,1)}, f32[1024,512]{1,0:T(8,128)}, bf16[1024,512]{1,0:T(8,128)(2,1)}, f32[51...) custom-call(bf16[1152,1024]{1,0:T(8,128)(2,1)} %bitcast.73.x_ref, ...), custom_call_target="tpu_custom_call" | custom-call | flops 14495514624 | bytes 19922944 | tf_op jit(solution)/shard_map/pallas_call | solution.py:276
  290.9 4.7 all-to-all-start.7
  295.6 4.7 convolution_bitcast_fusion.1
  305.4 4.0 copy.305
  310.7 4.0 copy.281
  314.7 3.9 copy.307
  318.6 6.7 %fusion.34 = f32[2,4,128,1024]{3,2,1,0:T(8,128)} fusion(bf16[2,4,128,1024]{3,2,1,0:T(8,128)(2,1)} %bitcast.370, bf16[1024,1024]{0,1:T(8,128)(2,1)} %fusion.7), kind=kOutput, calls=%fused_computation.65 | convolution fusion | flops 2147483648 | bytes 8388608 | tf_op jit(solution)/shard_map/dot_general | solution.py:31
  325.4 4.4 fusion.16
  329.7 19.2 %all-to-all-done.7 = bf16[4,288,1024]{2,1,0:T(8,128)(2,1)} async-done(((bf16[4,288,1024]{2,1,0:T(8,128)(2,1)}), bf16[4,288,1024]{2,1,0:T(8,128)(2,1)}, u32[]{:S(2)}, u32[]{:S(2)}) %all-to-all-start.7) | async-done | bytes 2359328 | tf_op jit(solution)/shard_map/all_to_all | solution.py:396
  348.9 4.7 all-to-all-start.6
  361.5 4.7 fusion.87
  372.2 10.6 %collective-permute-done.16 = bf16[1,2,256,1024]{3,2,1,0:T(8,128)(2,1)} collective-permute-done((bf16[1,2,256,1024]{3,2,1,0:T(8,128)(2,1)}, bf16[1,2,256,1024]{3,2,1,0:T(8,128)(2,1)}, u32[]{:S(2)}, u32[]{:S(2)}) %collective-permute-start.16) | collective-permute-done | bytes 1048608 | tf_op jit(solution)/shard_map/ppermute | solution.py:314
  396.2 21.5 %collective-permute-done.36 = bf16[4,256,1024]{2,1,0:T(8,128)(2,1)} collective-permute-done((bf16[4,256,1024]{2,1,0:T(8,128)(2,1)}, bf16[4,256,1024]{2,1,0:T(8,128)(2,1)}, u32[]{:S(2)}, u32[]{:S(2)}) %collective-permute-start.36) | collective-permute-done | bytes 2097184 | tf_op jit(solution)/shard_map/ppermute | solution.py:314
  417.7 5.1 fusion.22
  424.8 5.3 all-to-all-start.9
  436.7 4.9 collective-permute-done.29
  441.7 14.1 %shard_map.257 = (bf16[1024,256]{1,0:T(8,128)(2,1)S(1)}, bf16[1024,256]{1,0:T(8,128)(2,1)S(1)}, bf16[1024,256]{1,0:T(8,128)(2,1)S(1)}) custom-call(bf16[1024,768]{1,0:T(8,128)(2,1)S(1)} %convolution_convert_fusion.q_ref.k_ref.v_ref, bf16[1024,768]{1,0:T(8,128)(2,1)S(1)} %convolution_convert_fusion.q_ref.k_ref.v_ref, ...), custom_call_target="tpu_custom_call" | custom-call | flops 5368709120 | bytes 3670016 | tf_op jit(solution)/shard_map/pallas_call | solution.py:158
  461.9 3.4 fusion.38
  469.0 6.4 %collective-permute-done.34 = bf16[1,8,32,1024]{3,2,1,0:T(8,128)(2,1)S(1)} collective-permute-done((bf16[1,8,32,1024]{3,2,1,0:T(8,128)(2,1)S(1)}, bf16[1,8,32,1024]{3,2,1,0:T(8,128)(2,1)S(1)}, u32[]{:S(2)}, u32[]{:S(2)}) %collective-permute-start.34) | collective-permute-done | bytes 524320 | tf_op jit(solution)/shard_map/ppermute | solution.py:314
  499.0 5.1 all-to-all-start.11
  510.1 4.2 all-to-all-start.8
  514.4 3.8 add_bitcast_fusion
  519.9 5.7 collective-permute-start.25
  531.7 12.0 %collective-permute-done.25 = bf16[256,1024]{1,0:T(8,128)(2,1)S(1)} collective-permute-done((bf16[256,1024]{1,0:T(8,128)(2,1)S(1)}, bf16[256,1024]{1,0:T(8,128)(2,1)S(1)}, u32[]{:S(2)}, u32[]{:S(2)}) %collective-permute-start.25) | collective-permute-done | bytes 524320 | tf_op jit(solution)/shard_map/ppermute | solution.py:314
  546.9 34.0 %all-to-all-start.10 = ((bf16[4,32,1792]{2,1,0:T(8,128)(2,1)}), bf16[4,32,1792]{2,1,0:T(8,128)(2,1)S(1)}, u32[]{:S(2)}, u32[]{:S(2)}) async-start(bf16[4,32,1792]{2,1,0:T(8,128)(2,1)} %pad_maximum_fusion.12), calls=%async_computation.10 | async-start | bytes 917504 | tf_op jit(solution)/shard_map/all_to_all | solution.py:553
  (330 shorter events, 185.9 us)
Async XLA Ops:
  1.4 55.1 %collective-permute-start.4 = (s32[12,128]{1,0:T(8,128)S(1)}, s32[12,128]{1,0:T(8,128)S(1)}, u32[]{:S(2)}, u32[]{:S(2)}) collective-permute-start(s32[12,128]{1,0:T(8,128)S(1)} %add_bitcast_fusion.2), channel_id=1, source_target_pairs={{0,0},{1,8},{2,4},{3,12},{4,1},{5,9},{6,5},{7,13},{8,2},{9,10},{10... | collective-permute-start | bytes 18440 | tf_op jit(solution)/shard_map/ppermute | solution.py:314
  10.3 13.8 %all-to-all-start = ((bf16[32,2,128]{2,1,0:T(2,128)(2,1)}), bf16[32,2,128]{2,1,0:T(2,128)(2,1)S(1)}, u32[]{:S(2)}, u32[]{:S(2)}) async-start(bf16[32,2,128]{2,1,0:T(2,128)(2,1)} %reshape.734), calls=%async_computation | async-start | bytes 32768 | tf_op jit(solution)/shard_map/all_to_all | solution.py:426
  15.2 40.4 %collective-permute-start = (bf16[256,1024]{1,0:T(8,128)(2,1)}, bf16[256,1024]{1,0:T(8,128)(2,1)S(1)}, u32[]{:S(2)}, u32[]{:S(2)}) collective-permute-start(bf16[256,1024]{1,0:T(8,128)(2,1)} %bitcast.412), channel_id=1, source_target_pairs={{0,0},{1,8},{2,4},{3,12},{4,1},{5,9},{6,5},{7,13},{8,2},{9,10},{10... | collective-permute-start | bytes 1572872 | tf_op jit(solution)/shard_map/ppermute | solution.py:314
  18.6 71.1 %collective-permute-start.12 = (bf16[256,1024]{1,0:T(8,128)(2,1)}, bf16[256,1024]{1,0:T(8,128)(2,1)}, u32[]{:S(2)}, u32[]{:S(2)}) collective-permute-start(bf16[256,1024]{1,0:T(8,128)(2,1)} %bitcast.413), channel_id=1, source_target_pairs={{0,0},{1,8},{2,4},{3,12},{4,1},{5,9},{6,5},{7,13},{8,2},{9,10},{10... | collective-permute-start | bytes 1572872 | tf_op jit(solution)/shard_map/ppermute | solution.py:314
  24.1 26.0 %all-to-all-start.1 = ((bf16[4,32,1792]{2,1,0:T(8,128)(2,1)}), bf16[4,32,1792]{2,1,0:T(8,128)(2,1)S(1)}, u32[]{:S(2)}, u32[]{:S(2)}) async-start(bf16[4,32,1792]{2,1,0:T(8,128)(2,1)} %pad_maximum_fusion.11), calls=%async_computation.1 | async-start | bytes 917504 | tf_op jit(solution)/shard_map/all_to_all | solution.py:439
  51.3 30.6 %all-to-all-start.2 = ((bf16[4,128,1024]{2,1,0:T(8,128)(2,1)}), bf16[4,128,1024]{2,1,0:T(8,128)(2,1)}, u32[]{:S(2)}, u32[]{:S(2)}) async-start(bf16[4,128,1024]{2,1,0:T(8,128)(2,1)} %broadcast_in_dim.41), calls=%async_computation.2 | async-start | bytes 2097152 | tf_op jit(solution)/shard_map/all_to_all | solution.py:387
  56.4 14.0 %collective-permute-start.1 = (bf16[1,256,1024]{2,1,0:T(8,128)(2,1)S(1)}, bf16[1,256,1024]{2,1,0:T(8,128)(2,1)S(1)}, u32[]{:S(2)}, u32[]{:S(2)}) collective-permute-start(bf16[1,256,1024]{2,1,0:T(8,128)(2,1)S(1)} %get-tuple-element.134), channel_id=1, source_target_pairs={{0,2},{1,3},{2,0},{3,1},{4,6},{5,7},{6,4},{7,5},{8,10},{9,11},{10,... | collective-permute-start | bytes 1572872 | tf_op jit(solution)/shard_map/ppermute | solution.py:314
  71.5 23.6 %collective-permute-start.2 = (bf16[2,256,1024]{2,1,0:T(8,128)(2,1)}, bf16[2,256,1024]{2,1,0:T(8,128)(2,1)}, u32[]{:S(2)}, u32[]{:S(2)}) collective-permute-start(bf16[2,256,1024]{2,1,0:T(8,128)(2,1)} %maximum_select_fusion.5), channel_id=1, source_target_pairs={{0,1},{1,0},{2,3},{3,2},{4,5},{5,4},{6,7},{7,6},{8,9},{9,8},{10,11... | collective-permute-start | bytes 3145736 | tf_op jit(solution)/shard_map/ppermute | solution.py:314
  83.5 57.1 %all-to-all-start.3 = ((bf16[4,256,1024]{2,1,0:T(8,128)(2,1)}), bf16[4,256,1024]{2,1,0:T(8,128)(2,1)}, u32[]{:S(2)}, u32[]{:S(2)}) async-start(bf16[4,256,1024]{2,1,0:T(8,128)(2,1)} %broadcast_in_dim.45), calls=%async_computation.3 | async-start | bytes 4194304 | tf_op jit(solution)/shard_map/all_to_all | solution.py:387
  88.2 26.5 %collective-permute-start.3 = (bf16[4,128,1024]{2,1,0:T(8,128)(2,1)}, bf16[4,128,1024]{2,1,0:T(8,128)(2,1)}, u32[]{:S(2)}, u32[]{:S(2)}) collective-permute-start(bf16[4,128,1024]{2,1,0:T(8,128)(2,1)} %all-to-all-done.2), channel_id=1, source_target_pairs={{0,16},{1,17},{2,18},{3,19},{4,20},{5,21},{6,22},{7,23},{8,24},{9,... | collective-permute-start | bytes 3145736 | tf_op jit(solution)/shard_map/ppermute | solution.py:314
  91.2 71.1 %collective-permute-start.21 = (bf16[1024,512]{1,0:T(8,128)(2,1)}, bf16[1024,512]{1,0:T(8,128)(2,1)}, u32[]{:S(2)}, u32[]{:S(2)}) collective-permute-start(bf16[1024,512]{1,0:T(8,128)(2,1)} %bitcast.82), channel_id=1, source_target_pairs={{0,16},{1,17},{2,18},{3,19},{4,20},{5,21},{6,22},{7,23},{8,24},{9,... | collective-permute-start | bytes 3145736 | tf_op jit(solution)/shard_map/ppermute | solution.py:314
  91.9 117.8 %collective-permute-start.22 = (bf16[512,1024]{1,0:T(8,128)(2,1)}, bf16[512,1024]{1,0:T(8,128)(2,1)}, u32[]{:S(2)}, u32[]{:S(2)}) collective-permute-start(bf16[512,1024]{1,0:T(8,128)(2,1)} %bitcast.83), channel_id=1, source_target_pairs={{0,16},{1,17},{2,18},{3,19},{4,20},{5,21},{6,22},{7,23},{8,24},{9,... | collective-permute-start | bytes 3145736 | tf_op jit(solution)/shard_map/ppermute | solution.py:314
  94.8 34.9 %collective-permute-start.13 = (bf16[1,256,1024]{2,1,0:T(8,128)(2,1)}, bf16[1,256,1024]{2,1,0:T(8,128)(2,1)S(1)}, u32[]{:S(2)}, u32[]{:S(2)}) collective-permute-start(bf16[1,256,1024]{2,1,0:T(8,128)(2,1)} %bitcast.49), channel_id=1, source_target_pairs={{0,2},{1,3},{2,0},{3,1},{4,6},{5,7},{6,4},{7,5},{8,10},{9,11},{10,... | collective-permute-start | bytes 1572872 | tf_op jit(solution)/shard_map/ppermute | solution.py:314
  117.5 10.5 %collective-permute-start.7 = (bf16[1,8,4,32,256]{4,3,2,1,0:T(8,128)(2,1)S(1)}, bf16[1,8,4,32,256]{4,3,2,1,0:T(8,128)(2,1)S(1)}, u32[]{:S(2)}, u32[]{:S(2)}) collective-permute-start(bf16[1,8,4,32,256]{4,3,2,1,0:T(8,128)(2,1)S(1)} %bitcast.344), channel_id=1, source_target_pairs={{0,2},{1,3},{2,0},{3,1},{4,6},{5,7},{6,4},{7,5},{8,10},{9,11},{10,... | collective-permute-start | bytes 1572872 | tf_op jit(solution)/shard_map/ppermute | solution.py:314
  129.1 25.5 %collective-permute-start.8 = (bf16[2,8,4,32,256]{4,3,2,1,0:T(8,128)(2,1)}, bf16[2,8,4,32,256]{4,3,2,1,0:T(8,128)(2,1)}, u32[]{:S(2)}, u32[]{:S(2)}) collective-permute-start(bf16[2,8,4,32,256]{4,3,2,1,0:T(8,128)(2,1)} %maximum_select_fusion.7), channel_id=1, source_target_pairs={{0,1},{1,0},{2,3},{3,2},{4,5},{5,4},{6,7},{7,6},{8,9},{9,8},{10,11... | collective-permute-start | bytes 3145736 | tf_op jit(solution)/shard_map/ppermute | solution.py:314
  129.7 9.0 %collective-permute-start.20 = (bf16[1,2,72,1024]{3,2,1,0:T(8,128)(2,1)S(1)}, bf16[1,2,72,1024]{3,2,1,0:T(8,128)(2,1)S(1)}, u32[]{:S(2)}, u32[]{:S(2)}) collective-permute-start(bf16[1,2,72,1024]{3,2,1,0:T(8,128)(2,1)S(1)} %get-tuple-element.126), channel_id=1, source_target_pairs={{0,2},{1,3},{2,0},{3,1},{4,6},{5,7},{6,4},{7,5},{8,10},{9,11},{10,... | collective-permute-start | bytes 884744 | tf_op jit(solution)/shard_map/ppermute | solution.py:314
  133.1 79.6 %collective-permute-start.14 = (bf16[2,256,1024]{2,1,0:T(8,128)(2,1)}, bf16[2,256,1024]{2,1,0:T(8,128)(2,1)}, u32[]{:S(2)}, u32[]{:S(2)}) collective-permute-start(bf16[2,256,1024]{2,1,0:T(8,128)(2,1)} %get-tuple-element.114), channel_id=1, source_target_pairs={{0,1},{1,0},{2,3},{3,2},{4,5},{5,4},{6,7},{7,6},{8,9},{9,8},{10,11... | collective-permute-start | bytes 3145736 | tf_op jit(solution)/shard_map/ppermute | solution.py:314
  138.7 10.1 %collective-permute-start.6 = (bf16[1,2,256,256]{3,2,1,0:T(8,128)(2,1)}, bf16[1,2,256,256]{3,2,1,0:T(8,128)(2,1)}, u32[]{:S(2)}, u32[]{:S(2)}) collective-permute-start(bf16[1,2,256,256]{3,2,1,0:T(8,128)(2,1)} %get-tuple-element.140), channel_id=1, source_target_pairs={{0,2},{1,3},{2,0},{3,1},{4,6},{5,7},{6,4},{7,5},{8,10},{9,11},{10,... | collective-permute-start | bytes 786440 | tf_op jit(solution)/shard_map/ppermute | solution.py:314
  143.5 58.4 %all-to-all-start.5 = ((bf16[4,288,1024]{2,1,0:T(8,128)(2,1)}), bf16[4,288,1024]{2,1,0:T(8,128)(2,1)}, u32[]{:S(2)}, u32[]{:S(2)}) async-start(bf16[4,288,1024]{2,1,0:T(8,128)(2,1)} %broadcast_in_dim.51), calls=%async_computation.5 | async-start | bytes 4718592 | tf_op jit(solution)/shard_map/all_to_all | solution.py:387
  153.1 62.6 %collective-permute-start.11 = (bf16[4,256,1024]{2,1,0:T(8,128)(2,1)}, bf16[4,256,1024]{2,1,0:T(8,128)(2,1)}, u32[]{:S(2)}, u32[]{:S(2)}) collective-permute-start(bf16[4,256,1024]{2,1,0:T(8,128)(2,1)} %all-to-all-done.3), channel_id=1, source_target_pairs={{0,16},{1,17},{2,18},{3,19},{4,20},{5,21},{6,22},{7,23},{8,24},{9,... | collective-permute-start | bytes 6291464 | tf_op jit(solution)/shard_map/ppermute | solution.py:314
  165.8 14.8 %collective-permute-start.9 = (bf16[1,256,1024]{2,1,0:T(8,128)(2,1)S(1)}, bf16[1,256,1024]{2,1,0:T(8,128)(2,1)S(1)}, u32[]{:S(2)}, u32[]{:S(2)}) collective-permute-start(bf16[1,256,1024]{2,1,0:T(8,128)(2,1)S(1)} %fusion.113), channel_id=1, source_target_pairs={{0,2},{1,3},{2,0},{3,1},{4,6},{5,7},{6,4},{7,5},{8,10},{9,11},{10,... | collective-permute-start | bytes 1572872 | tf_op jit(solution)/shard_map/ppermute | solution.py:314
  166.6 19.9 %collective-permute-start.18 = (bf16[1,2,72,1024]{3,2,1,0:T(8,128)(2,1)S(1)}, bf16[1,2,72,1024]{3,2,1,0:T(8,128)(2,1)S(1)}, u32[]{:S(2)}, u32[]{:S(2)}) collective-permute-start(bf16[1,2,72,1024]{3,2,1,0:T(8,128)(2,1)S(1)} %get-tuple-element.130), channel_id=1, source_target_pairs={{0,2},{1,3},{2,0},{3,1},{4,6},{5,7},{6,4},{7,5},{8,10},{9,11},{10,... | collective-permute-start | bytes 884744 | tf_op jit(solution)/shard_map/ppermute | solution.py:314
  182.0 39.8 %collective-permute-start.10 = (bf16[2,256,1024]{2,1,0:T(8,128)(2,1)}, bf16[2,256,1024]{2,1,0:T(8,128)(2,1)}, u32[]{:S(2)}, u32[]{:S(2)}) collective-permute-start(bf16[2,256,1024]{2,1,0:T(8,128)(2,1)} %get-tuple-element.116), channel_id=1, source_target_pairs={{0,1},{1,0},{2,3},{3,2},{4,5},{5,4},{6,7},{7,6},{8,9},{9,8},{10,11... | collective-permute-start | bytes 3145736 | tf_op jit(solution)/shard_map/ppermute | solution.py:314
  204.8 58.2 %all-to-all-start.4 = ((bf16[4,288,1024]{2,1,0:T(8,128)(2,1)}), bf16[4,288,1024]{2,1,0:T(8,128)(2,1)}, u32[]{:S(2)}, u32[]{:S(2)}) async-start(bf16[4,288,1024]{2,1,0:T(8,128)(2,1)} %broadcast_in_dim.49), calls=%async_computation.4 | async-start | bytes 4718592 | tf_op jit(solution)/shard_map/all_to_all | solution.py:387
  290.9 58.1 %all-to-all-start.7 = ((bf16[4,288,1024]{2,1,0:T(8,128)(2,1)}), bf16[4,288,1024]{2,1,0:T(8,128)(2,1)}, u32[]{:S(2)}, u32[]{:S(2)}) async-start(bf16[4,288,1024]{2,1,0:T(8,128)(2,1)} %bitcast.353), calls=%async_computation.7 | async-start | bytes 4718592 | tf_op jit(solution)/shard_map/all_to_all | solution.py:396
  305.4 20.0 %collective-permute-start.15 = (bf16[2,2,256,1024]{3,2,1,0:T(8,128)(2,1)}, bf16[2,2,256,1024]{3,2,1,0:T(8,128)(2,1)}, u32[]{:S(2)}, u32[]{:S(2)}) collective-permute-start(bf16[2,2,256,1024]{3,2,1,0:T(8,128)(2,1)} %fusion.25), channel_id=1, source_target_pairs={{0,1},{1,0},{2,3},{3,2},{4,5},{5,4},{6,7},{7,6},{8,9},{9,8},{10,11... | collective-permute-start | bytes 6291464 | tf_op jit(solution)/shard_map/ppermute | solution.py:314
  348.9 75.9 %all-to-all-start.6 = ((bf16[4,288,1024]{2,1,0:T(8,128)(2,1)}), bf16[4,288,1024]{2,1,0:T(8,128)(2,1)}, u32[]{:S(2)}, u32[]{:S(2)}) async-start(bf16[4,288,1024]{2,1,0:T(8,128)(2,1)} %bitcast.352), calls=%async_computation.6 | async-start | bytes 4718592 | tf_op jit(solution)/shard_map/all_to_all | solution.py:396
  356.4 26.4 %collective-permute-start.16 = (bf16[1,2,256,1024]{3,2,1,0:T(8,128)(2,1)}, bf16[1,2,256,1024]{3,2,1,0:T(8,128)(2,1)}, u32[]{:S(2)}, u32[]{:S(2)}) collective-permute-start(bf16[1,2,256,1024]{3,2,1,0:T(8,128)(2,1)} %fusion.57), channel_id=1, source_target_pairs={{0,2},{1,3},{2,0},{3,1},{4,6},{5,7},{6,4},{7,5},{8,10},{9,11},{10,... | collective-permute-start | bytes 3145736 | tf_op jit(solution)/shard_map/ppermute | solution.py:314
  361.5 9.4 %collective-permute-start.26 = (bf16[2,1,72,1024]{3,2,0,1:T(8,128)(2,1)S(1)}, bf16[2,1,72,1024]{3,2,0,1:T(8,128)(2,1)S(1)}, u32[]{:S(2)}, u32[]{:S(2)}) collective-permute-start(bf16[2,1,72,1024]{3,2,0,1:T(8,128)(2,1)S(1)} %get-tuple-element.120), channel_id=1, source_target_pairs={{0,1},{1,0},{2,3},{3,2},{4,5},{5,4},{6,7},{7,6},{8,9},{9,8},{10,11... | collective-permute-start | bytes 884744 | tf_op jit(solution)/shard_map/ppermute | solution.py:314
  369.4 48.3 %collective-permute-start.36 = (bf16[4,256,1024]{2,1,0:T(8,128)(2,1)}, bf16[4,256,1024]{2,1,0:T(8,128)(2,1)}, u32[]{:S(2)}, u32[]{:S(2)}) collective-permute-start(bf16[4,256,1024]{2,1,0:T(8,128)(2,1)} %fusion.26), channel_id=1, source_target_pairs={{0,16},{1,17},{2,18},{3,19},{4,20},{5,21},{6,22},{7,23},{8,24},{9,... | collective-permute-start | bytes 6291464 | tf_op jit(solution)/shard_map/ppermute | solution.py:314
  371.0 16.1 %collective-permute-start.27 = (bf16[1,2,72,1024]{3,2,1,0:T(8,128)(2,1)S(1)}, bf16[1,2,72,1024]{3,2,1,0:T(8,128)(2,1)S(1)}, u32[]{:S(2)}, u32[]{:S(2)}) collective-permute-start(bf16[1,2,72,1024]{3,2,1,0:T(8,128)(2,1)S(1)} %get-tuple-element.118), channel_id=1, source_target_pairs={{0,2},{1,3},{2,0},{3,1},{4,6},{5,7},{6,4},{7,5},{8,10},{9,11},{10,... | collective-permute-start | bytes 884744 | tf_op jit(solution)/shard_map/ppermute | solution.py:314
  396.2 37.0 %collective-permute-start.28 = (bf16[2,1,256,256]{3,2,0,1:T(8,128)(2,1)}, bf16[2,1,256,256]{3,2,0,1:T(8,128)(2,1)}, u32[]{:S(2)}, u32[]{:S(2)}) collective-permute-start(bf16[2,1,256,256]{3,2,0,1:T(8,128)(2,1)} %get-tuple-element.138), channel_id=1, source_target_pairs={{0,1},{1,0},{2,3},{3,2},{4,5},{5,4},{6,7},{7,6},{8,9},{9,8},{10,11... | collective-permute-start | bytes 786440 | tf_op jit(solution)/shard_map/ppermute | solution.py:314
  422.8 60.1 %collective-permute-start.37 = (bf16[1024,512]{1,0:T(8,128)(2,1)}, bf16[1024,512]{1,0:T(8,128)(2,1)}, u32[]{:S(2)}, u32[]{:S(2)}) collective-permute-start(bf16[1024,512]{1,0:T(8,128)(2,1)} %get-tuple-element.30), channel_id=1, source_target_pairs={{0,16},{1,17},{2,18},{3,19},{4,20},{5,21},{6,22},{7,23},{8,24},{9,... | collective-permute-start | bytes 3145736 | tf_op jit(solution)/shard_map/ppermute | solution.py:314
  424.3 90.1 %collective-permute-start.38 = (bf16[512,1024]{1,0:T(8,128)(2,1)}, bf16[512,1024]{1,0:T(8,128)(2,1)}, u32[]{:S(2)}, u32[]{:S(2)}) collective-permute-start(bf16[512,1024]{1,0:T(8,128)(2,1)} %get-tuple-element.32), channel_id=1, source_target_pairs={{0,16},{1,17},{2,18},{3,19},{4,20},{5,21},{6,22},{7,23},{8,24},{9,... | collective-permute-start | bytes 3145736 | tf_op jit(solution)/shard_map/ppermute | solution.py:314
  424.8 74.2 %all-to-all-start.9 = ((bf16[4,256,1024]{2,1,0:T(8,128)(2,1)}), bf16[4,256,1024]{2,1,0:T(8,128)(2,1)}, u32[]{:S(2)}, u32[]{:S(2)}) async-start(bf16[4,256,1024]{2,1,0:T(8,128)(2,1)} %fusion.22), calls=%async_computation.9 | async-start | bytes 4194304 | tf_op jit(solution)/shard_map/all_to_all | solution.py:396
  434.5 7.1 %collective-permute-start.29 = (bf16[1,2,256,256]{3,2,1,0:T(8,128)(2,1)S(1)}, bf16[1,2,256,256]{3,2,1,0:T(8,128)(2,1)S(1)}, u32[]{:S(2)}, u32[]{:S(2)}) collective-permute-start(bf16[1,2,256,256]{3,2,1,0:T(8,128)(2,1)S(1)} %get-tuple-element.136), channel_id=1, source_target_pairs={{0,2},{1,3},{2,0},{3,1},{4,6},{5,7},{6,4},{7,5},{8,10},{9,11},{10,... | collective-permute-start | bytes 786440 | tf_op jit(solution)/shard_map/ppermute | solution.py:314
  436.7 23.6 %collective-permute-start.33 = (bf16[2,8,32,1024]{3,2,1,0:T(8,128)(2,1)S(1)}, bf16[2,8,32,1024]{3,2,1,0:T(8,128)(2,1)S(1)}, u32[]{:S(2)}, u32[]{:S(2)}) collective-permute-start(bf16[2,8,32,1024]{3,2,1,0:T(8,128)(2,1)S(1)} %fusion.55), channel_id=1, source_target_pairs={{0,1},{1,0},{2,3},{3,2},{4,5},{5,4},{6,7},{7,6},{8,9},{9,8},{10,11... | collective-permute-start | bytes 3145736 | tf_op jit(solution)/shard_map/ppermute | solution.py:314
  459.2 6.1 %collective-permute-start.30 = (bf16[2,256,1024]{2,1,0:T(8,128)(2,1)S(1)}, bf16[2,256,1024]{2,1,0:T(8,128)(2,1)S(1)}, u32[]{:S(2)}, u32[]{:S(2)}) collective-permute-start(bf16[2,256,1024]{2,1,0:T(8,128)(2,1)S(1)} %fusion.56), channel_id=1, source_target_pairs={{0,1},{1,0},{2,3},{3,2},{4,5},{5,4},{6,7},{7,6},{8,9},{9,8},{10,11... | collective-permute-start | bytes 3145736 | tf_op jit(solution)/shard_map/ppermute | solution.py:314
  460.2 25.7 %collective-permute-start.23 = (bf16[2,1,72,1024]{3,2,0,1:T(8,128)(2,1)S(1)}, bf16[2,1,72,1024]{3,2,0,1:T(8,128)(2,1)}, u32[]{:S(2)}, u32[]{:S(2)}) collective-permute-start(bf16[2,1,72,1024]{3,2,0,1:T(8,128)(2,1)S(1)} %get-tuple-element.124), channel_id=1, source_target_pairs={{0,1},{1,0},{2,3},{3,2},{4,5},{5,4},{6,7},{7,6},{8,9},{9,8},{10,11... | collective-permute-start | bytes 884744 | tf_op jit(solution)/shard_map/ppermute | solution.py:314
  460.7 14.8 %collective-permute-start.34 = (bf16[1,8,32,1024]{3,2,1,0:T(8,128)(2,1)S(1)}, bf16[1,8,32,1024]{3,2,1,0:T(8,128)(2,1)S(1)}, u32[]{:S(2)}, u32[]{:S(2)}) collective-permute-start(bf16[1,8,32,1024]{3,2,1,0:T(8,128)(2,1)S(1)} %dynamic-slice_convert_fusion), channel_id=1, source_target_pairs={{0,2},{1,3},{2,0},{3,1},{4,6},{5,7},{6,4},{7,5},{8,10},{9,11},{10,... | collective-permute-start | bytes 1572872 | tf_op jit(solution)/shard_map/ppermute | solution.py:314
  468.0 22.2 %collective-permute-start.31 = (bf16[1,256,1024]{2,1,0:T(8,128)(2,1)}, bf16[1,256,1024]{2,1,0:T(8,128)(2,1)}, u32[]{:S(2)}, u32[]{:S(2)}) collective-permute-start(bf16[1,256,1024]{2,1,0:T(8,128)(2,1)} %dynamic-slice_convert_fusion.1), channel_id=1, source_target_pairs={{0,2},{1,3},{2,0},{3,1},{4,6},{5,7},{6,4},{7,5},{8,10},{9,11},{10,... | collective-permute-start | bytes 1572872 | tf_op jit(solution)/shard_map/ppermute | solution.py:314
  481.5 24.8 %collective-permute-start.35 = (bf16[4,128,1024]{2,1,0:T(8,128)(2,1)}, bf16[4,128,1024]{2,1,0:T(8,128)(2,1)}, u32[]{:S(2)}, u32[]{:S(2)}) collective-permute-start(bf16[4,128,1024]{2,1,0:T(8,128)(2,1)} %fusion.58), channel_id=1, source_target_pairs={{0,16},{1,17},{2,18},{3,19},{4,20},{5,21},{6,22},{7,23},{8,24},{9,... | collective-permute-start | bytes 3145736 | tf_op jit(solution)/shard_map/ppermute | solution.py:314
  487.7 30.5 %collective-permute-start.24 = (bf16[1,2,72,1024]{3,2,1,0:T(8,128)(2,1)}, bf16[1,2,72,1024]{3,2,1,0:T(8,128)(2,1)}, u32[]{:S(2)}, u32[]{:S(2)}) collective-permute-start(bf16[1,2,72,1024]{3,2,1,0:T(8,128)(2,1)} %get-tuple-element.122), channel_id=1, source_target_pairs={{0,2},{1,3},{2,0},{3,1},{4,6},{5,7},{6,4},{7,5},{8,10},{9,11},{10,... | collective-permute-start | bytes 884744 | tf_op jit(solution)/shard_map/ppermute | solution.py:314
  499.0 11.1 %all-to-all-start.11 = ((f32[32,1,256]{2,1,0:T(1,128)}), f32[32,1,256]{2,1,0:T(1,128)S(1)}, u32[]{:S(2)}, u32[]{:S(2)}) async-start(f32[32,1,256]{2,1,0:T(1,128)} %all_to_all.56), calls=%async_computation.11 | async-start | bytes 65536 | tf_op jit(solution)/shard_map/all_to_all | solution.py:561
  510.1 34.5 %all-to-all-start.8 = ((bf16[4,128,1024]{2,1,0:T(8,128)(2,1)}), bf16[4,128,1024]{2,1,0:T(8,128)(2,1)}, u32[]{:S(2)}, u32[]{:S(2)}) async-start(bf16[4,128,1024]{2,1,0:T(8,128)(2,1)} %fusion.32), calls=%async_computation.8 | async-start | bytes 2097152 | tf_op jit(solution)/shard_map/all_to_all | solution.py:396
  519.9 23.8 %collective-permute-start.25 = (bf16[256,1024]{1,0:T(8,128)(2,1)S(1)}, bf16[256,1024]{1,0:T(8,128)(2,1)S(1)}, u32[]{:S(2)}, u32[]{:S(2)}) collective-permute-start(bf16[256,1024]{1,0:T(8,128)(2,1)S(1)} %fusion.62), channel_id=1, source_target_pairs={{0,0},{1,4},{2,8},{3,12},{4,2},{5,6},{6,10},{7,14},{8,1},{9,5},{10... | collective-permute-start | bytes 1572872 | tf_op jit(solution)/shard_map/ppermute | solution.py:314
  526.9 54.8 %collective-permute-start.32 = (bf16[256,1024]{1,0:T(8,128)(2,1)}, bf16[256,1024]{1,0:T(8,128)(2,1)S(1)}, u32[]{:S(2)}, u32[]{:S(2)}) collective-permute-start(bf16[256,1024]{1,0:T(8,128)(2,1)} %fusion.52), channel_id=1, source_target_pairs={{0,0},{1,4},{2,8},{3,12},{4,2},{5,6},{6,10},{7,14},{8,1},{9,5},{10... | collective-permute-start | bytes 1572872 | tf_op jit(solution)/shard_map/ppermute | solution.py:314
  546.9 39.8 %all-to-all-start.10 = ((bf16[4,32,1792]{2,1,0:T(8,128)(2,1)}), bf16[4,32,1792]{2,1,0:T(8,128)(2,1)S(1)}, u32[]{:S(2)}, u32[]{:S(2)}) async-start(bf16[4,32,1792]{2,1,0:T(8,128)(2,1)} %pad_maximum_fusion.12), calls=%async_computation.10 | async-start | bytes 917504 | tf_op jit(solution)/shard_map/all_to_all | solution.py:553
  (47 other events, 238.1 us)

commit v3 on v2

v3 whole, which is shorter than its diff:
```python
import functools
import math

import jax
import jax.numpy as jnp
from jax import lax
from jax.experimental import pallas as pl
from jax.experimental.pallas import tpu as pltpu
from jax.sharding import PartitionSpec as P

HEADS = 16
HEAD_DIM = 64
AXES = ("dp", "ctx", "exp")
EPS = 1e-05
NEG = -1e30
GELU_A = 0.7978845608028654
GELU_B = 0.044715
SPREAD = 10
F32 = jnp.float32
BF16 = jnp.bfloat16


def dot(a, b):
    return jnp.dot(a, b, preferred_element_type=F32)


def dot_nt(a, b):
    return lax.dot_general(a, b, (((1,), (1,)), ((), ())), preferred_element_type=F32)


def dot_tn(a, b):
    return lax.dot_general(a, b, (((0,), (0,)), ((), ())), preferred_element_type=F32)


def norm_parts(z):
    average = jnp.mean(z, axis=-1, keepdims=True)
    centred = z - average
    scale = lax.rsqrt(jnp.mean(centred * centred, axis=-1, keepdims=True) + EPS)
    return centred * scale, scale


def norm_back(grad, unit, scale, gain):
    w = grad * gain
    return scale * (
        w
        - jnp.mean(w, axis=-1, keepdims=True)
        - unit * jnp.mean(w * unit, axis=-1, keepdims=True)
    )


def gelu_pair(u):
    square = u * u
    t = jnp.tanh(u * (GELU_A + GELU_A * GELU_B * square))
    half = 0.5 * (1.0 + t)
    return u * half, half + 0.5 * u * (1.0 - t * t) * (GELU_A + 3.0 * GELU_A * GELU_B * square)


def softmax_rows(v):
    raised = jnp.exp(v - jnp.max(v, axis=-1, keepdims=True))
    return raised / jnp.sum(raised, axis=-1, keepdims=True)


def assemble(full_ref, own, other, here):
    half = full_ref.shape[0] // 2
    full_ref[pl.ds(pl.multiple_of(here * half, half), half), :] = own
    full_ref[pl.ds(pl.multiple_of((1 - here) * half, half), half), :] = other


def assemble_attention(n, own_ref, other_ref, w_ref, wo_ref, here):
    planes, rows, width = own_ref.shape
    group = width // n
    small = wo_ref.shape[0] // (2 * planes)
    for ref, d in ((own_ref, here), (other_ref, 1 - here)):
        for c in range(planes):
            at = pl.multiple_of((d * planes + c) * rows, rows)
            w_ref[pl.ds(at, rows), :] = ref[c, :, : 3 * group]
            at = pl.multiple_of((d * planes + c) * small, small)
            for g in range(n):
                wo_ref[pl.ds(at, small), g * group : (g + 1) * group] = ref[
                    c, g * small : (g + 1) * small, 3 * group :
                ]


def attention_fwd_kernel(n, where_ref, *refs):
    xs, refs = refs[:n], refs[n:]
    own_ref, other_ref, segrow_ref, segcol_ref = refs[:4]
    qkv_ref, att_ref, keep_ref, away_ref, w_ref, wo_ref = refs[4:]
    block = xs[0].shape[0]
    group = att_ref.shape[1]
    pair = 2 * HEAD_DIM
    low, here = where_ref[0], where_ref[1]
    scale = 1.0 / math.sqrt(HEAD_DIM)
    assemble_attention(n, own_ref, other_ref, w_ref, wo_ref, here)

    def natural(i):
        return pl.ds(pl.multiple_of((low ^ i) * block, block), block)

    for i in range(n):
        qkv_ref[natural(i), :] = dot(xs[i][...], w_ref[...]).astype(BF16)

    first = lax.broadcasted_iota(jnp.int32, (block, pair), 1) < HEAD_DIM

    @pl.loop(0, group // pair)
    def _(p):
        lanes = [pl.ds(pl.multiple_of(j * group + p * pair, pair), pair) for j in range(3)]
        for i in range(n):
            ext = (i + 1) * block
            rows = pl.ds(i * block, block)
            q = qkv_ref[rows, lanes[0]] * jnp.asarray(scale, BF16)
            k = qkv_ref[pl.ds(0, ext), lanes[1]]
            v = qkv_ref[pl.ds(0, ext), lanes[2]]
            qpos = lax.broadcasted_iota(jnp.int32, (block, ext), 0) + i * block
            kpos = lax.broadcasted_iota(jnp.int32, (block, ext), 1)
            visible = jnp.logical_and(
                kpos <= qpos, segcol_ref[rows, :] == segrow_ref[:, pl.ds(0, ext)]
            )
            outs = []
            for half in range(2):
                mine = first if half == 0 else jnp.logical_not(first)
                s = jnp.where(visible, dot_nt(jnp.where(mine, q, jnp.zeros_like(q)), k), NEG)
                e = jnp.exp(s - jnp.max(s, axis=1, keepdims=True))
                outs.append(dot(e.astype(BF16), v) / jnp.sum(e, axis=1, keepdims=True))
            att_ref[rows, lanes[0]] = jnp.where(first, outs[0], outs[1]).astype(BF16)

    for i in range(n):
        part = dot(att_ref[natural(i), :], wo_ref[...]).astype(BF16)
        (away_ref if i % 2 else keep_ref)[i // 2] = part


def attention_bwd_kernel(n, where_ref, *refs):
    ds_in, xs, refs = refs[:n], refs[n : 2 * n], refs[2 * n :]
    own_ref, other_ref, segrow_ref, segcol_ref, qkv_ref, att_ref = refs[:6]
    keep_ref, away_ref, gown_ref, gother_ref = refs[6:10]
    w_ref, wo_ref, x_ref, db_ref, do_ref, dqkv_ref, dk_acc, dv_acc = refs[10:]
    block = xs[0].shape[0]
    length, group = att_ref.shape
    width = x_ref.shape[1]
    planes, wrows = own_ref.shape[:2]
    small = group // (2 * planes)
    pair = 2 * HEAD_DIM
    low, here = where_ref[0], where_ref[1]
    scale = 1.0 / math.sqrt(HEAD_DIM)
    assemble_attention(n, own_ref, other_ref, w_ref, wo_ref, here)

    def natural(i):
        return pl.ds(pl.multiple_of((low ^ i) * block, block), block)

    for i in range(n):
        x_ref[natural(i), :] = xs[i][...]
        db_ref[natural(i), :] = ds_in[i][...]
        do_ref[natural(i), :] = dot_nt(ds_in[i][...], wo_ref[...]).astype(BF16)

    first = lax.broadcasted_iota(jnp.int32, (block, pair), 1) < HEAD_DIM

    @pl.loop(0, group // pair)
    def _(p):
        lanes = [pl.ds(pl.multiple_of(j * group + p * pair, pair), pair) for j in range(3)]
        dk_acc[...] = jnp.zeros_like(dk_acc)
        dv_acc[...] = jnp.zeros_like(dv_acc)
        for i in range(n):
            ext = (i + 1) * block
            rows = pl.ds(i * block, block)
            keys = pl.ds(0, ext)
            q = qkv_ref[rows, lanes[0]] * jnp.asarray(scale, BF16)
            do = do_ref[rows, lanes[0]]
            k = qkv_ref[keys, lanes[1]]
            v = qkv_ref[keys, lanes[2]]
            qpos = lax.broadcasted_iota(jnp.int32, (ext, block), 1) + i * block
            kpos = lax.broadcasted_iota(jnp.int32, (ext, block), 0)
            visible = jnp.logical_and(kpos <= qpos, segcol_ref[keys, :] == segrow_ref[:, rows])
            dq = []
            for half in range(2):
                mine = first if half == 0 else jnp.logical_not(first)
                qh = jnp.where(mine, q, jnp.zeros_like(q))
                doh = jnp.where(mine, do, jnp.zeros_like(do))
                s = jnp.where(visible, dot_nt(k, qh), NEG)
                e = jnp.exp(s - jnp.max(s, axis=0, keepdims=True))
                e = e * (1.0 / jnp.sum(e, axis=0, keepdims=True))
                dp = dot_nt(v, doh)
                delta = jnp.sum(e * dp, axis=0, keepdims=True)
                ds = (e * (dp - delta)).astype(BF16)
                dv_acc[keys, :] += dot(e.astype(BF16), doh)
                dk_acc[keys, :] += dot(ds, qh)
                dq.append(dot_tn(ds, k))
            dqkv_ref[rows, lanes[0]] = (jnp.where(first, dq[0], dq[1]) * scale).astype(BF16)
        dqkv_ref[:, lanes[1]] = dk_acc[...].astype(BF16)
        dqkv_ref[:, lanes[2]] = dv_acc[...].astype(BF16)

    for i in range(n):
        part = dot_nt(dqkv_ref[natural(i), :], w_ref[...]).astype(BF16)
        (away_ref if i % 2 else keep_ref)[i // 2] = part
    wo_ref[...] = dot_tn(att_ref[...], db_ref[...]).astype(BF16)
    for ref, d in ((gown_ref, here), (gother_ref, 1 - here)):
        at = pl.ds(pl.multiple_of(d * (width // 2), width // 2), width // 2)
        grad = dot_tn(x_ref[:, at], dqkv_ref[...]).astype(BF16)
        for c in range(planes):
            ref[c, :, : 3 * group] = grad[c * wrows : (c + 1) * wrows]
            at = pl.multiple_of((d * planes + c) * small, small)
            for g in range(n):
                ref[c, g * small : (g + 1) * small, 3 * group :] = wo_ref[
                    pl.ds(at, small), g * group : (g + 1) * group
                ]


def vmem_call(kernel, out_shape, scratch, flops, transcendentals, where, *args):
    bytes_of = lambda a: math.prod(a.shape) * a.dtype.itemsize
    vmem = pl.BlockSpec(memory_space=pltpu.VMEM)
    return pl.pallas_call(
        kernel,
        in_specs=[pl.BlockSpec(memory_space=pltpu.SMEM)] + [vmem] * len(args),
        out_specs=[vmem] * len(out_shape),
        out_shape=out_shape,
        scratch_shapes=scratch,
        compiler_params=pltpu.CompilerParams(vmem_limit_bytes=60 * 1024 * 1024),
        cost_estimate=pl.CostEstimate(
            flops=SPREAD * flops,
            bytes_accessed=sum(map(bytes_of, args)) + sum(map(bytes_of, out_shape)),
            transcendentals=transcendentals,
        ),
    )(where, *args)


def shape16(*dims):
    return jax.ShapeDtypeStruct(dims, BF16)


def attention_fwd(where, xs, own, other, segs):
    n, (block, width) = len(xs), xs[0].shape
    length, group = n * block, width // n
    return vmem_call(
        functools.partial(attention_fwd_kernel, n),
        [
            shape16(length, 3 * group), shape16(length, group),
            shape16(n // 2, block, width), shape16(n // 2, block, width),
        ],
        [pltpu.VMEM((width, 3 * group), BF16), pltpu.VMEM((group, width), BF16)],
        8 * length * width * group + 8 * length * length * group,
        length * length * group // HEAD_DIM // 2,
        where, *xs, own, other, segs[None, :], segs[:, None],
    )


def attention_bwd(where, d_branch, xs, own, other, segs, qkv, att):
    n, (block, width) = len(xs), xs[0].shape
    length, group = n * block, width // n
    return vmem_call(
        functools.partial(attention_bwd_kernel, n),
        [
            shape16(n // 2, block, width), shape16(n // 2, block, width),
            shape16(*own.shape), shape16(*own.shape),
        ],
        [
            pltpu.VMEM((width, 3 * group), BF16), pltpu.VMEM((group, width), BF16),
            pltpu.VMEM((length, width), BF16), pltpu.VMEM((length, width), BF16),
            pltpu.VMEM((length, group), BF16), pltpu.VMEM((length, 3 * group), BF16),
            pltpu.VMEM((length, 2 * HEAD_DIM), F32), pltpu.VMEM((length, 2 * HEAD_DIM), F32),
        ],
        16 * length * width * group + 20 * length * length * group,
        length * length * group // HEAD_DIM // 2,
        where, *d_branch, *xs, own, other, segs[None, :], segs[:, None], qkv, att,
    )


def dense_kernel(n, ff, where_ref, *refs):
    xs, gs, refs = refs[:n], refs[n : 2 * n], refs[2 * n :]
    own_ref, other_ref, keep_ref, away_ref, gown_ref, gother_ref = refs[:6]
    wi_ref, wo_ref, x_ref, g_ref, act_ref, dh_ref = refs[6:]
    rows, width = xs[0].shape
    planes = own_ref.shape[0]
    here = where_ref[1]
    inner, outer = width // (2 * planes), ff // (2 * planes)
    for ref, d in ((own_ref, here), (other_ref, 1 - here)):
        for c in range(planes):
            at = pl.multiple_of((d * planes + c) * inner, inner)
            for g in range(width // ff):
                wi_ref[pl.ds(at + g * (inner * ff // width), inner * ff // width), :] = ref[
                    c, : inner * ff // width, g * ff : (g + 1) * ff
                ]
            at = pl.multiple_of((d * planes + c) * outer, outer)
            wo_ref[pl.ds(at, outer), :] = ref[c, inner * ff // width :, :]
    for i in range(n):
        x_ref[pl.ds(i * rows, rows), :] = xs[i][...]
        g_ref[pl.ds(i * rows, rows), :] = gs[i][...]

    @pl.loop(0, n // 2)
    def _(t):
        for odd, out_ref in ((0, keep_ref), (1, away_ref)):
            r = pl.ds(pl.multiple_of((2 * t + odd) * rows, rows), rows)
            act, slope = gelu_pair(dot(x_ref[r, :], wi_ref[...]))
            act = act.astype(BF16)
            dh = (dot_nt(g_ref[r, :], wo_ref[...]) * slope).astype(BF16)
            act_ref[r, :] = act
            dh_ref[r, :] = dh
            out_ref[0, t] = dot(act, wo_ref[...]).astype(BF16)
            out_ref[1, t] = dot_nt(dh, wi_ref[...]).astype(BF16)

    small = inner * ff // width
    for ref, d in ((gother_ref, 1 - here), (gown_ref, here)):
        c = pl.ds(pl.multiple_of(d * (ff // 2), ff // 2), ff // 2)
        grad = dot_tn(act_ref[:, c], g_ref[...]).astype(BF16)
        ref[:, small:, :] = grad.reshape(planes, outer, width)
        c = pl.ds(pl.multiple_of(d * (width // 2), width // 2), width // 2)
        grad = dot_tn(x_ref[:, c], dh_ref[...]).astype(BF16).reshape(planes, inner, ff)
        for g in range(width // ff):
            ref[:, :small, g * ff : (g + 1) * ff] = grad[:, g * small : (g + 1) * small]


def dense_block(where, xs, gs, own, other, ff):
    n, (rows, width) = len(xs), xs[0].shape
    tokens = n * rows
    both = shape16(2, n // 2, rows, width)
    return vmem_call(
        functools.partial(dense_kernel, n, ff),
        [both, both, shape16(*own.shape), shape16(*own.shape)],
        [
            pltpu.VMEM((width, ff), BF16), pltpu.VMEM((ff, width), BF16),
            pltpu.VMEM((tokens, width), BF16), pltpu.VMEM((tokens, width), BF16),
            pltpu.VMEM((tokens, ff), BF16), pltpu.VMEM((tokens, ff), BF16),
        ],
        12 * tokens * width * ff, tokens * ff,
        where, *xs, *gs, own, other,
    )


def expert_kernel(rows, ne, where_ref, *refs):
    x_ref, c_ref, wi_own, wi_other, wo_own, wo_other, router_ref, mine_ref = refs[:8]
    y_ref, dx_ref, gi_own, gi_other, go_own, go_other, gr_ref = refs[8:15]
    wi_ref, wo_ref, g_ref, act_ref, dh_ref = refs[15:]
    width = x_ref.shape[1]
    ff = wo_ref.shape[0]
    half = ff // 2
    wi_ref[:, :half] = wi_own[...]
    wi_ref[:, half:ff] = wi_other[...]
    wi_ref[:, ff:] = router_ref[...]
    wo_ref[:half, :] = wo_own[...]
    wo_ref[half:, :] = wo_other[...]
    mine = mine_ref[...]
    lanes = lax.broadcasted_iota(jnp.int32, (rows, mine.shape[1]), 1)

    @pl.loop(0, x_ref.shape[0] // rows)
    def _(t):
        r = pl.ds(pl.multiple_of(t * rows, rows), rows)
        hidden = dot(x_ref[r, :], wi_ref[...])
        logits = jnp.where(lanes < ne, hidden[:, ff:], NEG)
        raised = jnp.exp(logits - jnp.max(logits, axis=1, keepdims=True))
        probs = raised / jnp.sum(raised, axis=1, keepdims=True)
        gate = jnp.sum(probs * mine, axis=1, keepdims=True)
        act, slope = gelu_pair(hidden[:, :ff])
        act = act.astype(BF16)
        cot = c_ref[r, :].astype(F32)
        grad = (gate * cot).astype(BF16)
        dh = (dot_nt(grad, wo_ref[...]) * slope).astype(BF16)
        result = dot(act, wo_ref[...])
        d_gate = jnp.sum(cot * result, axis=1, keepdims=True)
        act_ref[r, :] = act
        g_ref[r, :] = grad
        dh_ref[r, :ff] = dh
        dh_ref[r, ff:] = (d_gate * probs * (mine - gate)).astype(BF16)
        y_ref[r, :] = result.astype(BF16)
        dx_ref[r, :] = dot_nt(dh_ref[r, :], wi_ref[...]).astype(BF16)

    go_other[...] = dot_tn(act_ref[:, half:], g_ref[...]).astype(BF16)
    go_own[...] = dot_tn(act_ref[:, :half], g_ref[...]).astype(BF16)
    for j in range(2):
        c = pl.ds(j * (width // 2), width // 2)
        grad = dot_tn(x_ref[:, c], dh_ref[...])
        gi_own[c, :] = grad[:, :half].astype(BF16)
        gi_other[c, :] = grad[:, half:ff].astype(BF16)
        gr_ref[c, :] = grad[:, ff:]


def expert_block(where, x, cot, wi_own, wi_other, wo_own, wo_other, router, mine, rows, ne):
    tokens, width = x.shape
    ff, pad = 2 * wo_own.shape[0], router.shape[1]
    return vmem_call(
        functools.partial(expert_kernel, rows, ne),
        [shape16(tokens, width)] * 2
        + [shape16(*w.shape) for w in (wi_own, wi_other, wo_own, wo_other)]
        + [jax.ShapeDtypeStruct((width, pad), F32)],
        [
            pltpu.VMEM((width, ff + pad), BF16), pltpu.VMEM((ff, width), BF16),
            pltpu.VMEM((tokens, width), BF16),
            pltpu.VMEM((tokens, ff), BF16), pltpu.VMEM((tokens, ff + pad), BF16),
        ],
        12 * tokens * width * ff, tokens * ff,
        where, x, cot, wi_own, wi_other, wo_own, wo_other, router, mine,
    )


def solution(mesh):
    nd, nc, ne = (mesh.shape[a] for a in AXES)
    ndev = nd * nc * ne
    bits_of = lambda n: [1 << b for b in range(n.bit_length() - 1)]
    low_bits, all_bits = bits_of(nc), bits_of(ne)
    high_bits = [b for b in all_bits if b not in low_bits]
    nh = ne // nc


    def send(x, target):
        pairs = []
        for d in range(nd):
            for c in range(nc):
                for e in range(ne):
                    to = target(d, c, e)
                    if to is not None:
                        pairs.append(((d * nc + c) * ne + e, (to[0] * nc + to[1]) * ne + to[2]))
        return lax.ppermute(x, AXES, pairs)

    def swap_exp(x, bit):
        return send(x, lambda d, c, e: (d, c, e ^ bit))

    def swap_dp(x):
        return send(x, lambda d, c, e: (d ^ 1, c, e))

    def reverse(i):
        return int(format(i, "b").zfill(len(low_bits))[::-1], 2)

    def to_seq(x):
        return send(x, lambda d, c, e: (d, reverse(e % nc), e - e % nc + c))

    def from_seq(x):
        return send(x, lambda d, c, e: (d, e % nc, e - e % nc + reverse(c)))

    def to_seq_by(x, *others):
        x = after(swap_exp(x, nc // 2), *others)
        return send(x, lambda d, c, e: (d, reverse((e ^ (nc // 2)) % nc), e - e % nc + c))

    def from_seq_by(x):
        x = send(x, lambda d, c, e: (d, e % nc, (e - e % nc + reverse(c)) ^ (nc // 2)))
        return swap_exp(x, nc // 2)

    def after(x, *others):
        return lax.optimization_barrier((x,) + others)[0]

    def my_bit(bit):
        return (lax.axis_index("exp") // bit) % 2

    def ordered(mine, other, index, axis):
        return jnp.where(
            index == 0, jnp.stack([mine, other], axis), jnp.stack([other, mine], axis)
        )

    def gather_exp(x, bits):
        out = x[None]
        for bit in reversed(bits):
            out = ordered(out, swap_exp(out, bit), my_bit(bit), 1)
            out = out.reshape((-1,) + x.shape)
        return out

    def pieces_exp(x, bits):
        out = [x]
        for bit in reversed(bits):
            out = [v for own in out for v in (own, swap_exp(own, bit))]
        return out

    def scatter_exp_rel(keep, away, bits):
        parts = keep.astype(F32) + swap_exp(away, bits[0]).astype(F32)
        for bit in bits[1:]:
            pairs = parts.reshape((parts.shape[0], -1, 2) + parts.shape[2:])
            away = swap_exp(pairs[:, :, 1].astype(BF16), bit)
            parts = pairs[:, :, 0].astype(F32) + away.astype(F32)
        return parts[:, 0], away

    def split_bit(x, position, count):
        shape = x.shape
        return x.reshape((shape[0] >> (position + 1), 2, 1 << position) + shape[1:])

    def scatter_exp(parts, bits):
        for bit in bits:
            pairs = parts.reshape((-1, 2) + parts.shape[1:])
            mine = my_bit(bit)
            keep = lax.dynamic_index_in_dim(pairs, mine, 1, keepdims=False)
            away = lax.dynamic_index_in_dim(pairs, 1 - mine, 1, keepdims=False)
            parts = keep.astype(F32) + swap_exp(away.astype(BF16), bit).astype(F32)
        return parts[0]

    def trade_exp(parts, bits):
        for position, bit in enumerate(bits):
            pairs = split_bit(parts, position, len(bits))
            mine = my_bit(bit)
            keep = lax.dynamic_index_in_dim(pairs, mine, 1, keepdims=False)
            away = lax.dynamic_index_in_dim(pairs, 1 - mine, 1, keepdims=False)
            parts = ordered(keep, swap_exp(away, bit), mine, 1).reshape(parts.shape)
        return parts

    def gather_ctx(x):
        return lax.all_to_all(
            jnp.broadcast_to(x[None], (nc,) + x.shape), "ctx", 0, 0, tiled=True
        )

    def scatter_ctx(parts):
        parts = lax.all_to_all(parts.astype(BF16), "ctx", 0, 0, tiled=True)
        return jnp.sum(parts.astype(F32), axis=0)

    def scatter_plane(own, other, *others):
        both = (own.astype(F32) + other.astype(F32)).astype(BF16)
        return scatter_ctx(after(both, *others))

    def out_place(d, c, e):
        low, rest = divmod((d * nc + c) * ne + e, ndev // nc)
        return rest // (nc * nh), rest // nh % nc, rest % nh * nc + low

    def out_to(x):
        return send(x, out_place)

    def out_from(x):
        back = {
            out_place(d, c, e): (d, c, e) for d in range(nd) for c in range(nc) for e in range(ne)
        }
        return send(x, lambda d, c, e: back[(d, c, e)])

    def per_device(
        tokens, qkv_weight, out_weight, norm1_gain, norm1_shift, norm2_gain, norm2_shift,
        inner_weight, outer_weight, router_weight, expert_inner, expert_outer,
        segments, routes, priority, cotangent,
    ):
        rows, width = tokens.shape[1:]
        length = segments.shape[1]
        rw = qkv_weight.shape[0]
        ff_rows = outer_weight.shape[0]
        nplane = nd * nc
        e_here = lax.axis_index("exp")
        group = width // nc

        x_low = to_seq(tokens[0])
        capacity = (9 * rows + 8 * ne - 1) // (8 * ne)
        slots = ne * capacity
        route, order = routes[0, :, 0], priority[0, 0]
        same = route[:, None] == route[None, :]
        earlier = order[None, :] < order[:, None]
        slot = jnp.sum(jnp.logical_and(same, earlier).astype(jnp.int32), axis=1)
        place = jnp.where(slot < capacity, route * capacity + slot, -1)

        table_there = (jnp.arange(slots, dtype=jnp.int32)[:, None] == place[None, :]).astype(BF16)
        ints = jnp.concatenate([segments[0], route, place])
        ints = to_seq(ints.reshape(-1, 128)).reshape(-1)
        segs, route, place = ints[:length], ints[length : length + rows], ints[length + rows :]

        def table_of(place):
            return (jnp.arange(slots, dtype=jnp.int32)[:, None] == place[None, :]).astype(BF16)

        table = table_of(place)

        def rows_out(table, v):
            return dot(table, v).astype(BF16).reshape(ne, capacity, width)

        def to_experts(table, v):
            out = jnp.broadcast_to(rows_out(table, v)[None], (nc, ne, capacity, width))
            out = out.reshape(nc * ne, capacity, width)
            return lax.all_to_all(out, ("ctx", "exp"), 0, 0, tiled=True)

        def from_experts(v):
            back = v.reshape(nc * ne, capacity, width)
            back = lax.all_to_all(back, ("ctx", "exp"), 0, 0, tiled=True)
            return dot_tn(jnp.tile(table, (nc, 1)), back.reshape(nc * slots, width)), back

        small = jnp.concatenate(
            [norm1_gain, norm1_shift, norm2_gain, norm2_shift, router_weight.reshape(-1)]
        )
        small = lax.all_to_all(
            jnp.broadcast_to(small[None], (ndev,) + small.shape), AXES, 0, 0, tiled=True
        )
        ff = nplane * ff_rows
        where = jnp.stack([e_here % nc, lax.axis_index("dp")]).astype(jnp.int32)
        qkv_part = jnp.moveaxis(qkv_weight.reshape(rw, 3, nc, group), 2, 0)
        qkv_part = jnp.tile(qkv_part.reshape(nc, rw, 3 * group), (nh, 1, 1))
        inner_part = jnp.moveaxis(inner_weight.reshape(rw, nplane, ne, ff_rows), 2, 0)
        columns = jnp.concatenate([qkv_part, inner_part.reshape(ne, rw, ff)], axis=2)
        columns = lax.all_to_all(columns, "exp", 0, 0, tiled=True).reshape(ne * rw, -1)
        out_part = gather_exp(out_to(out_weight), high_bits).reshape(nh * rw, nc, group)
        out_part = jnp.swapaxes(out_part, 0, 1).reshape(ne * rw, group)
        bundle = jnp.concatenate([columns[:, : 3 * group], out_part], axis=1)
        cot_low = to_seq_by(cotangent[0])
        ei_other = swap_dp(expert_inner[0])
        att_own = gather_ctx(after(bundle, x_low, small, cot_low, ei_other))
        ei_own, eo_own = expert_inner[0], expert_outer[0]
        gain1, shift1, gain2, shift2 = (
            small[:, i * rw : (i + 1) * rw].reshape(width).astype(F32) for i in range(4)
        )
        router = small[:, 4 * rw :].reshape(width, ne)

        x = x_low.astype(F32)
        unit1, scale1 = norm_parts(x)
        normed = pieces_exp((unit1 * gain1 + shift1).astype(BF16), low_bits)
        att_other = swap_dp(att_own)
        eo_other = swap_dp(after(eo_own, att_other))
        qkv, attended, keep, away = attention_fwd(where, normed, att_own, att_other, segs)
        e_cot = trade_exp(rows_out(table_there, cotangent[0]), all_bits)
        part = columns[:, 3 * group :].reshape(width // ff, -1, ff)
        part = jnp.concatenate([jnp.swapaxes(part, 0, 1).reshape(-1, width), outer_weight])
        ff_own = gather_ctx(after(part, att_own, e_cot))
        ff_other = swap_dp(ff_own)
        keep = after(keep, ff_own)
        residual = x + scatter_exp_rel(keep[None], away[None], low_bits)[0][0]
        e_cot = gather_ctx(after(e_cot, ff_own, keep)).reshape(nc, nh, nc, capacity, width)
        cot_all = pieces_exp(cot_low, all_bits)
        residual = after(residual, eo_other, *cot_all)
        unit2, scale2 = norm_parts(residual)
        normed2 = (unit2 * gain2 + shift2).astype(BF16)

        cot = cot_low.astype(F32)
        e_cot = jnp.stack([e_cot[:, :, reverse(c)] for c in range(nc)])
        e_cot = jnp.moveaxis(e_cot, 1, 2).reshape(nc * slots, width)
        e_x = to_experts(table, normed2).reshape(nc * slots, width)
        n2_all = pieces_exp(normed2, all_bits)
        keep, away, ff_keep, ff_away = dense_block(where, n2_all, cot_all, ff_own, ff_other, ff)
        ff_away = swap_dp(ff_away)
        both, last = scatter_exp_rel(keep, away, all_bits)
        dense, d_n2_dense = both[0], both[1]

        e_x = after(e_x, keep)
        mine = (jnp.arange(128, dtype=jnp.int32) == e_here).astype(F32)[None, :]
        lanes = jnp.pad(router, ((0, 0), (0, 128 - ne)))
        e_result, d_e_x, gi_own, gi_other, go_own, go_other, d_router = expert_block(
            where, e_x, e_cot, ei_own, ei_other, eo_own, eo_other, lanes, mine,
            nc * slots // 4, ne,
        )
        d_router = d_router[:, :ne]
        gi_other, go_other = swap_dp(gi_other), swap_dp(go_other)

        d_e_x = after(d_e_x, ff_away, last)
        d_e_x, back = from_experts(d_e_x)
        d_n2 = d_n2_dense + d_e_x
        g_e_in = gi_own.astype(F32) + gi_other.astype(F32)
        g_e_out = go_own.astype(F32) + go_other.astype(F32)
        d_gain2 = jnp.sum(d_n2 * unit2, axis=0)
        d_shift2 = jnp.sum(d_n2, axis=0)
        d_residual = cot + norm_back(d_n2, unit2, scale2, gain2)
        d_branch = pieces_exp(d_residual.astype(BF16), low_bits)
        part = scatter_plane(ff_keep, ff_away, back, gi_other, go_other)
        e_result = scatter_ctx(after(e_result, part).reshape(nc, slots, width)).astype(BF16)
        picked = trade_exp(e_result.reshape(ne, capacity, width), all_bits)
        picked = dot_tn(table, picked.reshape(slots, width))
        probs = softmax_rows(dot(normed2, router))
        chosen = (route[:, None] == jnp.arange(ne, dtype=jnp.int32)[None, :]).astype(F32)
        gate = jnp.sum(probs * chosen, axis=1, keepdims=True)
        output = from_seq((residual + dense + gate * picked).astype(BF16))

        d_branch[0] = after(d_branch[0], part)
        keep, away, att_keep, att_away = attention_bwd(
            where, d_branch, normed, att_own, att_other, segs, qkv, attended
        )
        d_normed = scatter_exp_rel(keep[None], away[None], low_bits)[0][0]
        d_gain1 = jnp.sum(d_normed * unit1, axis=0)
        d_shift1 = jnp.sum(d_normed, axis=0)
        d_tokens = d_residual + norm_back(d_normed, unit1, scale1, gain1)
        d_tokens = from_seq(d_tokens.astype(BF16)).astype(F32)

        g_outer = part[width * ff // (nplane * width) :]
        g_inner = part[: width * ff // (nplane * width)].reshape(-1, width // ff, ff)
        g_inner = jnp.swapaxes(g_inner, 0, 1).reshape(ne, rw, ff)
        bundle = scatter_plane(att_keep, swap_dp(att_away), e_result)
        g_out = bundle[:, 3 * group :].reshape(nc, nh * rw, group)
        g_out = jnp.swapaxes(g_out, 0, 1).reshape(nh, rw, width)
        g_out = out_from(scatter_exp(g_out, high_bits).astype(BF16)).astype(F32)
        g_qkv = bundle[:, : 3 * group].reshape(ne, rw, 3 * group)
        columns = jnp.concatenate([g_qkv, g_inner], axis=2).astype(BF16)
        columns = lax.all_to_all(columns, "exp", 0, 0, tiled=True)
        g_inner = columns[:, :, 3 * group :].reshape(ne, rw, nplane, ff_rows)
        g_inner = jnp.transpose(g_inner, (1, 2, 0, 3)).reshape(rw, -1).astype(F32)
        g_qkv = columns[:, :, : 3 * group].reshape(nh, nc, rw, 3, group)
        g_qkv = jnp.sum(g_qkv.astype(F32), axis=0)
        g_qkv = jnp.transpose(g_qkv, (1, 2, 0, 3)).reshape(rw, 3 * width)

        small = jnp.concatenate([jnp.stack([d_gain1, d_shift1, d_gain2, d_shift2], 1), d_router], 1)
        small = after(small.reshape(ndev, -1), bundle)
        small = lax.all_to_all(small, AXES, 0, 0, tiled=True)
        small = jnp.sum(small, axis=0).reshape(rw, 4 + ne)

        return (
            output[None], d_tokens[None], g_qkv, g_out,
            small[:, 0], small[:, 1], small[:, 2], small[:, 3],
            g_inner, g_outer, small[:, 4:], g_e_in[None].astype(F32), g_e_out[None].astype(F32),
        )

    rest = ("dp", "ctx", "exp")
    seq = P(("dp", "exp"), "ctx", None)
    in_specs = (
        seq, P(rest, None), P(rest, None), P(rest), P(rest), P(rest), P(rest),
        P(rest, None), P(rest, None), P(rest, None),
        P("exp", None, ("dp", "ctx")), P("exp", ("dp", "ctx"), None),
        P(("dp", "exp"), None), seq, seq, seq,
    )
    out_specs = (
        seq, seq, P(rest, None), P(rest, None), P(rest), P(rest), P(rest), P(rest),
        P(rest, None), P(rest, None), P(rest, None),
        P("exp", None, ("dp", "ctx")), P("exp", ("dp", "ctx"), None),
    )
    return jax.shard_map(
        per_device, mesh=mesh, in_specs=in_specs, out_specs=out_specs, check_vma=False
    )
```

time: 601 us -> 581 us (0.967)
  waiting for transfers between devices: 188 us -> 261 us
  other arithmetic: 89.6 us -> 45 us
  matrix products: 47.7 us -> 3.43 us
  local copies, waits for them, and re-layouts: 87.5 us -> 49.7 us
  Pallas kernels: 49.3 us -> 81.2 us
    all_to_all x4 -> x3, waiting for transfers between devices: 31 us -> 71.2 us  [gather_ctx(): lax.all_to_all(jnp.broadcast_to(x[None], (nc,) + x.shape), 'ctx', 0, 0, t...]
    pallas_call x3 -> x4, Pallas kernels: 49.3 us -> 81.2 us  [vmem_call(): pl.pallas_call(kernel, in_specs=[pl.BlockSpec(memory_space=pltpu.SMEM)] +...]
    all_to_all x1 -> x3, starting transfers between devices: 5.13 us -> 36.5 us  [the longest x1 25.7 us: per_device(): small = lax.all_to_all(small, AXES, 0, 0, tiled=True)]
    all_to_all x1, starting transfers between devices: 34 us -> 3.87 us  [per_device(): columns = lax.all_to_all(columns, 'exp', 0, 0, tiled=True)]
    ppermute x39 -> x38, waiting for transfers between devices: 114 us -> 134 us  [send(): return lax.ppermute(x, AXES, pairs)]
    all_to_all x1, waiting for transfers between devices: 19.9 us -> 0.02 us  [per_device(): lax.all_to_all(columns, 'exp', 0, 0, tiled=True).reshape(ne * rw, -1)]
    all_to_all x1 -> x3, waiting for transfers between devices: 0.73 us -> 18.6 us  [the longest x1 17.5 us: per_device(): small = lax.all_to_all(small, AXES, 0, 0, tiled=True)]
    dot_general x4 -> x0, local copies, waits for them, and re-layouts: 17.2 us -> none  [the longest x3 11.9 us: dot_tn(): lax.dot_general(a, b, (((0,), (0,)), ((), ())), preferred_element_type=F32)]
  transfers between devices with their start and end apart: 51 -> 50, of which waited for: 20 -> 25; matrix products, arithmetic and copies ran while one was open for 36% -> 15% of each run, Pallas kernels for 4% -> 14%
where the time goes in v3:
time: 581 us; the launch traced here: 571 us
  waiting for transfers between devices  261 us (45%)
  starting transfers between devices  128 us (22%)
  Pallas kernels  81.2 us (14%)
  local copies, waits for them, and re-layouts  49.7 us (9%)
  other arithmetic  45 us (8%)
    ppermute x38, waiting for transfers between devices, send(): return lax.ppermute(x, AXES, pairs)  134 us
    pallas_call x4, Pallas kernels, vmem_call(): pl.pallas_call(kernel, in_specs=[pl.BlockSpec(memory_space=pltpu.SMEM)] +...  81.2 us
    all_to_all x3, waiting for transfers between devices, gather_ctx(): lax.all_to_all(jnp.broadcast_to(x[None], (nc,) + x.shape), 'ctx', 0, 0, t...  71.2 us
    ppermute x38, starting transfers between devices, send(): return lax.ppermute(x, AXES, pairs)  42.1 us
    all_to_all x3, waiting for transfers between devices, scatter_ctx(): parts = lax.all_to_all(parts.astype(BF16), 'ctx', 0, 0, tiled=True)  29.9 us
    all_to_all x1, starting transfers between devices, per_device(): small = lax.all_to_all(small, AXES, 0, 0, tiled=True)  25.7 us
    all_to_all x3, starting transfers between devices, gather_ctx(): lax.all_to_all(jnp.broadcast_to(x[None], (nc,) + x.shape), 'ctx', 0, 0, t...  18.7 us
    all_to_all x3, starting transfers between devices, scatter_ctx(): parts = lax.all_to_all(parts.astype(BF16), 'ctx', 0, 0, tiled=True)  17.8 us
  transfers between devices with their start and end apart: 50, of which 25 were waited for; matrix products, arithmetic and copies ran while one was open for 15% of the time, Pallas kernels for 14%

profile of v3, /device:TPU:4, one launch (start us, length us, event | category | flops | bytes accessed | tf_op | source)
XLA Modules:
  0.0 570.7 jit_solution(13441636961056243319)
XLA Ops:
  3.6 2.8 concatenate.62
  8.3 5.2 all-to-all-start
  13.5 3.4 collective-permute-start
  20.5 6.7 %all-to-all-done = bf16[32,2,128]{2,1,0:T(2,128)(2,1)S(1)} async-done(((bf16[32,2,128]{2,1,0:T(2,128)(2,1)}), bf16[32,2,128]{2,1,0:T(2,128)(2,1)S(1)}, u32[]{:S(2)}, u32[]{:S(2)}) %all-to-all-start) | async-done | bytes 16416 | tf_op jit(solution)/shard_map/all_to_all | solution.py:560
  27.2 4.1 all-to-all-start.1
  31.3 4.0 collective-permute-start.4
  35.5 2.9 collective-permute-done.4
  38.5 4.0 collective-permute-done.6.refs_4_
  43.7 9.2 %all-to-all-start.2 = ((bf16[4,128,1024]{2,1,0:T(8,128)(2,1)}), bf16[4,128,1024]{2,1,0:T(8,128)(2,1)S(1)}, u32[]{:S(2)}, u32[]{:S(2)}) async-start(bf16[4,128,1024]{2,1,0:T(8,128)(2,1)} %broadcast_in_dim.36), calls=%async_computation.2 | async-start | bytes 2097152 | tf_op jit(solution)/shard_map/all_to_all | solution.py:487
  55.2 23.7 %all-to-all-done.2.refs_4_.refs_8_ = bf16[4,128,1024]{2,1,0:T(8,128)(2,1)S(1)} async-done(((bf16[4,128,1024]{2,1,0:T(8,128)(2,1)}), bf16[4,128,1024]{2,1,0:T(8,128)(2,1)S(1)}, u32[]{:S(2)}, u32[]{:S(2)}) %all-to-all-start.2) | async-done | bytes 1048608 | tf_op jit(solution)/shard_map/all_to_all | solution.py:487
  87.7 4.9 collective-permute-done.9
  97.4 4.4 all-to-all-start.3
  103.1 13.2 %shard_map.255 = (bf16[1024,768]{1,0:T(8,128)(2,1)}, bf16[1024,256]{1,0:T(8,128)(2,1)}, bf16[2,256,1024]{2,1,0:T(8,128)(2,1)}, bf16[2,256,1024]{2,1,0:T(8,128)(2,1)}) custom-call(s32[2]{0:T(128)} %pad_add_fusion.where_ref, bf16[256,1024]{1,0:T(8,128)(2,1)} %copy-done.25, bf16[256,1024]{1,0:T(8,128)(2,1)} %collective-permute-done.1.refs_1_.refs_5_, ...), custom_call_target="tpu_custom_call" | custom-call | flops 42949672960 | bytes 8396800 | tf_op jit(solution)/shard_map/pallas_call | solution.py:208
  116.3 34.4 %all-to-all-done.3.refs_8_ = bf16[4,256,1024]{2,1,0:T(8,128)(2,1)} async-done(((bf16[4,256,1024]{2,1,0:T(8,128)(2,1)}), bf16[4,256,1024]{2,1,0:T(8,128)(2,1)}, u32[]{:S(2)}, u32[]{:S(2)}) %all-to-all-start.3) | async-done | bytes 2097184 | tf_op jit(solution)/shard_map/all_to_all | solution.py:487
  152.5 5.1 all-to-all-start.5
  161.9 10.7 %collective-permute-done.16.refs_6_ = bf16[256,1024]{1,0:T(8,128)(2,1)} collective-permute-done((bf16[256,1024]{1,0:T(8,128)(2,1)S(1)}, bf16[256,1024]{1,0:T(8,128)(2,1)}, u32[]{:S(2)}, u32[]{:S(2)}) %collective-permute-start.16) | collective-permute-done | bytes 524320 | tf_op jit(solution)/shard_map/ppermute | solution.py:407
  173.1 8.9 %collective-permute-done.13 = bf16[1,1,256,1024]{3,2,1,0:T(8,128)(2,1)S(1)} collective-permute-done((bf16[1,1,256,1024]{3,2,1,0:T(8,128)(2,1)S(1)}, bf16[1,1,256,1024]{3,2,1,0:T(8,128)(2,1)S(1)}, u32[]{:S(2)}, u32[]{:S(2)}) %collective-permute-start.13) | collective-permute-done | bytes 524320 | tf_op jit(solution)/shard_map/ppermute | solution.py:407
  186.9 9.8 %collective-permute-done.19.refs_2_ = bf16[256,1024]{1,0:T(8,128)(2,1)S(1)} collective-permute-done((bf16[256,1024]{1,0:T(8,128)(2,1)S(1)}, bf16[256,1024]{1,0:T(8,128)(2,1)S(1)}, u32[]{:S(2)}, u32[]{:S(2)}) %collective-permute-start.19) | collective-permute-done | bytes 524320 | tf_op jit(solution)/shard_map/ppermute | solution.py:407
  198.1 13.1 %all-to-all-done.5 = bf16[4,4,72,1024]{3,2,1,0:T(8,128)(2,1)} async-done(((bf16[4,4,72,1024]{3,2,1,0:T(8,128)(2,1)}), bf16[4,4,72,1024]{3,2,1,0:T(8,128)(2,1)}, u32[]{:S(2)}, u32[]{:S(2)}) %all-to-all-start.5) | async-done | bytes 2359328 | tf_op jit(solution)/shard_map/all_to_all | solution.py:487
  213.0 4.2 all-to-all-start.4
  217.2 10.2 %collective-permute-done.21.refs_9_ = bf16[4,256,1024]{2,1,0:T(8,128)(2,1)} collective-permute-done((bf16[4,256,1024]{2,1,0:T(8,128)(2,1)}, bf16[4,256,1024]{2,1,0:T(8,128)(2,1)}, u32[]{:S(2)}, u32[]{:S(2)}) %collective-permute-start.21) | collective-permute-done | bytes 2097184 | tf_op jit(solution)/shard_map/ppermute | solution.py:407
  227.4 19.3 %shard_map.256 = (bf16[2,2,256,1024]{3,2,1,0:T(8,128)(2,1)}, bf16[2,2,256,1024]{3,2,1,0:T(8,128)(2,1)}, bf16[4,256,1024]{2,1,0:T(8,128)(2,1)}, bf16[4,256,1024]{2,1,0:T(8,128)(2,1)}) custom-call(s32[2]{0:T(128)} %pad_add_fusion.where_ref, bf16[256,1024]{1,0:T(8,128)(2,1)} %copy-done.11, bf16[256,1024]{1,0:T(8,128)(2,1)} %collective-permute-done.18.refs_1_, ...), custom_call_target="tpu_custom_call" | custom-call | flops 128849018880 | bytes 16777216 | tf_op jit(solution)/shard_map/pallas_call | solution.py:208
  246.7 3.1 copy.123
  266.1 25.2 %shard_map.257 = (bf16[1152,1024]{1,0:T(8,128)(2,1)}, bf16[1152,1024]{1,0:T(8,128)(2,1)}, bf16[1024,512]{1,0:T(8,128)(2,1)}, bf16[1024,512]{1,0:T(8,128)(2,1)}, ...) custom-call(s32[2]{0:T(128)} %pad_add_fusion.where_ref, bf16[1152,1024]{1,0:T(8,128)(2,1)} %bitcast.190, ...), custom_call_target="tpu_custom_call" | custom-call | flops 144955146240 | bytes 18612736 | tf_op jit(solution)/shard_map/pallas_call | solution.py:208
  291.3 8.8 %collective-permute-done.24 = bf16[4,256,1024]{2,1,0:T(8,128)(2,1)} collective-permute-done((bf16[4,256,1024]{2,1,0:T(8,128)(2,1)}, bf16[4,256,1024]{2,1,0:T(8,128)(2,1)}, u32[]{:S(2)}, u32[]{:S(2)}) %collective-permute-start.24) | collective-permute-done | bytes 2097184 | tf_op jit(solution)/shard_map/ppermute | solution.py:407
  300.1 6.6 %all-to-all-start.6 = ((bf16[16,72,1024]{2,1,0:T(8,128)(2,1)}), bf16[16,72,1024]{2,1,0:T(8,128)(2,1)S(1)}, u32[]{:S(2)}, u32[]{:S(2)}) async-start(bf16[16,72,1024]{2,1,0:T(8,128)(2,1)} %bitcast.191), calls=%async_computation.6 | async-start | bytes 4718592 | tf_op jit(solution)/shard_map/all_to_all | solution.py:554
  308.7 4.5 add_convert_fusion
  313.2 19.7 %collective-permute-done.25 = bf16[1024,512]{1,0:T(8,128)(2,1)S(1)} collective-permute-done((bf16[1024,512]{1,0:T(8,128)(2,1)}, bf16[1024,512]{1,0:T(8,128)(2,1)S(1)}, u32[]{:S(2)}, u32[]{:S(2)}) %collective-permute-start.25) | collective-permute-done | bytes 1048608 | tf_op jit(solution)/shard_map/ppermute | solution.py:407
  333.9 20.8 %collective-permute-done.26 = bf16[512,1024]{1,0:T(8,128)(2,1)} collective-permute-done((bf16[512,1024]{1,0:T(8,128)(2,1)S(1)}, bf16[512,1024]{1,0:T(8,128)(2,1)}, u32[]{:S(2)}, u32[]{:S(2)}) %collective-permute-start.26) | collective-permute-done | bytes 1048608 | tf_op jit(solution)/shard_map/ppermute | solution.py:407
  354.7 8.5 %all-to-all-start.7 = ((bf16[4,256,1024]{2,1,0:T(8,128)(2,1)}), bf16[4,256,1024]{2,1,0:T(8,128)(2,1)}, u32[]{:S(2)}, u32[]{:S(2)}) async-start(bf16[4,256,1024]{2,1,0:T(8,128)(2,1)} %add_convert_fusion), calls=%async_computation.7 | async-start | bytes 4194304 | tf_op jit(solution)/shard_map/all_to_all | solution.py:492
  369.4 12.9 %collective-permute-done.31.refs_2_ = bf16[256,1024]{1,0:T(8,128)(2,1)} collective-permute-done((bf16[256,1024]{1,0:T(8,128)(2,1)S(1)}, bf16[256,1024]{1,0:T(8,128)(2,1)}, u32[]{:S(2)}, u32[]{:S(2)}) %collective-permute-start.31) | collective-permute-done | bytes 524320 | tf_op jit(solution)/shard_map/ppermute | solution.py:407
  382.4 29.5 %all-to-all-done.7 = bf16[4,256,1024]{2,1,0:T(8,128)(2,1)} async-done(((bf16[4,256,1024]{2,1,0:T(8,128)(2,1)}), bf16[4,256,1024]{2,1,0:T(8,128)(2,1)}, u32[]{:S(2)}, u32[]{:S(2)}) %all-to-all-start.7) | async-done | bytes 2097184 | tf_op jit(solution)/shard_map/all_to_all | solution.py:492
  414.0 4.7 all-to-all-start.8
  418.8 23.5 %shard_map.258 = (bf16[2,256,1024]{2,1,0:T(8,128)(2,1)}, bf16[2,256,1024]{2,1,0:T(8,128)(2,1)}, bf16[4,128,1024]{2,1,0:T(8,128)(2,1)}, bf16[4,128,1024]{2,1,0:T(8,128)(2,1)}) custom-call(s32[2]{0:T(128)} %pad_add_fusion.where_ref, bf16[256,1024]{1,0:T(8,128)(2,1)} %copy-done.31, bf16[256,1024]{1,0:T(8,128)(2,1)} %collective-permute-done.30.refs_1_, ...), custom_call_target="tpu_custom_call" | custom-call | flops 96636764160 | bytes 12591104 | tf_op jit(solution)/shard_map/pallas_call | solution.py:208
  443.0 3.3 add_bitcast_fusion.2
  448.8 2.9 add_bitcast_fusion.1
  455.4 13.2 %collective-permute-done.36 = bf16[4,128,1024]{2,1,0:T(8,128)(2,1)} collective-permute-done((bf16[4,128,1024]{2,1,0:T(8,128)(2,1)}, bf16[4,128,1024]{2,1,0:T(8,128)(2,1)}, u32[]{:S(2)}, u32[]{:S(2)}) %collective-permute-start.36) | collective-permute-done | bytes 1048608 | tf_op jit(solution)/shard_map/ppermute | solution.py:407
  472.2 3.1 reduce_sum.186
  475.3 4.7 all-to-all-start.9
  485.2 2.7 concatenate.68
  491.8 2.6 fusion.15
  494.4 5.1 collective-permute-start.35
  501.5 5.4 collective-permute-start.29
  507.8 25.7 %all-to-all-start.11 = ((f32[32,1,256]{2,1,0:T(1,128)}), f32[32,1,256]{2,1,0:T(1,128)S(1)}, u32[]{:S(2)}, u32[]{:S(2)}) async-start(f32[32,1,256]{2,1,0:T(1,128)} %copy.135), calls=%async_computation.11 | async-start | bytes 65536 | tf_op jit(solution)/shard_map/all_to_all | solution.py:667
  534.3 17.5 %all-to-all-done.11 = f32[32,1,256]{2,1,0:T(1,128)S(1)} async-done(((f32[32,1,256]{2,1,0:T(1,128)}), f32[32,1,256]{2,1,0:T(1,128)S(1)}, u32[]{:S(2)}, u32[]{:S(2)}) %all-to-all-start.11) | async-done | bytes 32800 | tf_op jit(solution)/shard_map/all_to_all | solution.py:667
  551.8 3.9 all-to-all-start.10
  557.8 3.0 collective-permute-start.37
  562.5 3.3 collective-permute-done.37
  (292 shorter events, 100.2 us)
Async XLA Ops:
  0.6 19.0 %collective-permute-start.5 = (bf16[256,1024]{1,0:T(8,128)(2,1)}, bf16[256,1024]{1,0:T(8,128)(2,1)S(1)}, u32[]{:S(2)}, u32[]{:S(2)}) collective-permute-start(bf16[256,1024]{1,0:T(8,128)(2,1)} %bitcast.209), channel_id=1, source_target_pairs={{0,2},{1,3},{2,0},{3,1},{4,6},{5,7},{6,4},{7,5},{8,10},{9,11},{10,... | collective-permute-start | bytes 1572872 | tf_op jit(solution)/shard_map/ppermute | solution.py:407
  0.7 41.8 %collective-permute-start.7 = (bf16[1024,512]{1,0:T(8,128)(2,1)}, bf16[1024,512]{1,0:T(8,128)(2,1)}, u32[]{:S(2)}, u32[]{:S(2)}) collective-permute-start(bf16[1024,512]{1,0:T(8,128)(2,1)} %bitcast.233), channel_id=1, source_target_pairs={{0,16},{1,17},{2,18},{3,19},{4,20},{5,21},{6,22},{7,23},{8,24},{9,... | collective-permute-start | bytes 3145736 | tf_op jit(solution)/shard_map/ppermute | solution.py:407
  8.3 18.9 %all-to-all-start = ((bf16[32,2,128]{2,1,0:T(2,128)(2,1)}), bf16[32,2,128]{2,1,0:T(2,128)(2,1)S(1)}, u32[]{:S(2)}, u32[]{:S(2)}) async-start(bf16[32,2,128]{2,1,0:T(2,128)(2,1)} %reshape.514), calls=%async_computation | async-start | bytes 32768 | tf_op jit(solution)/shard_map/all_to_all | solution.py:560
  13.5 25.0 %collective-permute-start = (bf16[256,1024]{1,0:T(8,128)(2,1)}, bf16[256,1024]{1,0:T(8,128)(2,1)S(1)}, u32[]{:S(2)}, u32[]{:S(2)}) collective-permute-start(bf16[256,1024]{1,0:T(8,128)(2,1)} %bitcast.239), channel_id=1, source_target_pairs={{0,0},{1,8},{2,4},{3,12},{4,1},{5,9},{6,5},{7,13},{8,2},{9,10},{10... | collective-permute-start | bytes 1572872 | tf_op jit(solution)/shard_map/ppermute | solution.py:407
  19.6 22.9 %collective-permute-start.6 = (bf16[256,1024]{1,0:T(8,128)(2,1)S(1)}, bf16[256,1024]{1,0:T(8,128)(2,1)S(1)}, u32[]{:S(2)}, u32[]{:S(2)}) collective-permute-start(bf16[256,1024]{1,0:T(8,128)(2,1)S(1)} %collective-permute-done.5), channel_id=1, source_target_pairs={{0,4},{1,12},{2,0},{3,8},{4,5},{5,13},{6,1},{7,9},{8,6},{9,14},{10... | collective-permute-start | bytes 1572872 | tf_op jit(solution)/shard_map/ppermute | solution.py:407
  27.2 11.3 %all-to-all-start.1 = ((bf16[4,32,1792]{2,1,0:T(8,128)(2,1)}), bf16[4,32,1792]{2,1,0:T(8,128)(2,1)S(1)}, u32[]{:S(2)}, u32[]{:S(2)}) async-start(bf16[4,32,1792]{2,1,0:T(8,128)(2,1)} %pad_maximum_fusion.2), calls=%async_computation.1 | async-start | bytes 917504 | tf_op jit(solution)/shard_map/all_to_all | solution.py:569
  31.3 7.2 %collective-permute-start.4 = (bf16[32,1024]{1,0:T(8,128)(2,1)S(1)}, bf16[32,1024]{1,0:T(8,128)(2,1)S(1)}, u32[]{:S(2)}, u32[]{:S(2)}) collective-permute-start(bf16[32,1024]{1,0:T(8,128)(2,1)S(1)} %copy-done.56), channel_id=1, source_target_pairs={{0,0},{1,4},{2,8},{3,12},{4,16},{5,20},{6,24},{7,28},{8,1},{9,5},{... | collective-permute-start | bytes 196616 | tf_op jit(solution)/shard_map/ppermute | solution.py:407
  43.7 35.2 %all-to-all-start.2 = ((bf16[4,128,1024]{2,1,0:T(8,128)(2,1)}), bf16[4,128,1024]{2,1,0:T(8,128)(2,1)S(1)}, u32[]{:S(2)}, u32[]{:S(2)}) async-start(bf16[4,128,1024]{2,1,0:T(8,128)(2,1)} %broadcast_in_dim.36), calls=%async_computation.2 | async-start | bytes 2097152 | tf_op jit(solution)/shard_map/all_to_all | solution.py:487
  54.2 28.2 %collective-permute-start.2 = (bf16[256,1024]{1,0:T(8,128)(2,1)S(1)}, bf16[256,1024]{1,0:T(8,128)(2,1)}, u32[]{:S(2)}, u32[]{:S(2)}) collective-permute-start(bf16[256,1024]{1,0:T(8,128)(2,1)S(1)} %fusion.10.refs_0_.refs_4_), channel_id=1, source_target_pairs={{0,2},{1,3},{2,0},{3,1},{4,6},{5,7},{6,4},{7,5},{8,10},{9,11},{10,... | collective-permute-start | bytes 1572872 | tf_op jit(solution)/shard_map/ppermute | solution.py:407
  78.9 24.3 %collective-permute-start.8 = (bf16[4,128,1024]{2,1,0:T(8,128)(2,1)S(1)}, bf16[4,128,1024]{2,1,0:T(8,128)(2,1)}, u32[]{:S(2)}, u32[]{:S(2)}) collective-permute-start(bf16[4,128,1024]{2,1,0:T(8,128)(2,1)S(1)} %all-to-all-done.2.refs_4_.refs_8_), channel_id=1, source_target_pairs={{0,16},{1,17},{2,18},{3,19},{4,20},{5,21},{6,22},{7,23},{8,24},{9,... | collective-permute-start | bytes 3145736 | tf_op jit(solution)/shard_map/ppermute | solution.py:407
  82.2 19.6 %collective-permute-start.1 = (bf16[256,1024]{1,0:T(8,128)(2,1)S(1)}, bf16[256,1024]{1,0:T(8,128)(2,1)}, u32[]{:S(2)}, u32[]{:S(2)}) collective-permute-start(bf16[256,1024]{1,0:T(8,128)(2,1)S(1)} %fusion.10.refs_0_.refs_4_), channel_id=1, source_target_pairs={{0,1},{1,0},{2,3},{3,2},{4,5},{5,4},{6,7},{7,6},{8,9},{9,8},{10,11... | collective-permute-start | bytes 1572872 | tf_op jit(solution)/shard_map/ppermute | solution.py:407
  82.4 19.4 %collective-permute-start.3 = (bf16[256,1024]{1,0:T(8,128)(2,1)}, bf16[256,1024]{1,0:T(8,128)(2,1)}, u32[]{:S(2)}, u32[]{:S(2)}) collective-permute-start(bf16[256,1024]{1,0:T(8,128)(2,1)} %collective-permute-done.2.refs_2_.refs_6_), channel_id=1, source_target_pairs={{0,1},{1,0},{2,3},{3,2},{4,5},{5,4},{6,7},{7,6},{8,9},{9,8},{10,11... | collective-permute-start | bytes 1572872 | tf_op jit(solution)/shard_map/ppermute | solution.py:407
  82.9 11.8 %collective-permute-start.11 = (bf16[1,2,72,1024]{3,2,1,0:T(8,128)(2,1)S(1)}, bf16[1,2,72,1024]{3,2,1,0:T(8,128)(2,1)}, u32[]{:S(2)}, u32[]{:S(2)}) collective-permute-start(bf16[1,2,72,1024]{3,2,1,0:T(8,128)(2,1)S(1)} %get-tuple-element.165), channel_id=1, source_target_pairs={{0,2},{1,3},{2,0},{3,1},{4,6},{5,7},{6,4},{7,5},{8,10},{9,11},{10,... | collective-permute-start | bytes 884744 | tf_op jit(solution)/shard_map/ppermute | solution.py:407
  85.2 7.4 %collective-permute-start.9 = (s32[12,128]{1,0:T(8,128)S(1)}, s32[12,128]{1,0:T(8,128)S(1)}, u32[]{:S(2)}, u32[]{:S(2)}) collective-permute-start(s32[12,128]{1,0:T(8,128)S(1)} %add_bitcast_fusion.3), channel_id=1, source_target_pairs={{0,0},{1,8},{2,4},{3,12},{4,1},{5,9},{6,5},{7,13},{8,2},{9,10},{10... | collective-permute-start | bytes 18440 | tf_op jit(solution)/shard_map/ppermute | solution.py:407
  97.4 53.3 %all-to-all-start.3 = ((bf16[4,256,1024]{2,1,0:T(8,128)(2,1)}), bf16[4,256,1024]{2,1,0:T(8,128)(2,1)}, u32[]{:S(2)}, u32[]{:S(2)}) async-start(bf16[4,256,1024]{2,1,0:T(8,128)(2,1)} %broadcast_in_dim.40), calls=%async_computation.3 | async-start | bytes 4194304 | tf_op jit(solution)/shard_map/all_to_all | solution.py:487
  116.3 41.8 %collective-permute-start.12 = (bf16[1,2,256,1024]{3,2,1,0:T(8,128)(2,1)}, bf16[1,2,256,1024]{3,2,1,0:T(8,128)(2,1)S(1)}, u32[]{:S(2)}, u32[]{:S(2)}) collective-permute-start(bf16[1,2,256,1024]{3,2,1,0:T(8,128)(2,1)} %bitcast.238), channel_id=1, source_target_pairs={{0,1},{1,0},{2,3},{3,2},{4,5},{5,4},{6,7},{7,6},{8,9},{9,8},{10,11... | collective-permute-start | bytes 3145736 | tf_op jit(solution)/shard_map/ppermute | solution.py:407
  152.5 58.7 %all-to-all-start.5 = ((bf16[4,4,72,1024]{3,2,1,0:T(8,128)(2,1)}), bf16[4,4,72,1024]{3,2,1,0:T(8,128)(2,1)}, u32[]{:S(2)}, u32[]{:S(2)}) async-start(bf16[4,4,72,1024]{3,2,1,0:T(8,128)(2,1)} %broadcast_in_dim.44), calls=%async_computation.5 | async-start | bytes 4718592 | tf_op jit(solution)/shard_map/all_to_all | solution.py:487
  157.6 15.0 %collective-permute-start.16 = (bf16[256,1024]{1,0:T(8,128)(2,1)S(1)}, bf16[256,1024]{1,0:T(8,128)(2,1)}, u32[]{:S(2)}, u32[]{:S(2)}) collective-permute-start(bf16[256,1024]{1,0:T(8,128)(2,1)S(1)} %copy-done.29), channel_id=1, source_target_pairs={{0,2},{1,3},{2,0},{3,1},{4,6},{5,7},{6,4},{7,5},{8,10},{9,11},{10,... | collective-permute-start | bytes 1572872 | tf_op jit(solution)/shard_map/ppermute | solution.py:407
  157.7 26.5 %collective-permute-start.14 = (bf16[512,1024]{1,0:T(8,128)(2,1)}, bf16[512,1024]{1,0:T(8,128)(2,1)}, u32[]{:S(2)}, u32[]{:S(2)}) collective-permute-start(bf16[512,1024]{1,0:T(8,128)(2,1)} %bitcast.235), channel_id=1, source_target_pairs={{0,16},{1,17},{2,18},{3,19},{4,20},{5,21},{6,22},{7,23},{8,24},{9,... | collective-permute-start | bytes 3145736 | tf_op jit(solution)/shard_map/ppermute | solution.py:407
  159.9 22.1 %collective-permute-start.13 = (bf16[1,1,256,1024]{3,2,1,0:T(8,128)(2,1)S(1)}, bf16[1,1,256,1024]{3,2,1,0:T(8,128)(2,1)S(1)}, u32[]{:S(2)}, u32[]{:S(2)}) collective-permute-start(bf16[1,1,256,1024]{3,2,1,0:T(8,128)(2,1)S(1)} %fusion.27), channel_id=1, source_target_pairs={{0,2},{1,3},{2,0},{3,1},{4,6},{5,7},{6,4},{7,5},{8,10},{9,11},{10,... | collective-permute-start | bytes 1572872 | tf_op jit(solution)/shard_map/ppermute | solution.py:407
  161.9 21.6 %collective-permute-start.15 = (bf16[256,1024]{1,0:T(8,128)(2,1)S(1)}, bf16[256,1024]{1,0:T(8,128)(2,1)S(1)}, u32[]{:S(2)}, u32[]{:S(2)}) collective-permute-start(bf16[256,1024]{1,0:T(8,128)(2,1)S(1)} %copy-done.29), channel_id=1, source_target_pairs={{0,1},{1,0},{2,3},{3,2},{4,5},{5,4},{6,7},{7,6},{8,9},{9,8},{10,11... | collective-permute-start | bytes 1572872 | tf_op jit(solution)/shard_map/ppermute | solution.py:407
  172.6 10.9 %collective-permute-start.17 = (bf16[256,1024]{1,0:T(8,128)(2,1)}, bf16[256,1024]{1,0:T(8,128)(2,1)}, u32[]{:S(2)}, u32[]{:S(2)}) collective-permute-start(bf16[256,1024]{1,0:T(8,128)(2,1)} %collective-permute-done.16.refs_6_), channel_id=1, source_target_pairs={{0,1},{1,0},{2,3},{3,2},{4,5},{5,4},{6,7},{7,6},{8,9},{9,8},{10,11... | collective-permute-start | bytes 1572872 | tf_op jit(solution)/shard_map/ppermute | solution.py:407
  172.8 54.6 %collective-permute-start.21 = (bf16[4,256,1024]{2,1,0:T(8,128)(2,1)}, bf16[4,256,1024]{2,1,0:T(8,128)(2,1)}, u32[]{:S(2)}, u32[]{:S(2)}) collective-permute-start(bf16[4,256,1024]{2,1,0:T(8,128)(2,1)} %all-to-all-done.3.refs_8_), channel_id=1, source_target_pairs={{0,16},{1,17},{2,18},{3,19},{4,20},{5,21},{6,22},{7,23},{8,24},{9,... | collective-permute-start | bytes 6291464 | tf_op jit(solution)/shard_map/ppermute | solution.py:407
  184.9 11.8 %collective-permute-start.19 = (bf16[256,1024]{1,0:T(8,128)(2,1)S(1)}, bf16[256,1024]{1,0:T(8,128)(2,1)S(1)}, u32[]{:S(2)}, u32[]{:S(2)}) collective-permute-start(bf16[256,1024]{1,0:T(8,128)(2,1)S(1)} %add_convert_fusion.2.refs_0_), channel_id=1, source_target_pairs={{0,2},{1,3},{2,0},{3,1},{4,6},{5,7},{6,4},{7,5},{8,10},{9,11},{10,... | collective-permute-start | bytes 1572872 | tf_op jit(solution)/shard_map/ppermute | solution.py:407
  186.9 30.3 %collective-permute-start.18 = (bf16[256,1024]{1,0:T(8,128)(2,1)S(1)}, bf16[256,1024]{1,0:T(8,128)(2,1)}, u32[]{:S(2)}, u32[]{:S(2)}) collective-permute-start(bf16[256,1024]{1,0:T(8,128)(2,1)S(1)} %add_convert_fusion.2.refs_0_), channel_id=1, source_target_pairs={{0,1},{1,0},{2,3},{3,2},{4,5},{5,4},{6,7},{7,6},{8,9},{9,8},{10,11... | collective-permute-start | bytes 1572872 | tf_op jit(solution)/shard_map/ppermute | solution.py:407
  196.6 20.5 %collective-permute-start.20 = (bf16[256,1024]{1,0:T(8,128)(2,1)S(1)}, bf16[256,1024]{1,0:T(8,128)(2,1)}, u32[]{:S(2)}, u32[]{:S(2)}) collective-permute-start(bf16[256,1024]{1,0:T(8,128)(2,1)S(1)} %collective-permute-done.19.refs_2_), channel_id=1, source_target_pairs={{0,1},{1,0},{2,3},{3,2},{4,5},{5,4},{6,7},{7,6},{8,9},{9,8},{10,11... | collective-permute-start | bytes 1572872 | tf_op jit(solution)/shard_map/ppermute | solution.py:407
  213.0 51.7 %all-to-all-start.4 = ((bf16[16,72,1024]{2,1,0:T(8,128)(2,1)}), bf16[16,72,1024]{2,1,0:T(8,128)(2,1)S(1)}, u32[]{:S(2)}, u32[]{:S(2)}) async-start(bf16[16,72,1024]{2,1,0:T(8,128)(2,1)} %bitcast.38), calls=%async_computation.4 | async-start | bytes 4718592 | tf_op jit(solution)/shard_map/all_to_all | solution.py:550
  249.8 5.9 %collective-permute-start.22 = (bf16[2,2,256,1024]{3,2,0,1:T(8,128)(2,1)}, bf16[2,2,256,1024]{3,2,0,1:T(8,128)(2,1)}, u32[]{:S(2)}, u32[]{:S(2)}) collective-permute-start(bf16[2,2,256,1024]{3,2,0,1:T(8,128)(2,1)} %copy.123), channel_id=1, source_target_pairs={{0,1},{1,0},{2,3},{3,2},{4,5},{5,4},{6,7},{7,6},{8,9},{9,8},{10,11... | collective-permute-start | bytes 6291464 | tf_op jit(solution)/shard_map/ppermute | solution.py:407
  251.7 48.4 %collective-permute-start.24 = (bf16[4,256,1024]{2,1,0:T(8,128)(2,1)}, bf16[4,256,1024]{2,1,0:T(8,128)(2,1)}, u32[]{:S(2)}, u32[]{:S(2)}) collective-permute-start(bf16[4,256,1024]{2,1,0:T(8,128)(2,1)} %get-tuple-element.58), channel_id=1, source_target_pairs={{0,16},{1,17},{2,18},{3,19},{4,20},{5,21},{6,22},{7,23},{8,24},{9,... | collective-permute-start | bytes 6291464 | tf_op jit(solution)/shard_map/ppermute | solution.py:407
  261.9 38.2 %collective-permute-start.23 = (bf16[2,1,256,1024]{3,2,1,0:T(8,128)(2,1)}, bf16[2,1,256,1024]{3,2,1,0:T(8,128)(2,1)}, u32[]{:S(2)}, u32[]{:S(2)}) collective-permute-start(bf16[2,1,256,1024]{3,2,1,0:T(8,128)(2,1)} %fusion.18), channel_id=1, source_target_pairs={{0,2},{1,3},{2,0},{3,1},{4,6},{5,7},{6,4},{7,5},{8,10},{9,11},{10,... | collective-permute-start | bytes 3145736 | tf_op jit(solution)/shard_map/ppermute | solution.py:407
  300.1 54.6 %all-to-all-start.6 = ((bf16[16,72,1024]{2,1,0:T(8,128)(2,1)}), bf16[16,72,1024]{2,1,0:T(8,128)(2,1)S(1)}, u32[]{:S(2)}, u32[]{:S(2)}) async-start(bf16[16,72,1024]{2,1,0:T(8,128)(2,1)} %bitcast.191), calls=%async_computation.6 | async-start | bytes 4718592 | tf_op jit(solution)/shard_map/all_to_all | solution.py:554
  306.6 26.2 %collective-permute-start.25 = (bf16[1024,512]{1,0:T(8,128)(2,1)}, bf16[1024,512]{1,0:T(8,128)(2,1)S(1)}, u32[]{:S(2)}, u32[]{:S(2)}) collective-permute-start(bf16[1024,512]{1,0:T(8,128)(2,1)} %get-tuple-element.61), channel_id=1, source_target_pairs={{0,16},{1,17},{2,18},{3,19},{4,20},{5,21},{6,22},{7,23},{8,24},{9,... | collective-permute-start | bytes 3145736 | tf_op jit(solution)/shard_map/ppermute | solution.py:407
  307.0 47.7 %collective-permute-start.26 = (bf16[512,1024]{1,0:T(8,128)(2,1)S(1)}, bf16[512,1024]{1,0:T(8,128)(2,1)}, u32[]{:S(2)}, u32[]{:S(2)}) collective-permute-start(bf16[512,1024]{1,0:T(8,128)(2,1)S(1)} %copy-done.53), channel_id=1, source_target_pairs={{0,16},{1,17},{2,18},{3,19},{4,20},{5,21},{6,22},{7,23},{8,24},{9,... | collective-permute-start | bytes 3145736 | tf_op jit(solution)/shard_map/ppermute | solution.py:407
  354.7 57.2 %all-to-all-start.7 = ((bf16[4,256,1024]{2,1,0:T(8,128)(2,1)}), bf16[4,256,1024]{2,1,0:T(8,128)(2,1)}, u32[]{:S(2)}, u32[]{:S(2)}) async-start(bf16[4,256,1024]{2,1,0:T(8,128)(2,1)} %add_convert_fusion), calls=%async_computation.7 | async-start | bytes 4194304 | tf_op jit(solution)/shard_map/all_to_all | solution.py:492
  368.4 14.0 %collective-permute-start.31 = (bf16[256,1024]{1,0:T(8,128)(2,1)S(1)}, bf16[256,1024]{1,0:T(8,128)(2,1)}, u32[]{:S(2)}, u32[]{:S(2)}) collective-permute-start(bf16[256,1024]{1,0:T(8,128)(2,1)S(1)} %get-tuple-element.65.refs_0_), channel_id=1, source_target_pairs={{0,2},{1,3},{2,0},{3,1},{4,6},{5,7},{6,4},{7,5},{8,10},{9,11},{10,... | collective-permute-start | bytes 1572872 | tf_op jit(solution)/shard_map/ppermute | solution.py:407
  369.4 49.3 %collective-permute-start.30 = (bf16[256,1024]{1,0:T(8,128)(2,1)S(1)}, bf16[256,1024]{1,0:T(8,128)(2,1)}, u32[]{:S(2)}, u32[]{:S(2)}) collective-permute-start(bf16[256,1024]{1,0:T(8,128)(2,1)S(1)} %get-tuple-element.65.refs_0_), channel_id=1, source_target_pairs={{0,1},{1,0},{2,3},{3,2},{4,5},{5,4},{6,7},{7,6},{8,9},{9,8},{10,11... | collective-permute-start | bytes 1572872 | tf_op jit(solution)/shard_map/ppermute | solution.py:407
  382.4 36.4 %collective-permute-start.32 = (bf16[256,1024]{1,0:T(8,128)(2,1)}, bf16[256,1024]{1,0:T(8,128)(2,1)}, u32[]{:S(2)}, u32[]{:S(2)}) collective-permute-start(bf16[256,1024]{1,0:T(8,128)(2,1)} %collective-permute-done.31.refs_2_), channel_id=1, source_target_pairs={{0,1},{1,0},{2,3},{3,2},{4,5},{5,4},{6,7},{7,6},{8,9},{9,8},{10,11... | collective-permute-start | bytes 1572872 | tf_op jit(solution)/shard_map/ppermute | solution.py:407
  414.0 58.2 %all-to-all-start.8 = ((bf16[4,288,1024]{2,1,0:T(8,128)(2,1)}), bf16[4,288,1024]{2,1,0:T(8,128)(2,1)}, u32[]{:S(2)}, u32[]{:S(2)}) async-start(bf16[4,288,1024]{2,1,0:T(8,128)(2,1)} %bitcast.189), calls=%async_computation.8 | async-start | bytes 4718592 | tf_op jit(solution)/shard_map/all_to_all | solution.py:492
  442.7 25.9 %collective-permute-start.36 = (bf16[4,128,1024]{2,1,0:T(8,128)(2,1)}, bf16[4,128,1024]{2,1,0:T(8,128)(2,1)}, u32[]{:S(2)}, u32[]{:S(2)}) collective-permute-start(bf16[4,128,1024]{2,1,0:T(8,128)(2,1)} %get-tuple-element.71), channel_id=1, source_target_pairs={{0,16},{1,17},{2,18},{3,19},{4,20},{5,21},{6,22},{7,23},{8,24},{9,... | collective-permute-start | bytes 3145736 | tf_op jit(solution)/shard_map/ppermute | solution.py:407
  447.6 23.6 %collective-permute-start.34 = (bf16[1,1,256,1024]{3,2,1,0:T(8,128)(2,1)}, bf16[1,1,256,1024]{3,2,1,0:T(8,128)(2,1)S(1)}, u32[]{:S(2)}, u32[]{:S(2)}) collective-permute-start(bf16[1,1,256,1024]{3,2,1,0:T(8,128)(2,1)} %fusion.28), channel_id=1, source_target_pairs={{0,2},{1,3},{2,0},{3,1},{4,6},{5,7},{6,4},{7,5},{8,10},{9,11},{10,... | collective-permute-start | bytes 1572872 | tf_op jit(solution)/shard_map/ppermute | solution.py:407
  475.3 31.6 %all-to-all-start.9 = ((bf16[4,128,1024]{2,1,0:T(8,128)(2,1)}), bf16[4,128,1024]{2,1,0:T(8,128)(2,1)S(1)}, u32[]{:S(2)}, u32[]{:S(2)}) async-start(bf16[4,128,1024]{2,1,0:T(8,128)(2,1)} %add_convert_fusion.1), calls=%async_computation.9 | async-start | bytes 2097152 | tf_op jit(solution)/shard_map/all_to_all | solution.py:492
  481.8 7.5 %collective-permute-start.27 = (bf16[2,1,72,1024]{3,2,0,1:T(8,128)(2,1)}, bf16[2,1,72,1024]{3,2,0,1:T(8,128)(2,1)}, u32[]{:S(2)}, u32[]{:S(2)}) collective-permute-start(bf16[2,1,72,1024]{3,2,0,1:T(8,128)(2,1)} %get-tuple-element.163), channel_id=1, source_target_pairs={{0,1},{1,0},{2,3},{3,2},{4,5},{5,4},{6,7},{7,6},{8,9},{9,8},{10,11... | collective-permute-start | bytes 884744 | tf_op jit(solution)/shard_map/ppermute | solution.py:407
  490.6 9.5 %collective-permute-start.28 = (bf16[1,2,72,1024]{3,2,1,0:T(8,128)(2,1)S(1)}, bf16[1,2,72,1024]{3,2,1,0:T(8,128)(2,1)S(1)}, u32[]{:S(2)}, u32[]{:S(2)}) collective-permute-start(bf16[1,2,72,1024]{3,2,1,0:T(8,128)(2,1)S(1)} %get-tuple-element.161), channel_id=1, source_target_pairs={{0,2},{1,3},{2,0},{3,1},{4,6},{5,7},{6,4},{7,5},{8,10},{9,11},{10,... | collective-permute-start | bytes 884744 | tf_op jit(solution)/shard_map/ppermute | solution.py:407
  494.4 61.2 %collective-permute-start.35 = (bf16[256,1024]{1,0:T(8,128)(2,1)}, bf16[256,1024]{1,0:T(8,128)(2,1)}, u32[]{:S(2)}, u32[]{:S(2)}) collective-permute-start(bf16[256,1024]{1,0:T(8,128)(2,1)} %fusion.15), channel_id=1, source_target_pairs={{0,0},{1,4},{2,8},{3,12},{4,2},{5,6},{6,10},{7,14},{8,1},{9,5},{10... | collective-permute-start | bytes 1572872 | tf_op jit(solution)/shard_map/ppermute | solution.py:407
  501.5 56.3 %collective-permute-start.29 = (bf16[256,1024]{1,0:T(8,128)(2,1)}, bf16[256,1024]{1,0:T(8,128)(2,1)S(1)}, u32[]{:S(2)}, u32[]{:S(2)}) collective-permute-start(bf16[256,1024]{1,0:T(8,128)(2,1)} %fusion.23), channel_id=1, source_target_pairs={{0,0},{1,4},{2,8},{3,12},{4,2},{5,6},{6,10},{7,14},{8,1},{9,5},{10... | collective-permute-start | bytes 1572872 | tf_op jit(solution)/shard_map/ppermute | solution.py:407
  507.8 44.0 %all-to-all-start.11 = ((f32[32,1,256]{2,1,0:T(1,128)}), f32[32,1,256]{2,1,0:T(1,128)S(1)}, u32[]{:S(2)}, u32[]{:S(2)}) async-start(f32[32,1,256]{2,1,0:T(1,128)} %copy.135), calls=%async_computation.11 | async-start | bytes 65536 | tf_op jit(solution)/shard_map/all_to_all | solution.py:667
  551.8 14.7 %all-to-all-start.10 = ((bf16[4,32,1792]{2,1,0:T(8,128)(2,1)}), bf16[4,32,1792]{2,1,0:T(8,128)(2,1)S(1)}, u32[]{:S(2)}, u32[]{:S(2)}) async-start(bf16[4,32,1792]{2,1,0:T(8,128)(2,1)} %pad_maximum_fusion.3), calls=%async_computation.10 | async-start | bytes 917504 | tf_op jit(solution)/shard_map/all_to_all | solution.py:658
  557.8 8.0 %collective-permute-start.37 = (bf16[32,1024]{1,0:T(8,128)(2,1)S(1)}, bf16[32,1024]{1,0:T(8,128)(2,1)S(1)}, u32[]{:S(2)}, u32[]{:S(2)}) collective-permute-start(bf16[32,1024]{1,0:T(8,128)(2,1)S(1)} %bitcast.219), channel_id=1, source_target_pairs={{0,0},{1,8},{2,16},{3,24},{4,1},{5,9},{6,17},{7,25},{8,2},{9,10},{... | collective-permute-start | bytes 196616 | tf_op jit(solution)/shard_map/ppermute | solution.py:407
  (59 other events, 905.5 us)

commit v4 on v3

--- a/solution.py
+++ b/solution.py
@@ -572,7 +572,7 @@
         bundle = jnp.concatenate([columns[:, : 3 * group], out_part], axis=1)
         cot_low = to_seq_by(cotangent[0])
         ei_other = swap_dp(expert_inner[0])
-        att_own = gather_ctx(after(bundle, x_low, small, cot_low, ei_other))
+        att_own = gather_ctx(after(bundle, x_low, ei_other))
         ei_own, eo_own = expert_inner[0], expert_outer[0]
         gain1, shift1, gain2, shift2 = (
             small[:, i * rw : (i + 1) * rw].reshape(width).astype(F32) for i in range(4)
@@ -590,11 +590,11 @@
         part = jnp.concatenate([jnp.swapaxes(part, 0, 1).reshape(-1, width), outer_weight])
         ff_own = gather_ctx(after(part, att_own, e_cot))
         ff_other = swap_dp(ff_own)
-        keep = after(keep, ff_own)
+        keep = after(keep, ff_own, eo_other)
         residual = x + scatter_exp_rel(keep[None], away[None], low_bits)[0][0]
         e_cot = gather_ctx(after(e_cot, ff_own, keep)).reshape(nc, nh, nc, capacity, width)
         cot_all = pieces_exp(cot_low, all_bits)
-        residual = after(residual, eo_other, *cot_all)
+        residual = after(residual, *cot_all)
         unit2, scale2 = norm_parts(residual)
         normed2 = (unit2 * gain2 + shift2).astype(BF16)
 

time: 581 us -> 573 us (0.986)
  waiting for transfers between devices: 261 us -> 254 us
    all_to_all x3, waiting for transfers between devices: 71.2 us -> 64.1 us  [gather_ctx(): lax.all_to_all(jnp.broadcast_to(x[None], (nc,) + x.shape), 'ctx', 0, 0, t...]
    all_to_all x1, waiting for transfers between devices: 1.11 us -> 7.04 us  [to_experts(): return lax.all_to_all(out, ('ctx', 'exp'), 0, 0, tiled=True)]
  transfers between devices with their start and end apart: 50 -> 50, of which waited for: 25 -> 25; matrix products, arithmetic and copies ran while one was open for 15% -> 14% of each run, Pallas kernels for 14% -> 14%
where the time goes in v4:
time: 573 us; the launch traced here: 563 us
  waiting for transfers between devices  254 us (44%)
  starting transfers between devices  130 us (23%)
  Pallas kernels  81.3 us (14%)
  local copies, waits for them, and re-layouts  46.5 us (8%)
  other arithmetic  45.9 us (8%)
    ppermute x38, waiting for transfers between devices, send(): return lax.ppermute(x, AXES, pairs)  129 us
    pallas_call x4, Pallas kernels, vmem_call(): pl.pallas_call(kernel, in_specs=[pl.BlockSpec(memory_space=pltpu.SMEM)] +...  81.3 us
    all_to_all x3, waiting for transfers between devices, gather_ctx(): lax.all_to_all(jnp.broadcast_to(x[None], (nc,) + x.shape), 'ctx', 0, 0, t...  64.1 us
    ppermute x38, starting transfers between devices, send(): return lax.ppermute(x, AXES, pairs)  43.8 us
    all_to_all x3, waiting for transfers between devices, scatter_ctx(): parts = lax.all_to_all(parts.astype(BF16), 'ctx', 0, 0, tiled=True)  29.9 us
    all_to_all x1, starting transfers between devices, per_device(): small = lax.all_to_all(small, AXES, 0, 0, tiled=True)  26.7 us
    all_to_all x3, starting transfers between devices, scatter_ctx(): parts = lax.all_to_all(parts.astype(BF16), 'ctx', 0, 0, tiled=True)  17.9 us
    all_to_all x1, waiting for transfers between devices, per_device(): small = lax.all_to_all(small, AXES, 0, 0, tiled=True)  17.4 us
  transfers between devices with their start and end apart: 50, of which 25 were waited for; matrix products, arithmetic and copies ran while one was open for 14% of the time, Pallas kernels for 14%

profile of v4, /device:TPU:4, one launch (start us, length us, event | category | flops | bytes accessed | tf_op | source)
XLA Modules:
  0.0 562.7 jit_solution(7757555340956928320)
XLA Ops:
  2.2 3.4 collective-permute-start
  9.2 5.0 all-to-all-start.1
  14.3 2.7 collective-permute-start.4
  19.4 7.6 %collective-permute-done.4 = bf16[32,1024]{1,0:T(8,128)(2,1)S(1)} collective-permute-done((bf16[32,1024]{1,0:T(8,128)(2,1)S(1)}, bf16[32,1024]{1,0:T(8,128)(2,1)S(1)}, u32[]{:S(2)}, u32[]{:S(2)}) %collective-permute-start.4) | collective-permute-done | bytes 65568 | tf_op jit(solution)/shard_map/ppermute | solution.py:407
  27.3 5.0 all-to-all-start
  32.4 5.7 %all-to-all-done = bf16[32,2,128]{2,1,0:T(2,128)(2,1)S(1)} async-done(((bf16[32,2,128]{2,1,0:T(2,128)(2,1)}), bf16[32,2,128]{2,1,0:T(2,128)(2,1)S(1)}, u32[]{:S(2)}, u32[]{:S(2)}) %all-to-all-start) | async-done | bytes 16416 | tf_op jit(solution)/shard_map/all_to_all | solution.py:560
  39.3 3.5 all-to-all-start.2
  46.5 22.3 %all-to-all-done.2.refs_4_.refs_8_ = bf16[4,128,1024]{2,1,0:T(8,128)(2,1)S(1)} async-done(((bf16[4,128,1024]{2,1,0:T(8,128)(2,1)}), bf16[4,128,1024]{2,1,0:T(8,128)(2,1)S(1)}, u32[]{:S(2)}, u32[]{:S(2)}) %all-to-all-start.2) | async-done | bytes 1048608 | tf_op jit(solution)/shard_map/all_to_all | solution.py:487
  76.7 4.9 collective-permute-done.7
  86.5 4.4 all-to-all-start.3
  93.7 13.3 %shard_map.255 = (bf16[1024,768]{1,0:T(8,128)(2,1)}, bf16[1024,256]{1,0:T(8,128)(2,1)}, bf16[2,256,1024]{2,1,0:T(8,128)(2,1)}, bf16[2,256,1024]{2,1,0:T(8,128)(2,1)}) custom-call(s32[2]{0:T(128)} %pad_add_fusion.where_ref, bf16[256,1024]{1,0:T(8,128)(2,1)} %fusion.10.refs_0_.refs_4_, bf16[256,1024]{1,0:T(8,128)(2,1)} %collective-permute-done.1.refs_1_.refs_5_, ...), custom_call_target="tpu_custom_call" | custom-call | flops 42949672960 | bytes 8396800 | tf_op jit(solution)/shard_map/pallas_call | solution.py:208
  108.4 8.2 %collective-permute-done.10.refs_5_ = bf16[512,1024]{1,0:T(8,128)(2,1)} collective-permute-done((bf16[512,1024]{1,0:T(8,128)(2,1)}, bf16[512,1024]{1,0:T(8,128)(2,1)}, u32[]{:S(2)}, u32[]{:S(2)}) %collective-permute-start.10) | collective-permute-done | bytes 1048608 | tf_op jit(solution)/shard_map/ppermute | solution.py:407
  116.6 28.7 %all-to-all-done.3.refs_8_ = bf16[4,256,1024]{2,1,0:T(8,128)(2,1)} async-done(((bf16[4,256,1024]{2,1,0:T(8,128)(2,1)}), bf16[4,256,1024]{2,1,0:T(8,128)(2,1)}, u32[]{:S(2)}, u32[]{:S(2)}) %all-to-all-start.3) | async-done | bytes 2097184 | tf_op jit(solution)/shard_map/all_to_all | solution.py:487
  147.1 5.1 all-to-all-start.5
  156.2 11.1 %collective-permute-done.16.refs_6_ = bf16[256,1024]{1,0:T(8,128)(2,1)} collective-permute-done((bf16[256,1024]{1,0:T(8,128)(2,1)S(1)}, bf16[256,1024]{1,0:T(8,128)(2,1)}, u32[]{:S(2)}, u32[]{:S(2)}) %collective-permute-start.16) | collective-permute-done | bytes 524320 | tf_op jit(solution)/shard_map/ppermute | solution.py:407
  168.9 7.7 %collective-permute-done.12 = bf16[1,1,256,1024]{3,2,1,0:T(8,128)(2,1)S(1)} collective-permute-done((bf16[1,1,256,1024]{3,2,1,0:T(8,128)(2,1)S(1)}, bf16[1,1,256,1024]{3,2,1,0:T(8,128)(2,1)S(1)}, u32[]{:S(2)}, u32[]{:S(2)}) %collective-permute-start.12) | collective-permute-done | bytes 524320 | tf_op jit(solution)/shard_map/ppermute | solution.py:407
  180.4 10.7 %collective-permute-done.19.refs_2_ = bf16[256,1024]{1,0:T(8,128)(2,1)S(1)} collective-permute-done((bf16[256,1024]{1,0:T(8,128)(2,1)S(1)}, bf16[256,1024]{1,0:T(8,128)(2,1)S(1)}, u32[]{:S(2)}, u32[]{:S(2)}) %collective-permute-start.19) | collective-permute-done | bytes 524320 | tf_op jit(solution)/shard_map/ppermute | solution.py:407
  192.6 13.1 %all-to-all-done.5 = bf16[4,4,72,1024]{3,2,1,0:T(8,128)(2,1)} async-done(((bf16[4,4,72,1024]{3,2,1,0:T(8,128)(2,1)}), bf16[4,4,72,1024]{3,2,1,0:T(8,128)(2,1)}, u32[]{:S(2)}, u32[]{:S(2)}) %all-to-all-start.5) | async-done | bytes 2359328 | tf_op jit(solution)/shard_map/all_to_all | solution.py:487
  207.5 5.1 all-to-all-start.4
  212.6 3.1 collective-permute-done.21.refs_9_
  215.8 19.3 %shard_map.256 = (bf16[2,2,256,1024]{3,2,1,0:T(8,128)(2,1)}, bf16[2,2,256,1024]{3,2,1,0:T(8,128)(2,1)}, bf16[4,256,1024]{2,1,0:T(8,128)(2,1)}, bf16[4,256,1024]{2,1,0:T(8,128)(2,1)}) custom-call(s32[2]{0:T(128)} %pad_add_fusion.where_ref, bf16[256,1024]{1,0:T(8,128)(2,1)} %copy-done.11, bf16[256,1024]{1,0:T(8,128)(2,1)} %collective-permute-done.18.refs_1_, ...), custom_call_target="tpu_custom_call" | custom-call | flops 128849018880 | bytes 16777216 | tf_op jit(solution)/shard_map/pallas_call | solution.py:208
  235.1 3.1 copy.123
  245.8 2.5 add_bitcast_fusion
  253.1 7.0 %all-to-all-done.4 = bf16[16,72,1024]{2,1,0:T(8,128)(2,1)S(1)} async-done(((bf16[16,72,1024]{2,1,0:T(8,128)(2,1)}), bf16[16,72,1024]{2,1,0:T(8,128)(2,1)S(1)}, u32[]{:S(2)}, u32[]{:S(2)}) %all-to-all-start.4) | async-done | bytes 2359328 | tf_op jit(solution)/shard_map/all_to_all | solution.py:550
  261.6 25.2 %shard_map.257 = (bf16[1152,1024]{1,0:T(8,128)(2,1)}, bf16[1152,1024]{1,0:T(8,128)(2,1)}, bf16[1024,512]{1,0:T(8,128)(2,1)}, bf16[1024,512]{1,0:T(8,128)(2,1)}, ...) custom-call(s32[2]{0:T(128)} %pad_add_fusion.where_ref, bf16[1152,1024]{1,0:T(8,128)(2,1)} %bitcast.190, ...), custom_call_target="tpu_custom_call" | custom-call | flops 144955146240 | bytes 18612736 | tf_op jit(solution)/shard_map/pallas_call | solution.py:208
  288.4 9.2 %all-to-all-start.6 = ((bf16[16,72,1024]{2,1,0:T(8,128)(2,1)}), bf16[16,72,1024]{2,1,0:T(8,128)(2,1)S(1)}, u32[]{:S(2)}, u32[]{:S(2)}) async-start(bf16[16,72,1024]{2,1,0:T(8,128)(2,1)} %bitcast.191), calls=%async_computation.6 | async-start | bytes 4718592 | tf_op jit(solution)/shard_map/all_to_all | solution.py:554
  299.6 4.5 add_convert_fusion
  304.1 19.7 %collective-permute-done.25 = bf16[1024,512]{1,0:T(8,128)(2,1)S(1)} collective-permute-done((bf16[1024,512]{1,0:T(8,128)(2,1)}, bf16[1024,512]{1,0:T(8,128)(2,1)S(1)}, u32[]{:S(2)}, u32[]{:S(2)}) %collective-permute-start.25) | collective-permute-done | bytes 1048608 | tf_op jit(solution)/shard_map/ppermute | solution.py:407
  324.8 20.8 %collective-permute-done.26 = bf16[512,1024]{1,0:T(8,128)(2,1)} collective-permute-done((bf16[512,1024]{1,0:T(8,128)(2,1)S(1)}, bf16[512,1024]{1,0:T(8,128)(2,1)}, u32[]{:S(2)}, u32[]{:S(2)}) %collective-permute-start.26) | collective-permute-done | bytes 1048608 | tf_op jit(solution)/shard_map/ppermute | solution.py:407
  345.6 8.5 %all-to-all-start.7 = ((bf16[4,256,1024]{2,1,0:T(8,128)(2,1)}), bf16[4,256,1024]{2,1,0:T(8,128)(2,1)}, u32[]{:S(2)}, u32[]{:S(2)}) async-start(bf16[4,256,1024]{2,1,0:T(8,128)(2,1)} %add_convert_fusion), calls=%async_computation.7 | async-start | bytes 4194304 | tf_op jit(solution)/shard_map/all_to_all | solution.py:492
  360.3 12.9 %collective-permute-done.31.refs_2_ = bf16[256,1024]{1,0:T(8,128)(2,1)} collective-permute-done((bf16[256,1024]{1,0:T(8,128)(2,1)S(1)}, bf16[256,1024]{1,0:T(8,128)(2,1)}, u32[]{:S(2)}, u32[]{:S(2)}) %collective-permute-start.31) | collective-permute-done | bytes 524320 | tf_op jit(solution)/shard_map/ppermute | solution.py:407
  373.3 29.5 %all-to-all-done.7 = bf16[4,256,1024]{2,1,0:T(8,128)(2,1)} async-done(((bf16[4,256,1024]{2,1,0:T(8,128)(2,1)}), bf16[4,256,1024]{2,1,0:T(8,128)(2,1)}, u32[]{:S(2)}, u32[]{:S(2)}) %all-to-all-start.7) | async-done | bytes 2097184 | tf_op jit(solution)/shard_map/all_to_all | solution.py:492
  404.9 4.7 all-to-all-start.8
  409.7 23.6 %shard_map.258 = (bf16[2,256,1024]{2,1,0:T(8,128)(2,1)}, bf16[2,256,1024]{2,1,0:T(8,128)(2,1)}, bf16[4,128,1024]{2,1,0:T(8,128)(2,1)}, bf16[4,128,1024]{2,1,0:T(8,128)(2,1)}) custom-call(s32[2]{0:T(128)} %pad_add_fusion.where_ref, bf16[256,1024]{1,0:T(8,128)(2,1)} %copy-done.29, bf16[256,1024]{1,0:T(8,128)(2,1)} %collective-permute-done.30.refs_1_, ...), custom_call_target="tpu_custom_call" | custom-call | flops 96636764160 | bytes 12591104 | tf_op jit(solution)/shard_map/pallas_call | solution.py:208
  435.1 3.3 add_bitcast_fusion.2
  440.9 2.9 add_bitcast_fusion.1
  447.5 12.0 %collective-permute-done.36 = bf16[4,128,1024]{2,1,0:T(8,128)(2,1)} collective-permute-done((bf16[4,128,1024]{2,1,0:T(8,128)(2,1)}, bf16[4,128,1024]{2,1,0:T(8,128)(2,1)}, u32[]{:S(2)}, u32[]{:S(2)}) %collective-permute-start.36) | collective-permute-done | bytes 1048608 | tf_op jit(solution)/shard_map/ppermute | solution.py:407
  459.5 2.6 add_convert_fusion.1
  463.1 3.1 reduce_sum.186
  466.2 4.7 all-to-all-start.9
  476.1 2.7 concatenate.68
  482.7 2.6 fusion.15
  485.4 5.1 collective-permute-start.35
  492.4 5.4 collective-permute-start.29
  498.7 26.7 %all-to-all-start.11 = ((f32[32,1,256]{2,1,0:T(1,128)}), f32[32,1,256]{2,1,0:T(1,128)S(1)}, u32[]{:S(2)}, u32[]{:S(2)}) async-start(f32[32,1,256]{2,1,0:T(1,128)} %copy.135), calls=%async_computation.11 | async-start | bytes 65536 | tf_op jit(solution)/shard_map/all_to_all | solution.py:667
  526.2 17.4 %all-to-all-done.11 = f32[32,1,256]{2,1,0:T(1,128)S(1)} async-done(((f32[32,1,256]{2,1,0:T(1,128)}), f32[32,1,256]{2,1,0:T(1,128)S(1)}, u32[]{:S(2)}, u32[]{:S(2)}) %all-to-all-start.11) | async-done | bytes 32800 | tf_op jit(solution)/shard_map/all_to_all | solution.py:667
  543.6 4.0 all-to-all-start.10
  553.4 4.4 collective-permute-done.37
  (300 shorter events, 102.4 us)
Async XLA Ops:
  0.6 31.8 %collective-permute-start.5 = (bf16[1024,512]{1,0:T(8,128)(2,1)}, bf16[1024,512]{1,0:T(8,128)(2,1)S(1)}, u32[]{:S(2)}, u32[]{:S(2)}) collective-permute-start(bf16[1024,512]{1,0:T(8,128)(2,1)} %bitcast.233), channel_id=1, source_target_pairs={{0,16},{1,17},{2,18},{3,19},{4,20},{5,21},{6,22},{7,23},{8,24},{9,... | collective-permute-start | bytes 3145736 | tf_op jit(solution)/shard_map/ppermute | solution.py:407
  2.2 30.2 %collective-permute-start = (bf16[256,1024]{1,0:T(8,128)(2,1)}, bf16[256,1024]{1,0:T(8,128)(2,1)S(1)}, u32[]{:S(2)}, u32[]{:S(2)}) collective-permute-start(bf16[256,1024]{1,0:T(8,128)(2,1)} %bitcast.239), channel_id=1, source_target_pairs={{0,0},{1,8},{2,4},{3,12},{4,1},{5,9},{6,5},{7,13},{8,2},{9,10},{10... | collective-permute-start | bytes 1572872 | tf_op jit(solution)/shard_map/ppermute | solution.py:407
  9.2 18.1 %all-to-all-start.1 = ((bf16[4,32,1792]{2,1,0:T(8,128)(2,1)}), bf16[4,32,1792]{2,1,0:T(8,128)(2,1)S(1)}, u32[]{:S(2)}, u32[]{:S(2)}) async-start(bf16[4,32,1792]{2,1,0:T(8,128)(2,1)} %pad_maximum_fusion.2), calls=%async_computation.1 | async-start | bytes 917504 | tf_op jit(solution)/shard_map/all_to_all | solution.py:569
  14.3 12.8 %collective-permute-start.4 = (bf16[32,1024]{1,0:T(8,128)(2,1)S(1)}, bf16[32,1024]{1,0:T(8,128)(2,1)S(1)}, u32[]{:S(2)}, u32[]{:S(2)}) collective-permute-start(bf16[32,1024]{1,0:T(8,128)(2,1)S(1)} %copy-done.60), channel_id=1, source_target_pairs={{0,0},{1,4},{2,8},{3,12},{4,16},{5,20},{6,24},{7,28},{8,1},{9,5},{... | collective-permute-start | bytes 196616 | tf_op jit(solution)/shard_map/ppermute | solution.py:407
  27.3 10.9 %all-to-all-start = ((bf16[32,2,128]{2,1,0:T(2,128)(2,1)}), bf16[32,2,128]{2,1,0:T(2,128)(2,1)S(1)}, u32[]{:S(2)}, u32[]{:S(2)}) async-start(bf16[32,2,128]{2,1,0:T(2,128)(2,1)} %reshape.514), calls=%async_computation | async-start | bytes 32768 | tf_op jit(solution)/shard_map/all_to_all | solution.py:560
  39.3 29.5 %all-to-all-start.2 = ((bf16[4,128,1024]{2,1,0:T(8,128)(2,1)}), bf16[4,128,1024]{2,1,0:T(8,128)(2,1)S(1)}, u32[]{:S(2)}, u32[]{:S(2)}) async-start(bf16[4,128,1024]{2,1,0:T(8,128)(2,1)} %broadcast_in_dim.36), calls=%async_computation.2 | async-start | bytes 2097152 | tf_op jit(solution)/shard_map/all_to_all | solution.py:487
  45.0 27.2 %collective-permute-start.2 = (bf16[256,1024]{1,0:T(8,128)(2,1)}, bf16[256,1024]{1,0:T(8,128)(2,1)}, u32[]{:S(2)}, u32[]{:S(2)}) collective-permute-start(bf16[256,1024]{1,0:T(8,128)(2,1)} %fusion.10.refs_0_.refs_4_), channel_id=1, source_target_pairs={{0,2},{1,3},{2,0},{3,1},{4,6},{5,7},{6,4},{7,5},{8,10},{9,11},{10,... | collective-permute-start | bytes 1572872 | tf_op jit(solution)/shard_map/ppermute | solution.py:407
  68.8 24.3 %collective-permute-start.6 = (bf16[4,128,1024]{2,1,0:T(8,128)(2,1)S(1)}, bf16[4,128,1024]{2,1,0:T(8,128)(2,1)}, u32[]{:S(2)}, u32[]{:S(2)}) collective-permute-start(bf16[4,128,1024]{2,1,0:T(8,128)(2,1)S(1)} %all-to-all-done.2.refs_4_.refs_8_), channel_id=1, source_target_pairs={{0,16},{1,17},{2,18},{3,19},{4,20},{5,21},{6,22},{7,23},{8,24},{9,... | collective-permute-start | bytes 3145736 | tf_op jit(solution)/shard_map/ppermute | solution.py:407
  72.0 21.6 %collective-permute-start.1 = (bf16[256,1024]{1,0:T(8,128)(2,1)}, bf16[256,1024]{1,0:T(8,128)(2,1)}, u32[]{:S(2)}, u32[]{:S(2)}) collective-permute-start(bf16[256,1024]{1,0:T(8,128)(2,1)} %fusion.10.refs_0_.refs_4_), channel_id=1, source_target_pairs={{0,1},{1,0},{2,3},{3,2},{4,5},{5,4},{6,7},{7,6},{8,9},{9,8},{10,11... | collective-permute-start | bytes 1572872 | tf_op jit(solution)/shard_map/ppermute | solution.py:407
  72.2 21.4 %collective-permute-start.3 = (bf16[256,1024]{1,0:T(8,128)(2,1)}, bf16[256,1024]{1,0:T(8,128)(2,1)}, u32[]{:S(2)}, u32[]{:S(2)}) collective-permute-start(bf16[256,1024]{1,0:T(8,128)(2,1)} %collective-permute-done.2.refs_2_.refs_6_), channel_id=1, source_target_pairs={{0,1},{1,0},{2,3},{3,2},{4,5},{5,4},{6,7},{7,6},{8,9},{9,8},{10,11... | collective-permute-start | bytes 1572872 | tf_op jit(solution)/shard_map/ppermute | solution.py:407
  72.6 11.0 %collective-permute-start.9 = (bf16[1,2,72,1024]{3,2,1,0:T(8,128)(2,1)S(1)}, bf16[1,2,72,1024]{3,2,1,0:T(8,128)(2,1)}, u32[]{:S(2)}, u32[]{:S(2)}) collective-permute-start(bf16[1,2,72,1024]{3,2,1,0:T(8,128)(2,1)S(1)} %get-tuple-element.165), channel_id=1, source_target_pairs={{0,2},{1,3},{2,0},{3,1},{4,6},{5,7},{6,4},{7,5},{8,10},{9,11},{10,... | collective-permute-start | bytes 884744 | tf_op jit(solution)/shard_map/ppermute | solution.py:407
  74.2 7.5 %collective-permute-start.7 = (s32[12,128]{1,0:T(8,128)S(1)}, s32[12,128]{1,0:T(8,128)S(1)}, u32[]{:S(2)}, u32[]{:S(2)}) collective-permute-start(s32[12,128]{1,0:T(8,128)S(1)} %add_bitcast_fusion.3), channel_id=1, source_target_pairs={{0,0},{1,8},{2,4},{3,12},{4,1},{5,9},{6,5},{7,13},{8,2},{9,10},{10... | collective-permute-start | bytes 18440 | tf_op jit(solution)/shard_map/ppermute | solution.py:407
  81.6 25.3 %collective-permute-start.13 = (bf16[256,1024]{1,0:T(8,128)(2,1)S(1)}, bf16[256,1024]{1,0:T(8,128)(2,1)}, u32[]{:S(2)}, u32[]{:S(2)}) collective-permute-start(bf16[256,1024]{1,0:T(8,128)(2,1)S(1)} %bitcast.209), channel_id=1, source_target_pairs={{0,2},{1,3},{2,0},{3,1},{4,6},{5,7},{6,4},{7,5},{8,10},{9,11},{10,... | collective-permute-start | bytes 1572872 | tf_op jit(solution)/shard_map/ppermute | solution.py:407
  86.5 58.9 %all-to-all-start.3 = ((bf16[4,256,1024]{2,1,0:T(8,128)(2,1)}), bf16[4,256,1024]{2,1,0:T(8,128)(2,1)}, u32[]{:S(2)}, u32[]{:S(2)}) async-start(bf16[4,256,1024]{2,1,0:T(8,128)(2,1)} %broadcast_in_dim.40), calls=%async_computation.3 | async-start | bytes 4194304 | tf_op jit(solution)/shard_map/all_to_all | solution.py:487
  93.1 23.6 %collective-permute-start.10 = (bf16[512,1024]{1,0:T(8,128)(2,1)}, bf16[512,1024]{1,0:T(8,128)(2,1)}, u32[]{:S(2)}, u32[]{:S(2)}) collective-permute-start(bf16[512,1024]{1,0:T(8,128)(2,1)} %bitcast.235), channel_id=1, source_target_pairs={{0,16},{1,17},{2,18},{3,19},{4,20},{5,21},{6,22},{7,23},{8,24},{9,... | collective-permute-start | bytes 3145736 | tf_op jit(solution)/shard_map/ppermute | solution.py:407
  106.9 47.1 %collective-permute-start.11 = (bf16[1,2,256,1024]{3,2,1,0:T(8,128)(2,1)}, bf16[1,2,256,1024]{3,2,1,0:T(8,128)(2,1)S(1)}, u32[]{:S(2)}, u32[]{:S(2)}) collective-permute-start(bf16[1,2,256,1024]{3,2,1,0:T(8,128)(2,1)} %bitcast.238), channel_id=1, source_target_pairs={{0,1},{1,0},{2,3},{3,2},{4,5},{5,4},{6,7},{7,6},{8,9},{9,8},{10,11... | collective-permute-start | bytes 3145736 | tf_op jit(solution)/shard_map/ppermute | solution.py:407
  106.9 45.3 %collective-permute-start.14 = (bf16[256,1024]{1,0:T(8,128)(2,1)}, bf16[256,1024]{1,0:T(8,128)(2,1)S(1)}, u32[]{:S(2)}, u32[]{:S(2)}) collective-permute-start(bf16[256,1024]{1,0:T(8,128)(2,1)} %collective-permute-done.13), channel_id=1, source_target_pairs={{0,4},{1,12},{2,0},{3,8},{4,5},{5,13},{6,1},{7,9},{8,6},{9,14},{10... | collective-permute-start | bytes 1572872 | tf_op jit(solution)/shard_map/ppermute | solution.py:407
  147.1 58.7 %all-to-all-start.5 = ((bf16[4,4,72,1024]{3,2,1,0:T(8,128)(2,1)}), bf16[4,4,72,1024]{3,2,1,0:T(8,128)(2,1)}, u32[]{:S(2)}, u32[]{:S(2)}) async-start(bf16[4,4,72,1024]{3,2,1,0:T(8,128)(2,1)} %broadcast_in_dim.44), calls=%async_computation.5 | async-start | bytes 4718592 | tf_op jit(solution)/shard_map/all_to_all | solution.py:487
  152.2 15.0 %collective-permute-start.16 = (bf16[256,1024]{1,0:T(8,128)(2,1)S(1)}, bf16[256,1024]{1,0:T(8,128)(2,1)}, u32[]{:S(2)}, u32[]{:S(2)}) collective-permute-start(bf16[256,1024]{1,0:T(8,128)(2,1)S(1)} %collective-permute-done.14.refs_4_), channel_id=1, source_target_pairs={{0,2},{1,3},{2,0},{3,1},{4,6},{5,7},{6,4},{7,5},{8,10},{9,11},{10,... | collective-permute-start | bytes 1572872 | tf_op jit(solution)/shard_map/ppermute | solution.py:407
  155.8 20.8 %collective-permute-start.12 = (bf16[1,1,256,1024]{3,2,1,0:T(8,128)(2,1)S(1)}, bf16[1,1,256,1024]{3,2,1,0:T(8,128)(2,1)S(1)}, u32[]{:S(2)}, u32[]{:S(2)}) collective-permute-start(bf16[1,1,256,1024]{3,2,1,0:T(8,128)(2,1)S(1)} %fusion.27), channel_id=1, source_target_pairs={{0,2},{1,3},{2,0},{3,1},{4,6},{5,7},{6,4},{7,5},{8,10},{9,11},{10,... | collective-permute-start | bytes 1572872 | tf_op jit(solution)/shard_map/ppermute | solution.py:407
  156.2 21.9 %collective-permute-start.15 = (bf16[256,1024]{1,0:T(8,128)(2,1)S(1)}, bf16[256,1024]{1,0:T(8,128)(2,1)S(1)}, u32[]{:S(2)}, u32[]{:S(2)}) collective-permute-start(bf16[256,1024]{1,0:T(8,128)(2,1)S(1)} %collective-permute-done.14.refs_4_), channel_id=1, source_target_pairs={{0,1},{1,0},{2,3},{3,2},{4,5},{5,4},{6,7},{7,6},{8,9},{9,8},{10,11... | collective-permute-start | bytes 1572872 | tf_op jit(solution)/shard_map/ppermute | solution.py:407
  167.2 10.8 %collective-permute-start.17 = (bf16[256,1024]{1,0:T(8,128)(2,1)}, bf16[256,1024]{1,0:T(8,128)(2,1)}, u32[]{:S(2)}, u32[]{:S(2)}) collective-permute-start(bf16[256,1024]{1,0:T(8,128)(2,1)} %collective-permute-done.16.refs_6_), channel_id=1, source_target_pairs={{0,1},{1,0},{2,3},{3,2},{4,5},{5,4},{6,7},{7,6},{8,9},{9,8},{10,11... | collective-permute-start | bytes 1572872 | tf_op jit(solution)/shard_map/ppermute | solution.py:407
  167.4 48.4 %collective-permute-start.21 = (bf16[4,256,1024]{2,1,0:T(8,128)(2,1)}, bf16[4,256,1024]{2,1,0:T(8,128)(2,1)}, u32[]{:S(2)}, u32[]{:S(2)}) collective-permute-start(bf16[4,256,1024]{2,1,0:T(8,128)(2,1)} %all-to-all-done.3.refs_8_), channel_id=1, source_target_pairs={{0,16},{1,17},{2,18},{3,19},{4,20},{5,21},{6,22},{7,23},{8,24},{9,... | collective-permute-start | bytes 6291464 | tf_op jit(solution)/shard_map/ppermute | solution.py:407
  178.8 12.3 %collective-permute-start.19 = (bf16[256,1024]{1,0:T(8,128)(2,1)S(1)}, bf16[256,1024]{1,0:T(8,128)(2,1)S(1)}, u32[]{:S(2)}, u32[]{:S(2)}) collective-permute-start(bf16[256,1024]{1,0:T(8,128)(2,1)S(1)} %add_convert_fusion.2.refs_0_), channel_id=1, source_target_pairs={{0,2},{1,3},{2,0},{3,1},{4,6},{5,7},{6,4},{7,5},{8,10},{9,11},{10,... | collective-permute-start | bytes 1572872 | tf_op jit(solution)/shard_map/ppermute | solution.py:407
  180.4 32.2 %collective-permute-start.18 = (bf16[256,1024]{1,0:T(8,128)(2,1)S(1)}, bf16[256,1024]{1,0:T(8,128)(2,1)}, u32[]{:S(2)}, u32[]{:S(2)}) collective-permute-start(bf16[256,1024]{1,0:T(8,128)(2,1)S(1)} %add_convert_fusion.2.refs_0_), channel_id=1, source_target_pairs={{0,1},{1,0},{2,3},{3,2},{4,5},{5,4},{6,7},{7,6},{8,9},{9,8},{10,11... | collective-permute-start | bytes 1572872 | tf_op jit(solution)/shard_map/ppermute | solution.py:407
  191.1 21.5 %collective-permute-start.20 = (bf16[256,1024]{1,0:T(8,128)(2,1)S(1)}, bf16[256,1024]{1,0:T(8,128)(2,1)}, u32[]{:S(2)}, u32[]{:S(2)}) collective-permute-start(bf16[256,1024]{1,0:T(8,128)(2,1)S(1)} %collective-permute-done.19.refs_2_), channel_id=1, source_target_pairs={{0,1},{1,0},{2,3},{3,2},{4,5},{5,4},{6,7},{7,6},{8,9},{9,8},{10,11... | collective-permute-start | bytes 1572872 | tf_op jit(solution)/shard_map/ppermute | solution.py:407
  207.5 52.7 %all-to-all-start.4 = ((bf16[16,72,1024]{2,1,0:T(8,128)(2,1)}), bf16[16,72,1024]{2,1,0:T(8,128)(2,1)S(1)}, u32[]{:S(2)}, u32[]{:S(2)}) async-start(bf16[16,72,1024]{2,1,0:T(8,128)(2,1)} %bitcast.38), calls=%async_computation.4 | async-start | bytes 4718592 | tf_op jit(solution)/shard_map/all_to_all | solution.py:550
  238.2 7.1 %collective-permute-start.22 = (bf16[2,2,256,1024]{3,2,0,1:T(8,128)(2,1)}, bf16[2,2,256,1024]{3,2,0,1:T(8,128)(2,1)}, u32[]{:S(2)}, u32[]{:S(2)}) collective-permute-start(bf16[2,2,256,1024]{3,2,0,1:T(8,128)(2,1)} %copy.123), channel_id=1, source_target_pairs={{0,1},{1,0},{2,3},{3,2},{4,5},{5,4},{6,7},{7,6},{8,9},{9,8},{10,11... | collective-permute-start | bytes 6291464 | tf_op jit(solution)/shard_map/ppermute | solution.py:407
  240.0 48.4 %collective-permute-start.24 = (bf16[4,256,1024]{2,1,0:T(8,128)(2,1)}, bf16[4,256,1024]{2,1,0:T(8,128)(2,1)}, u32[]{:S(2)}, u32[]{:S(2)}) collective-permute-start(bf16[4,256,1024]{2,1,0:T(8,128)(2,1)} %get-tuple-element.58), channel_id=1, source_target_pairs={{0,16},{1,17},{2,18},{3,19},{4,20},{5,21},{6,22},{7,23},{8,24},{9,... | collective-permute-start | bytes 6291464 | tf_op jit(solution)/shard_map/ppermute | solution.py:407
  251.4 37.0 %collective-permute-start.23 = (bf16[2,1,256,1024]{3,2,1,0:T(8,128)(2,1)}, bf16[2,1,256,1024]{3,2,1,0:T(8,128)(2,1)}, u32[]{:S(2)}, u32[]{:S(2)}) collective-permute-start(bf16[2,1,256,1024]{3,2,1,0:T(8,128)(2,1)} %fusion.18), channel_id=1, source_target_pairs={{0,2},{1,3},{2,0},{3,1},{4,6},{5,7},{6,4},{7,5},{8,10},{9,11},{10,... | collective-permute-start | bytes 3145736 | tf_op jit(solution)/shard_map/ppermute | solution.py:407
  288.4 57.2 %all-to-all-start.6 = ((bf16[16,72,1024]{2,1,0:T(8,128)(2,1)}), bf16[16,72,1024]{2,1,0:T(8,128)(2,1)S(1)}, u32[]{:S(2)}, u32[]{:S(2)}) async-start(bf16[16,72,1024]{2,1,0:T(8,128)(2,1)} %bitcast.191), calls=%async_computation.6 | async-start | bytes 4718592 | tf_op jit(solution)/shard_map/all_to_all | solution.py:554
  297.6 26.2 %collective-permute-start.25 = (bf16[1024,512]{1,0:T(8,128)(2,1)}, bf16[1024,512]{1,0:T(8,128)(2,1)S(1)}, u32[]{:S(2)}, u32[]{:S(2)}) collective-permute-start(bf16[1024,512]{1,0:T(8,128)(2,1)} %get-tuple-element.61), channel_id=1, source_target_pairs={{0,16},{1,17},{2,18},{3,19},{4,20},{5,21},{6,22},{7,23},{8,24},{9,... | collective-permute-start | bytes 3145736 | tf_op jit(solution)/shard_map/ppermute | solution.py:407
  299.0 46.5 %collective-permute-start.26 = (bf16[512,1024]{1,0:T(8,128)(2,1)S(1)}, bf16[512,1024]{1,0:T(8,128)(2,1)}, u32[]{:S(2)}, u32[]{:S(2)}) collective-permute-start(bf16[512,1024]{1,0:T(8,128)(2,1)S(1)} %copy-done.57), channel_id=1, source_target_pairs={{0,16},{1,17},{2,18},{3,19},{4,20},{5,21},{6,22},{7,23},{8,24},{9,... | collective-permute-start | bytes 3145736 | tf_op jit(solution)/shard_map/ppermute | solution.py:407
  345.6 57.2 %all-to-all-start.7 = ((bf16[4,256,1024]{2,1,0:T(8,128)(2,1)}), bf16[4,256,1024]{2,1,0:T(8,128)(2,1)}, u32[]{:S(2)}, u32[]{:S(2)}) async-start(bf16[4,256,1024]{2,1,0:T(8,128)(2,1)} %add_convert_fusion), calls=%async_computation.7 | async-start | bytes 4194304 | tf_op jit(solution)/shard_map/all_to_all | solution.py:492
  359.3 14.0 %collective-permute-start.31 = (bf16[256,1024]{1,0:T(8,128)(2,1)S(1)}, bf16[256,1024]{1,0:T(8,128)(2,1)}, u32[]{:S(2)}, u32[]{:S(2)}) collective-permute-start(bf16[256,1024]{1,0:T(8,128)(2,1)S(1)} %get-tuple-element.65.refs_0_), channel_id=1, source_target_pairs={{0,2},{1,3},{2,0},{3,1},{4,6},{5,7},{6,4},{7,5},{8,10},{9,11},{10,... | collective-permute-start | bytes 1572872 | tf_op jit(solution)/shard_map/ppermute | solution.py:407
  360.3 49.3 %collective-permute-start.30 = (bf16[256,1024]{1,0:T(8,128)(2,1)S(1)}, bf16[256,1024]{1,0:T(8,128)(2,1)}, u32[]{:S(2)}, u32[]{:S(2)}) collective-permute-start(bf16[256,1024]{1,0:T(8,128)(2,1)S(1)} %get-tuple-element.65.refs_0_), channel_id=1, source_target_pairs={{0,1},{1,0},{2,3},{3,2},{4,5},{5,4},{6,7},{7,6},{8,9},{9,8},{10,11... | collective-permute-start | bytes 1572872 | tf_op jit(solution)/shard_map/ppermute | solution.py:407
  373.3 36.4 %collective-permute-start.32 = (bf16[256,1024]{1,0:T(8,128)(2,1)}, bf16[256,1024]{1,0:T(8,128)(2,1)}, u32[]{:S(2)}, u32[]{:S(2)}) collective-permute-start(bf16[256,1024]{1,0:T(8,128)(2,1)} %collective-permute-done.31.refs_2_), channel_id=1, source_target_pairs={{0,1},{1,0},{2,3},{3,2},{4,5},{5,4},{6,7},{7,6},{8,9},{9,8},{10,11... | collective-permute-start | bytes 1572872 | tf_op jit(solution)/shard_map/ppermute | solution.py:407
  404.9 58.2 %all-to-all-start.8 = ((bf16[4,288,1024]{2,1,0:T(8,128)(2,1)}), bf16[4,288,1024]{2,1,0:T(8,128)(2,1)}, u32[]{:S(2)}, u32[]{:S(2)}) async-start(bf16[4,288,1024]{2,1,0:T(8,128)(2,1)} %bitcast.189), calls=%async_computation.8 | async-start | bytes 4718592 | tf_op jit(solution)/shard_map/all_to_all | solution.py:492
  433.6 25.9 %collective-permute-start.36 = (bf16[4,128,1024]{2,1,0:T(8,128)(2,1)}, bf16[4,128,1024]{2,1,0:T(8,128)(2,1)}, u32[]{:S(2)}, u32[]{:S(2)}) collective-permute-start(bf16[4,128,1024]{2,1,0:T(8,128)(2,1)} %get-tuple-element.71), channel_id=1, source_target_pairs={{0,16},{1,17},{2,18},{3,19},{4,20},{5,21},{6,22},{7,23},{8,24},{9,... | collective-permute-start | bytes 3145736 | tf_op jit(solution)/shard_map/ppermute | solution.py:407
  439.7 22.4 %collective-permute-start.34 = (bf16[1,1,256,1024]{3,2,1,0:T(8,128)(2,1)}, bf16[1,1,256,1024]{3,2,1,0:T(8,128)(2,1)S(1)}, u32[]{:S(2)}, u32[]{:S(2)}) collective-permute-start(bf16[1,1,256,1024]{3,2,1,0:T(8,128)(2,1)} %fusion.28), channel_id=1, source_target_pairs={{0,2},{1,3},{2,0},{3,1},{4,6},{5,7},{6,4},{7,5},{8,10},{9,11},{10,... | collective-permute-start | bytes 1572872 | tf_op jit(solution)/shard_map/ppermute | solution.py:407
  466.2 31.6 %all-to-all-start.9 = ((bf16[4,128,1024]{2,1,0:T(8,128)(2,1)}), bf16[4,128,1024]{2,1,0:T(8,128)(2,1)S(1)}, u32[]{:S(2)}, u32[]{:S(2)}) async-start(bf16[4,128,1024]{2,1,0:T(8,128)(2,1)} %add_convert_fusion.1), calls=%async_computation.9 | async-start | bytes 2097152 | tf_op jit(solution)/shard_map/all_to_all | solution.py:492
  472.7 7.5 %collective-permute-start.27 = (bf16[2,1,72,1024]{3,2,0,1:T(8,128)(2,1)}, bf16[2,1,72,1024]{3,2,0,1:T(8,128)(2,1)}, u32[]{:S(2)}, u32[]{:S(2)}) collective-permute-start(bf16[2,1,72,1024]{3,2,0,1:T(8,128)(2,1)} %get-tuple-element.163), channel_id=1, source_target_pairs={{0,1},{1,0},{2,3},{3,2},{4,5},{5,4},{6,7},{7,6},{8,9},{9,8},{10,11... | collective-permute-start | bytes 884744 | tf_op jit(solution)/shard_map/ppermute | solution.py:407
  481.5 9.5 %collective-permute-start.28 = (bf16[1,2,72,1024]{3,2,1,0:T(8,128)(2,1)S(1)}, bf16[1,2,72,1024]{3,2,1,0:T(8,128)(2,1)S(1)}, u32[]{:S(2)}, u32[]{:S(2)}) collective-permute-start(bf16[1,2,72,1024]{3,2,1,0:T(8,128)(2,1)S(1)} %get-tuple-element.161), channel_id=1, source_target_pairs={{0,2},{1,3},{2,0},{3,1},{4,6},{5,7},{6,4},{7,5},{8,10},{9,11},{10,... | collective-permute-start | bytes 884744 | tf_op jit(solution)/shard_map/ppermute | solution.py:407
  485.4 62.3 %collective-permute-start.35 = (bf16[256,1024]{1,0:T(8,128)(2,1)}, bf16[256,1024]{1,0:T(8,128)(2,1)}, u32[]{:S(2)}, u32[]{:S(2)}) collective-permute-start(bf16[256,1024]{1,0:T(8,128)(2,1)} %fusion.15), channel_id=1, source_target_pairs={{0,0},{1,4},{2,8},{3,12},{4,2},{5,6},{6,10},{7,14},{8,1},{9,5},{10... | collective-permute-start | bytes 1572872 | tf_op jit(solution)/shard_map/ppermute | solution.py:407
  492.4 57.4 %collective-permute-start.29 = (bf16[256,1024]{1,0:T(8,128)(2,1)}, bf16[256,1024]{1,0:T(8,128)(2,1)S(1)}, u32[]{:S(2)}, u32[]{:S(2)}) collective-permute-start(bf16[256,1024]{1,0:T(8,128)(2,1)} %fusion.23), channel_id=1, source_target_pairs={{0,0},{1,4},{2,8},{3,12},{4,2},{5,6},{6,10},{7,14},{8,1},{9,5},{10... | collective-permute-start | bytes 1572872 | tf_op jit(solution)/shard_map/ppermute | solution.py:407
  498.7 44.9 %all-to-all-start.11 = ((f32[32,1,256]{2,1,0:T(1,128)}), f32[32,1,256]{2,1,0:T(1,128)S(1)}, u32[]{:S(2)}, u32[]{:S(2)}) async-start(f32[32,1,256]{2,1,0:T(1,128)} %copy.135), calls=%async_computation.11 | async-start | bytes 65536 | tf_op jit(solution)/shard_map/all_to_all | solution.py:667
  543.6 14.8 %all-to-all-start.10 = ((bf16[4,32,1792]{2,1,0:T(8,128)(2,1)}), bf16[4,32,1792]{2,1,0:T(8,128)(2,1)S(1)}, u32[]{:S(2)}, u32[]{:S(2)}) async-start(bf16[4,32,1792]{2,1,0:T(8,128)(2,1)} %pad_maximum_fusion.3), calls=%async_computation.10 | async-start | bytes 917504 | tf_op jit(solution)/shard_map/all_to_all | solution.py:658
  549.8 8.0 %collective-permute-start.37 = (bf16[32,1024]{1,0:T(8,128)(2,1)S(1)}, bf16[32,1024]{1,0:T(8,128)(2,1)S(1)}, u32[]{:S(2)}, u32[]{:S(2)}) collective-permute-start(bf16[32,1024]{1,0:T(8,128)(2,1)S(1)} %bitcast.220), channel_id=1, source_target_pairs={{0,0},{1,8},{2,16},{3,24},{4,1},{5,9},{6,17},{7,25},{8,2},{9,10},{... | collective-permute-start | bytes 196616 | tf_op jit(solution)/shard_map/ppermute | solution.py:407
  (63 other events, 899.2 us)

commit v5 on v4

--- a/solution.py
+++ b/solution.py
@@ -588,7 +588,7 @@
         e_cot = trade_exp(rows_out(table_there, cotangent[0]), all_bits)
         part = columns[:, 3 * group :].reshape(width // ff, -1, ff)
         part = jnp.concatenate([jnp.swapaxes(part, 0, 1).reshape(-1, width), outer_weight])
-        ff_own = gather_ctx(after(part, att_own, e_cot))
+        ff_own = gather_ctx(after(part, att_own))
         ff_other = swap_dp(ff_own)
         keep = after(keep, ff_own, eo_other)
         residual = x + scatter_exp_rel(keep[None], away[None], low_bits)[0][0]

time: 573 us -> 571 us (level)
  starting transfers between devices: 130 us -> 136 us
    all_to_all x3, waiting for transfers between devices: 64.1 us -> 50.1 us  [gather_ctx(): lax.all_to_all(jnp.broadcast_to(x[None], (nc,) + x.shape), 'ctx', 0, 0, t...]
    all_to_all x3, starting transfers between devices: 13.1 us -> 22.5 us  [gather_ctx(): lax.all_to_all(jnp.broadcast_to(x[None], (nc,) + x.shape), 'ctx', 0, 0, t...]
    ppermute x38, waiting for transfers between devices: 129 us -> 139 us  [send(): return lax.ppermute(x, AXES, pairs)]
  transfers between devices with their start and end apart: 50 -> 50, of which waited for: 25 -> 24; matrix products, arithmetic and copies ran while one was open for 14% -> 14% of each run, Pallas kernels for 14% -> 14%
where the time goes in v5:
time: 571 us; the launch traced here: 565 us
  waiting for transfers between devices  250 us (44%)
  starting transfers between devices  136 us (24%)
  Pallas kernels  81.3 us (14%)
  local copies, waits for them, and re-layouts  46.4 us (8%)
  other arithmetic  46 us (8%)
    ppermute x38, waiting for transfers between devices, send(): return lax.ppermute(x, AXES, pairs)  139 us
    pallas_call x4, Pallas kernels, vmem_call(): pl.pallas_call(kernel, in_specs=[pl.BlockSpec(memory_space=pltpu.SMEM)] +...  81.3 us
    all_to_all x3, waiting for transfers between devices, gather_ctx(): lax.all_to_all(jnp.broadcast_to(x[None], (nc,) + x.shape), 'ctx', 0, 0, t...  50.1 us
    ppermute x38, starting transfers between devices, send(): return lax.ppermute(x, AXES, pairs)  41.8 us
    all_to_all x3, waiting for transfers between devices, scatter_ctx(): parts = lax.all_to_all(parts.astype(BF16), 'ctx', 0, 0, tiled=True)  30 us
    all_to_all x1, starting transfers between devices, per_device(): small = lax.all_to_all(small, AXES, 0, 0, tiled=True)  26.7 us
    all_to_all x3, starting transfers between devices, gather_ctx(): lax.all_to_all(jnp.broadcast_to(x[None], (nc,) + x.shape), 'ctx', 0, 0, t...  22.5 us
    all_to_all x3, starting transfers between devices, scatter_ctx(): parts = lax.all_to_all(parts.astype(BF16), 'ctx', 0, 0, tiled=True)  18 us
  transfers between devices with their start and end apart: 50, of which 24 were waited for; matrix products, arithmetic and copies ran while one was open for 14% of the time, Pallas kernels for 14%

profile of v5, /device:TPU:4, one launch (start us, length us, event | category | flops | bytes accessed | tf_op | source)
XLA Modules:
  0.0 565.0 jit_solution(14613030192444260349)
XLA Ops:
  2.2 3.4 collective-permute-start
  9.2 5.0 all-to-all-start.1
  14.2 2.7 collective-permute-start.4
  19.2 7.9 %collective-permute-done.4 = bf16[32,1024]{1,0:T(8,128)(2,1)S(1)} collective-permute-done((bf16[32,1024]{1,0:T(8,128)(2,1)S(1)}, bf16[32,1024]{1,0:T(8,128)(2,1)S(1)}, u32[]{:S(2)}, u32[]{:S(2)}) %collective-permute-start.4) | collective-permute-done | bytes 65568 | tf_op jit(solution)/shard_map/ppermute | solution.py:407
  27.3 5.0 all-to-all-start
  32.4 5.8 %all-to-all-done = bf16[32,2,128]{2,1,0:T(2,128)(2,1)S(1)} async-done(((bf16[32,2,128]{2,1,0:T(2,128)(2,1)}), bf16[32,2,128]{2,1,0:T(2,128)(2,1)S(1)}, u32[]{:S(2)}, u32[]{:S(2)}) %all-to-all-start) | async-done | bytes 16416 | tf_op jit(solution)/shard_map/all_to_all | solution.py:560
  39.3 3.7 all-to-all-start.2
  46.3 22.7 %all-to-all-done.2.refs_4_.refs_8_ = bf16[4,128,1024]{2,1,0:T(8,128)(2,1)S(1)} async-done(((bf16[4,128,1024]{2,1,0:T(8,128)(2,1)}), bf16[4,128,1024]{2,1,0:T(8,128)(2,1)S(1)}, u32[]{:S(2)}, u32[]{:S(2)}) %all-to-all-start.2) | async-done | bytes 1048608 | tf_op jit(solution)/shard_map/all_to_all | solution.py:487
  80.0 4.5 all-to-all-start.3
  84.5 8.8 %collective-permute-done.6.refs_5_.refs_9_ = bf16[4,128,1024]{2,1,0:T(8,128)(2,1)} collective-permute-done((bf16[4,128,1024]{2,1,0:T(8,128)(2,1)S(1)}, bf16[4,128,1024]{2,1,0:T(8,128)(2,1)}, u32[]{:S(2)}, u32[]{:S(2)}) %collective-permute-start.6) | collective-permute-done | bytes 1048608 | tf_op jit(solution)/shard_map/ppermute | solution.py:407
  93.8 13.3 %shard_map.255 = (bf16[1024,768]{1,0:T(8,128)(2,1)}, bf16[1024,256]{1,0:T(8,128)(2,1)}, bf16[2,256,1024]{2,1,0:T(8,128)(2,1)}, bf16[2,256,1024]{2,1,0:T(8,128)(2,1)}) custom-call(s32[2]{0:T(128)} %pad_add_fusion.where_ref, bf16[256,1024]{1,0:T(8,128)(2,1)} %fusion.10.refs_0_.refs_4_, bf16[256,1024]{1,0:T(8,128)(2,1)} %collective-permute-done.1.refs_1_.refs_5_, ...), custom_call_target="tpu_custom_call" | custom-call | flops 42949672960 | bytes 8396800 | tf_op jit(solution)/shard_map/pallas_call | solution.py:208
  110.4 12.0 %collective-permute-done.23 = bf16[1,2,72,1024]{3,2,1,0:T(8,128)(2,1)S(1)} collective-permute-done((bf16[1,2,72,1024]{3,2,1,0:T(8,128)(2,1)S(1)}, bf16[1,2,72,1024]{3,2,1,0:T(8,128)(2,1)S(1)}, u32[]{:S(2)}, u32[]{:S(2)}) %collective-permute-start.23) | collective-permute-done | bytes 294944 | tf_op jit(solution)/shard_map/ppermute | solution.py:407
  124.2 15.1 %all-to-all-done.3.refs_8_ = bf16[4,256,1024]{2,1,0:T(8,128)(2,1)} async-done(((bf16[4,256,1024]{2,1,0:T(8,128)(2,1)}), bf16[4,256,1024]{2,1,0:T(8,128)(2,1)}, u32[]{:S(2)}, u32[]{:S(2)}) %all-to-all-start.3) | async-done | bytes 2097184 | tf_op jit(solution)/shard_map/all_to_all | solution.py:487
  141.1 14.4 %all-to-all-start.5 = ((bf16[4,4,72,1024]{3,2,1,0:T(8,128)(2,1)}), bf16[4,4,72,1024]{3,2,1,0:T(8,128)(2,1)}, u32[]{:S(2)}, u32[]{:S(2)}) async-start(bf16[4,4,72,1024]{3,2,1,0:T(8,128)(2,1)} %broadcast_in_dim.44), calls=%async_computation.5 | async-start | bytes 4718592 | tf_op jit(solution)/shard_map/all_to_all | solution.py:487
  159.4 11.0 %collective-permute-done.14.refs_6_ = bf16[256,1024]{1,0:T(8,128)(2,1)} collective-permute-done((bf16[256,1024]{1,0:T(8,128)(2,1)S(1)}, bf16[256,1024]{1,0:T(8,128)(2,1)}, u32[]{:S(2)}, u32[]{:S(2)}) %collective-permute-start.14) | collective-permute-done | bytes 524320 | tf_op jit(solution)/shard_map/ppermute | solution.py:407
  172.0 8.3 %collective-permute-done.10 = bf16[1,1,256,1024]{3,2,1,0:T(8,128)(2,1)S(1)} collective-permute-done((bf16[1,1,256,1024]{3,2,1,0:T(8,128)(2,1)S(1)}, bf16[1,1,256,1024]{3,2,1,0:T(8,128)(2,1)S(1)}, u32[]{:S(2)}, u32[]{:S(2)}) %collective-permute-start.10) | collective-permute-done | bytes 524320 | tf_op jit(solution)/shard_map/ppermute | solution.py:407
  182.8 12.5 %collective-permute-done.17.refs_2_ = bf16[256,1024]{1,0:T(8,128)(2,1)S(1)} collective-permute-done((bf16[256,1024]{1,0:T(8,128)(2,1)S(1)}, bf16[256,1024]{1,0:T(8,128)(2,1)S(1)}, u32[]{:S(2)}, u32[]{:S(2)}) %collective-permute-start.17) | collective-permute-done | bytes 524320 | tf_op jit(solution)/shard_map/ppermute | solution.py:407
  196.8 12.4 %all-to-all-done.5 = bf16[4,4,72,1024]{3,2,1,0:T(8,128)(2,1)} async-done(((bf16[4,4,72,1024]{3,2,1,0:T(8,128)(2,1)}), bf16[4,4,72,1024]{3,2,1,0:T(8,128)(2,1)}, u32[]{:S(2)}, u32[]{:S(2)}) %all-to-all-start.5) | async-done | bytes 2359328 | tf_op jit(solution)/shard_map/all_to_all | solution.py:487
  211.0 4.2 all-to-all-start.4
  215.2 3.8 collective-permute-done.19.refs_9_
  219.0 19.3 %shard_map.256 = (bf16[2,2,256,1024]{3,2,1,0:T(8,128)(2,1)}, bf16[2,2,256,1024]{3,2,1,0:T(8,128)(2,1)}, bf16[4,256,1024]{2,1,0:T(8,128)(2,1)}, bf16[4,256,1024]{2,1,0:T(8,128)(2,1)}) custom-call(s32[2]{0:T(128)} %pad_add_fusion.where_ref, bf16[256,1024]{1,0:T(8,128)(2,1)} %copy-done.11, bf16[256,1024]{1,0:T(8,128)(2,1)} %collective-permute-done.16.refs_1_, ...), custom_call_target="tpu_custom_call" | custom-call | flops 128849018880 | bytes 16777216 | tf_op jit(solution)/shard_map/pallas_call | solution.py:208
  238.2 3.1 copy.123
  248.9 2.5 add_bitcast_fusion
  254.5 8.1 %all-to-all-done.4 = bf16[16,72,1024]{2,1,0:T(8,128)(2,1)S(1)} async-done(((bf16[16,72,1024]{2,1,0:T(8,128)(2,1)}), bf16[16,72,1024]{2,1,0:T(8,128)(2,1)S(1)}, u32[]{:S(2)}, u32[]{:S(2)}) %all-to-all-start.4) | async-done | bytes 2359328 | tf_op jit(solution)/shard_map/all_to_all | solution.py:550
  264.1 25.2 %shard_map.257 = (bf16[1152,1024]{1,0:T(8,128)(2,1)}, bf16[1152,1024]{1,0:T(8,128)(2,1)}, bf16[1024,512]{1,0:T(8,128)(2,1)}, bf16[1024,512]{1,0:T(8,128)(2,1)}, ...) custom-call(s32[2]{0:T(128)} %pad_add_fusion.where_ref, bf16[1152,1024]{1,0:T(8,128)(2,1)} %bitcast.190, ...), custom_call_target="tpu_custom_call" | custom-call | flops 144955146240 | bytes 18612736 | tf_op jit(solution)/shard_map/pallas_call | solution.py:208
  291.6 8.5 %all-to-all-start.6 = ((bf16[16,72,1024]{2,1,0:T(8,128)(2,1)}), bf16[16,72,1024]{2,1,0:T(8,128)(2,1)S(1)}, u32[]{:S(2)}, u32[]{:S(2)}) async-start(bf16[16,72,1024]{2,1,0:T(8,128)(2,1)} %bitcast.191), calls=%async_computation.6 | async-start | bytes 4718592 | tf_op jit(solution)/shard_map/all_to_all | solution.py:554
  302.1 4.5 add_convert_fusion
  306.7 19.7 %collective-permute-done.25 = bf16[1024,512]{1,0:T(8,128)(2,1)S(1)} collective-permute-done((bf16[1024,512]{1,0:T(8,128)(2,1)}, bf16[1024,512]{1,0:T(8,128)(2,1)S(1)}, u32[]{:S(2)}, u32[]{:S(2)}) %collective-permute-start.25) | collective-permute-done | bytes 1048608 | tf_op jit(solution)/shard_map/ppermute | solution.py:407
  327.3 20.8 %collective-permute-done.26 = bf16[512,1024]{1,0:T(8,128)(2,1)} collective-permute-done((bf16[512,1024]{1,0:T(8,128)(2,1)S(1)}, bf16[512,1024]{1,0:T(8,128)(2,1)}, u32[]{:S(2)}, u32[]{:S(2)}) %collective-permute-start.26) | collective-permute-done | bytes 1048608 | tf_op jit(solution)/shard_map/ppermute | solution.py:407
  348.1 8.5 %all-to-all-start.7 = ((bf16[4,256,1024]{2,1,0:T(8,128)(2,1)}), bf16[4,256,1024]{2,1,0:T(8,128)(2,1)}, u32[]{:S(2)}, u32[]{:S(2)}) async-start(bf16[4,256,1024]{2,1,0:T(8,128)(2,1)} %add_convert_fusion), calls=%async_computation.7 | async-start | bytes 4194304 | tf_op jit(solution)/shard_map/all_to_all | solution.py:492
  362.8 12.9 %collective-permute-done.31.refs_2_ = bf16[256,1024]{1,0:T(8,128)(2,1)} collective-permute-done((bf16[256,1024]{1,0:T(8,128)(2,1)S(1)}, bf16[256,1024]{1,0:T(8,128)(2,1)}, u32[]{:S(2)}, u32[]{:S(2)}) %collective-permute-start.31) | collective-permute-done | bytes 524320 | tf_op jit(solution)/shard_map/ppermute | solution.py:407
  375.8 29.5 %all-to-all-done.7 = bf16[4,256,1024]{2,1,0:T(8,128)(2,1)} async-done(((bf16[4,256,1024]{2,1,0:T(8,128)(2,1)}), bf16[4,256,1024]{2,1,0:T(8,128)(2,1)}, u32[]{:S(2)}, u32[]{:S(2)}) %all-to-all-start.7) | async-done | bytes 2097184 | tf_op jit(solution)/shard_map/all_to_all | solution.py:492
  407.4 4.9 all-to-all-start.8
  412.4 23.5 %shard_map.258 = (bf16[2,256,1024]{2,1,0:T(8,128)(2,1)}, bf16[2,256,1024]{2,1,0:T(8,128)(2,1)}, bf16[4,128,1024]{2,1,0:T(8,128)(2,1)}, bf16[4,128,1024]{2,1,0:T(8,128)(2,1)}) custom-call(s32[2]{0:T(128)} %pad_add_fusion.where_ref, bf16[256,1024]{1,0:T(8,128)(2,1)} %copy-done.29, bf16[256,1024]{1,0:T(8,128)(2,1)} %collective-permute-done.30.refs_1_, ...), custom_call_target="tpu_custom_call" | custom-call | flops 96636764160 | bytes 12591104 | tf_op jit(solution)/shard_map/pallas_call | solution.py:208
  437.8 3.3 add_bitcast_fusion.2
  443.5 2.9 add_bitcast_fusion.1
  450.1 12.1 %collective-permute-done.36 = bf16[4,128,1024]{2,1,0:T(8,128)(2,1)} collective-permute-done((bf16[4,128,1024]{2,1,0:T(8,128)(2,1)}, bf16[4,128,1024]{2,1,0:T(8,128)(2,1)}, u32[]{:S(2)}, u32[]{:S(2)}) %collective-permute-start.36) | collective-permute-done | bytes 1048608 | tf_op jit(solution)/shard_map/ppermute | solution.py:407
  462.2 2.6 add_convert_fusion.1
  465.8 3.1 reduce_sum.186
  468.9 4.6 all-to-all-start.9
  478.8 2.7 concatenate.68
  485.4 2.6 fusion.15
  488.0 5.2 collective-permute-start.35
  495.1 5.4 collective-permute-start.29
  501.3 26.7 %all-to-all-start.11 = ((f32[32,1,256]{2,1,0:T(1,128)}), f32[32,1,256]{2,1,0:T(1,128)S(1)}, u32[]{:S(2)}, u32[]{:S(2)}) async-start(f32[32,1,256]{2,1,0:T(1,128)} %copy.135), calls=%async_computation.11 | async-start | bytes 65536 | tf_op jit(solution)/shard_map/all_to_all | solution.py:667
  528.8 17.4 %all-to-all-done.11 = f32[32,1,256]{2,1,0:T(1,128)S(1)} async-done(((f32[32,1,256]{2,1,0:T(1,128)}), f32[32,1,256]{2,1,0:T(1,128)S(1)}, u32[]{:S(2)}, u32[]{:S(2)}) %all-to-all-start.11) | async-done | bytes 32800 | tf_op jit(solution)/shard_map/all_to_all | solution.py:667
  546.2 4.0 all-to-all-start.10
  556.0 4.4 collective-permute-done.37
  (304 shorter events, 99.0 us)
Async XLA Ops:
  0.6 31.8 %collective-permute-start.5 = (bf16[1024,512]{1,0:T(8,128)(2,1)}, bf16[1024,512]{1,0:T(8,128)(2,1)S(1)}, u32[]{:S(2)}, u32[]{:S(2)}) collective-permute-start(bf16[1024,512]{1,0:T(8,128)(2,1)} %bitcast.233), channel_id=1, source_target_pairs={{0,16},{1,17},{2,18},{3,19},{4,20},{5,21},{6,22},{7,23},{8,24},{9,... | collective-permute-start | bytes 3145736 | tf_op jit(solution)/shard_map/ppermute | solution.py:407
  2.2 30.2 %collective-permute-start = (bf16[256,1024]{1,0:T(8,128)(2,1)}, bf16[256,1024]{1,0:T(8,128)(2,1)S(1)}, u32[]{:S(2)}, u32[]{:S(2)}) collective-permute-start(bf16[256,1024]{1,0:T(8,128)(2,1)} %bitcast.239), channel_id=1, source_target_pairs={{0,0},{1,8},{2,4},{3,12},{4,1},{5,9},{6,5},{7,13},{8,2},{9,10},{10... | collective-permute-start | bytes 1572872 | tf_op jit(solution)/shard_map/ppermute | solution.py:407
  9.2 18.1 %all-to-all-start.1 = ((bf16[4,32,1792]{2,1,0:T(8,128)(2,1)}), bf16[4,32,1792]{2,1,0:T(8,128)(2,1)S(1)}, u32[]{:S(2)}, u32[]{:S(2)}) async-start(bf16[4,32,1792]{2,1,0:T(8,128)(2,1)} %pad_maximum_fusion.2), calls=%async_computation.1 | async-start | bytes 917504 | tf_op jit(solution)/shard_map/all_to_all | solution.py:569
  14.2 12.8 %collective-permute-start.4 = (bf16[32,1024]{1,0:T(8,128)(2,1)S(1)}, bf16[32,1024]{1,0:T(8,128)(2,1)S(1)}, u32[]{:S(2)}, u32[]{:S(2)}) collective-permute-start(bf16[32,1024]{1,0:T(8,128)(2,1)S(1)} %copy-done.62), channel_id=1, source_target_pairs={{0,0},{1,4},{2,8},{3,12},{4,16},{5,20},{6,24},{7,28},{8,1},{9,5},{... | collective-permute-start | bytes 196616 | tf_op jit(solution)/shard_map/ppermute | solution.py:407
  27.3 10.9 %all-to-all-start = ((bf16[32,2,128]{2,1,0:T(2,128)(2,1)}), bf16[32,2,128]{2,1,0:T(2,128)(2,1)S(1)}, u32[]{:S(2)}, u32[]{:S(2)}) async-start(bf16[32,2,128]{2,1,0:T(2,128)(2,1)} %reshape.514), calls=%async_computation | async-start | bytes 32768 | tf_op jit(solution)/shard_map/all_to_all | solution.py:560
  39.3 29.7 %all-to-all-start.2 = ((bf16[4,128,1024]{2,1,0:T(8,128)(2,1)}), bf16[4,128,1024]{2,1,0:T(8,128)(2,1)S(1)}, u32[]{:S(2)}, u32[]{:S(2)}) async-start(bf16[4,128,1024]{2,1,0:T(8,128)(2,1)} %broadcast_in_dim.36), calls=%async_computation.2 | async-start | bytes 2097152 | tf_op jit(solution)/shard_map/all_to_all | solution.py:487
  44.8 29.6 %collective-permute-start.2 = (bf16[256,1024]{1,0:T(8,128)(2,1)}, bf16[256,1024]{1,0:T(8,128)(2,1)}, u32[]{:S(2)}, u32[]{:S(2)}) collective-permute-start(bf16[256,1024]{1,0:T(8,128)(2,1)} %fusion.10.refs_0_.refs_4_), channel_id=1, source_target_pairs={{0,2},{1,3},{2,0},{3,1},{4,6},{5,7},{6,4},{7,5},{8,10},{9,11},{10,... | collective-permute-start | bytes 1572872 | tf_op jit(solution)/shard_map/ppermute | solution.py:407
  69.0 24.3 %collective-permute-start.6 = (bf16[4,128,1024]{2,1,0:T(8,128)(2,1)S(1)}, bf16[4,128,1024]{2,1,0:T(8,128)(2,1)}, u32[]{:S(2)}, u32[]{:S(2)}) collective-permute-start(bf16[4,128,1024]{2,1,0:T(8,128)(2,1)S(1)} %all-to-all-done.2.refs_4_.refs_8_), channel_id=1, source_target_pairs={{0,16},{1,17},{2,18},{3,19},{4,20},{5,21},{6,22},{7,23},{8,24},{9,... | collective-permute-start | bytes 3145736 | tf_op jit(solution)/shard_map/ppermute | solution.py:407
  69.8 7.4 %collective-permute-start.7 = (s32[12,128]{1,0:T(8,128)S(1)}, s32[12,128]{1,0:T(8,128)S(1)}, u32[]{:S(2)}, u32[]{:S(2)}) collective-permute-start(s32[12,128]{1,0:T(8,128)S(1)} %add_bitcast_fusion.3), channel_id=1, source_target_pairs={{0,0},{1,8},{2,4},{3,12},{4,1},{5,9},{6,5},{7,13},{8,2},{9,10},{10... | collective-permute-start | bytes 18440 | tf_op jit(solution)/shard_map/ppermute | solution.py:407
  71.7 38.1 %collective-permute-start.11 = (bf16[256,1024]{1,0:T(8,128)(2,1)S(1)}, bf16[256,1024]{1,0:T(8,128)(2,1)}, u32[]{:S(2)}, u32[]{:S(2)}) collective-permute-start(bf16[256,1024]{1,0:T(8,128)(2,1)S(1)} %bitcast.209), channel_id=1, source_target_pairs={{0,2},{1,3},{2,0},{3,1},{4,6},{5,7},{6,4},{7,5},{8,10},{9,11},{10,... | collective-permute-start | bytes 1572872 | tf_op jit(solution)/shard_map/ppermute | solution.py:407
  72.0 21.8 %collective-permute-start.1 = (bf16[256,1024]{1,0:T(8,128)(2,1)}, bf16[256,1024]{1,0:T(8,128)(2,1)}, u32[]{:S(2)}, u32[]{:S(2)}) collective-permute-start(bf16[256,1024]{1,0:T(8,128)(2,1)} %fusion.10.refs_0_.refs_4_), channel_id=1, source_target_pairs={{0,1},{1,0},{2,3},{3,2},{4,5},{5,4},{6,7},{7,6},{8,9},{9,8},{10,11... | collective-permute-start | bytes 1572872 | tf_op jit(solution)/shard_map/ppermute | solution.py:407
  74.4 19.5 %collective-permute-start.3 = (bf16[256,1024]{1,0:T(8,128)(2,1)}, bf16[256,1024]{1,0:T(8,128)(2,1)}, u32[]{:S(2)}, u32[]{:S(2)}) collective-permute-start(bf16[256,1024]{1,0:T(8,128)(2,1)} %collective-permute-done.2.refs_2_.refs_6_), channel_id=1, source_target_pairs={{0,1},{1,0},{2,3},{3,2},{4,5},{5,4},{6,7},{7,6},{8,9},{9,8},{10,11... | collective-permute-start | bytes 1572872 | tf_op jit(solution)/shard_map/ppermute | solution.py:407
  77.2 29.8 %collective-permute-start.22 = (bf16[2,1,72,1024]{3,2,0,1:T(8,128)(2,1)S(1)}, bf16[2,1,72,1024]{3,2,0,1:T(8,128)(2,1)}, u32[]{:S(2)}, u32[]{:S(2)}) collective-permute-start(bf16[2,1,72,1024]{3,2,0,1:T(8,128)(2,1)S(1)} %get-tuple-element.167), channel_id=1, source_target_pairs={{0,1},{1,0},{2,3},{3,2},{4,5},{5,4},{6,7},{7,6},{8,9},{9,8},{10,11... | collective-permute-start | bytes 884744 | tf_op jit(solution)/shard_map/ppermute | solution.py:407
  80.0 59.3 %all-to-all-start.3 = ((bf16[4,256,1024]{2,1,0:T(8,128)(2,1)}), bf16[4,256,1024]{2,1,0:T(8,128)(2,1)}, u32[]{:S(2)}, u32[]{:S(2)}) async-start(bf16[4,256,1024]{2,1,0:T(8,128)(2,1)} %broadcast_in_dim.40), calls=%async_computation.3 | async-start | bytes 4194304 | tf_op jit(solution)/shard_map/all_to_all | solution.py:487
  93.2 31.0 %collective-permute-start.8 = (bf16[512,1024]{1,0:T(8,128)(2,1)}, bf16[512,1024]{1,0:T(8,128)(2,1)}, u32[]{:S(2)}, u32[]{:S(2)}) collective-permute-start(bf16[512,1024]{1,0:T(8,128)(2,1)} %bitcast.235), channel_id=1, source_target_pairs={{0,16},{1,17},{2,18},{3,19},{4,20},{5,21},{6,22},{7,23},{8,24},{9,... | collective-permute-start | bytes 3145736 | tf_op jit(solution)/shard_map/ppermute | solution.py:407
  107.1 48.5 %collective-permute-start.9 = (bf16[1,2,256,1024]{3,2,1,0:T(8,128)(2,1)}, bf16[1,2,256,1024]{3,2,1,0:T(8,128)(2,1)S(1)}, u32[]{:S(2)}, u32[]{:S(2)}) collective-permute-start(bf16[1,2,256,1024]{3,2,1,0:T(8,128)(2,1)} %bitcast.237), channel_id=1, source_target_pairs={{0,1},{1,0},{2,3},{3,2},{4,5},{5,4},{6,7},{7,6},{8,9},{9,8},{10,11... | collective-permute-start | bytes 3145736 | tf_op jit(solution)/shard_map/ppermute | solution.py:407
  108.3 14.1 %collective-permute-start.23 = (bf16[1,2,72,1024]{3,2,1,0:T(8,128)(2,1)S(1)}, bf16[1,2,72,1024]{3,2,1,0:T(8,128)(2,1)S(1)}, u32[]{:S(2)}, u32[]{:S(2)}) collective-permute-start(bf16[1,2,72,1024]{3,2,1,0:T(8,128)(2,1)S(1)} %get-tuple-element.165), channel_id=1, source_target_pairs={{0,2},{1,3},{2,0},{3,1},{4,6},{5,7},{6,4},{7,5},{8,10},{9,11},{10,... | collective-permute-start | bytes 884744 | tf_op jit(solution)/shard_map/ppermute | solution.py:407
  109.8 45.6 %collective-permute-start.12 = (bf16[256,1024]{1,0:T(8,128)(2,1)}, bf16[256,1024]{1,0:T(8,128)(2,1)S(1)}, u32[]{:S(2)}, u32[]{:S(2)}) collective-permute-start(bf16[256,1024]{1,0:T(8,128)(2,1)} %collective-permute-done.11), channel_id=1, source_target_pairs={{0,4},{1,12},{2,0},{3,8},{4,5},{5,13},{6,1},{7,9},{8,6},{9,14},{10... | collective-permute-start | bytes 1572872 | tf_op jit(solution)/shard_map/ppermute | solution.py:407
  141.1 68.1 %all-to-all-start.5 = ((bf16[4,4,72,1024]{3,2,1,0:T(8,128)(2,1)}), bf16[4,4,72,1024]{3,2,1,0:T(8,128)(2,1)}, u32[]{:S(2)}, u32[]{:S(2)}) async-start(bf16[4,4,72,1024]{3,2,1,0:T(8,128)(2,1)} %broadcast_in_dim.44), calls=%async_computation.5 | async-start | bytes 4718592 | tf_op jit(solution)/shard_map/all_to_all | solution.py:487
  155.4 15.0 %collective-permute-start.14 = (bf16[256,1024]{1,0:T(8,128)(2,1)S(1)}, bf16[256,1024]{1,0:T(8,128)(2,1)}, u32[]{:S(2)}, u32[]{:S(2)}) collective-permute-start(bf16[256,1024]{1,0:T(8,128)(2,1)S(1)} %collective-permute-done.12.refs_4_), channel_id=1, source_target_pairs={{0,2},{1,3},{2,0},{3,1},{4,6},{5,7},{6,4},{7,5},{8,10},{9,11},{10,... | collective-permute-start | bytes 1572872 | tf_op jit(solution)/shard_map/ppermute | solution.py:407
  157.3 23.0 %collective-permute-start.10 = (bf16[1,1,256,1024]{3,2,1,0:T(8,128)(2,1)S(1)}, bf16[1,1,256,1024]{3,2,1,0:T(8,128)(2,1)S(1)}, u32[]{:S(2)}, u32[]{:S(2)}) collective-permute-start(bf16[1,1,256,1024]{3,2,1,0:T(8,128)(2,1)S(1)} %fusion.27), channel_id=1, source_target_pairs={{0,2},{1,3},{2,0},{3,1},{4,6},{5,7},{6,4},{7,5},{8,10},{9,11},{10,... | collective-permute-start | bytes 1572872 | tf_op jit(solution)/shard_map/ppermute | solution.py:407
  159.4 22.4 %collective-permute-start.13 = (bf16[256,1024]{1,0:T(8,128)(2,1)S(1)}, bf16[256,1024]{1,0:T(8,128)(2,1)S(1)}, u32[]{:S(2)}, u32[]{:S(2)}) collective-permute-start(bf16[256,1024]{1,0:T(8,128)(2,1)S(1)} %collective-permute-done.12.refs_4_), channel_id=1, source_target_pairs={{0,1},{1,0},{2,3},{3,2},{4,5},{5,4},{6,7},{7,6},{8,9},{9,8},{10,11... | collective-permute-start | bytes 1572872 | tf_op jit(solution)/shard_map/ppermute | solution.py:407
  170.4 11.3 %collective-permute-start.15 = (bf16[256,1024]{1,0:T(8,128)(2,1)}, bf16[256,1024]{1,0:T(8,128)(2,1)}, u32[]{:S(2)}, u32[]{:S(2)}) collective-permute-start(bf16[256,1024]{1,0:T(8,128)(2,1)} %collective-permute-done.14.refs_6_), channel_id=1, source_target_pairs={{0,1},{1,0},{2,3},{3,2},{4,5},{5,4},{6,7},{7,6},{8,9},{9,8},{10,11... | collective-permute-start | bytes 1572872 | tf_op jit(solution)/shard_map/ppermute | solution.py:407
  170.6 48.4 %collective-permute-start.19 = (bf16[4,256,1024]{2,1,0:T(8,128)(2,1)}, bf16[4,256,1024]{2,1,0:T(8,128)(2,1)}, u32[]{:S(2)}, u32[]{:S(2)}) collective-permute-start(bf16[4,256,1024]{2,1,0:T(8,128)(2,1)} %all-to-all-done.3.refs_8_), channel_id=1, source_target_pairs={{0,16},{1,17},{2,18},{3,19},{4,20},{5,21},{6,22},{7,23},{8,24},{9,... | collective-permute-start | bytes 6291464 | tf_op jit(solution)/shard_map/ppermute | solution.py:407
  182.5 12.8 %collective-permute-start.17 = (bf16[256,1024]{1,0:T(8,128)(2,1)S(1)}, bf16[256,1024]{1,0:T(8,128)(2,1)S(1)}, u32[]{:S(2)}, u32[]{:S(2)}) collective-permute-start(bf16[256,1024]{1,0:T(8,128)(2,1)S(1)} %add_convert_fusion.2.refs_0_), channel_id=1, source_target_pairs={{0,2},{1,3},{2,0},{3,1},{4,6},{5,7},{6,4},{7,5},{8,10},{9,11},{10,... | collective-permute-start | bytes 1572872 | tf_op jit(solution)/shard_map/ppermute | solution.py:407
  182.8 32.3 %collective-permute-start.16 = (bf16[256,1024]{1,0:T(8,128)(2,1)S(1)}, bf16[256,1024]{1,0:T(8,128)(2,1)}, u32[]{:S(2)}, u32[]{:S(2)}) collective-permute-start(bf16[256,1024]{1,0:T(8,128)(2,1)S(1)} %add_convert_fusion.2.refs_0_), channel_id=1, source_target_pairs={{0,1},{1,0},{2,3},{3,2},{4,5},{5,4},{6,7},{7,6},{8,9},{9,8},{10,11... | collective-permute-start | bytes 1572872 | tf_op jit(solution)/shard_map/ppermute | solution.py:407
  195.3 19.8 %collective-permute-start.18 = (bf16[256,1024]{1,0:T(8,128)(2,1)S(1)}, bf16[256,1024]{1,0:T(8,128)(2,1)}, u32[]{:S(2)}, u32[]{:S(2)}) collective-permute-start(bf16[256,1024]{1,0:T(8,128)(2,1)S(1)} %collective-permute-done.17.refs_2_), channel_id=1, source_target_pairs={{0,1},{1,0},{2,3},{3,2},{4,5},{5,4},{6,7},{7,6},{8,9},{9,8},{10,11... | collective-permute-start | bytes 1572872 | tf_op jit(solution)/shard_map/ppermute | solution.py:407
  211.0 51.7 %all-to-all-start.4 = ((bf16[16,72,1024]{2,1,0:T(8,128)(2,1)}), bf16[16,72,1024]{2,1,0:T(8,128)(2,1)S(1)}, u32[]{:S(2)}, u32[]{:S(2)}) async-start(bf16[16,72,1024]{2,1,0:T(8,128)(2,1)} %bitcast.31), calls=%async_computation.4 | async-start | bytes 4718592 | tf_op jit(solution)/shard_map/all_to_all | solution.py:550
  243.2 48.4 %collective-permute-start.24 = (bf16[4,256,1024]{2,1,0:T(8,128)(2,1)}, bf16[4,256,1024]{2,1,0:T(8,128)(2,1)}, u32[]{:S(2)}, u32[]{:S(2)}) collective-permute-start(bf16[4,256,1024]{2,1,0:T(8,128)(2,1)} %get-tuple-element.58), channel_id=1, source_target_pairs={{0,16},{1,17},{2,18},{3,19},{4,20},{5,21},{6,22},{7,23},{8,24},{9,... | collective-permute-start | bytes 6291464 | tf_op jit(solution)/shard_map/ppermute | solution.py:407
  254.5 37.0 %collective-permute-start.21 = (bf16[2,1,256,1024]{3,2,1,0:T(8,128)(2,1)}, bf16[2,1,256,1024]{3,2,1,0:T(8,128)(2,1)}, u32[]{:S(2)}, u32[]{:S(2)}) collective-permute-start(bf16[2,1,256,1024]{3,2,1,0:T(8,128)(2,1)} %fusion.18), channel_id=1, source_target_pairs={{0,2},{1,3},{2,0},{3,1},{4,6},{5,7},{6,4},{7,5},{8,10},{9,11},{10,... | collective-permute-start | bytes 3145736 | tf_op jit(solution)/shard_map/ppermute | solution.py:407
  291.6 56.5 %all-to-all-start.6 = ((bf16[16,72,1024]{2,1,0:T(8,128)(2,1)}), bf16[16,72,1024]{2,1,0:T(8,128)(2,1)S(1)}, u32[]{:S(2)}, u32[]{:S(2)}) async-start(bf16[16,72,1024]{2,1,0:T(8,128)(2,1)} %bitcast.191), calls=%async_computation.6 | async-start | bytes 4718592 | tf_op jit(solution)/shard_map/all_to_all | solution.py:554
  300.1 26.2 %collective-permute-start.25 = (bf16[1024,512]{1,0:T(8,128)(2,1)}, bf16[1024,512]{1,0:T(8,128)(2,1)S(1)}, u32[]{:S(2)}, u32[]{:S(2)}) collective-permute-start(bf16[1024,512]{1,0:T(8,128)(2,1)} %get-tuple-element.61), channel_id=1, source_target_pairs={{0,16},{1,17},{2,18},{3,19},{4,20},{5,21},{6,22},{7,23},{8,24},{9,... | collective-permute-start | bytes 3145736 | tf_op jit(solution)/shard_map/ppermute | solution.py:407
  301.5 46.6 %collective-permute-start.26 = (bf16[512,1024]{1,0:T(8,128)(2,1)S(1)}, bf16[512,1024]{1,0:T(8,128)(2,1)}, u32[]{:S(2)}, u32[]{:S(2)}) collective-permute-start(bf16[512,1024]{1,0:T(8,128)(2,1)S(1)} %copy-done.59), channel_id=1, source_target_pairs={{0,16},{1,17},{2,18},{3,19},{4,20},{5,21},{6,22},{7,23},{8,24},{9,... | collective-permute-start | bytes 3145736 | tf_op jit(solution)/shard_map/ppermute | solution.py:407
  348.1 57.2 %all-to-all-start.7 = ((bf16[4,256,1024]{2,1,0:T(8,128)(2,1)}), bf16[4,256,1024]{2,1,0:T(8,128)(2,1)}, u32[]{:S(2)}, u32[]{:S(2)}) async-start(bf16[4,256,1024]{2,1,0:T(8,128)(2,1)} %add_convert_fusion), calls=%async_computation.7 | async-start | bytes 4194304 | tf_op jit(solution)/shard_map/all_to_all | solution.py:492
  361.8 14.0 %collective-permute-start.31 = (bf16[256,1024]{1,0:T(8,128)(2,1)S(1)}, bf16[256,1024]{1,0:T(8,128)(2,1)}, u32[]{:S(2)}, u32[]{:S(2)}) collective-permute-start(bf16[256,1024]{1,0:T(8,128)(2,1)S(1)} %get-tuple-element.65.refs_0_), channel_id=1, source_target_pairs={{0,2},{1,3},{2,0},{3,1},{4,6},{5,7},{6,4},{7,5},{8,10},{9,11},{10,... | collective-permute-start | bytes 1572872 | tf_op jit(solution)/shard_map/ppermute | solution.py:407
  362.8 49.5 %collective-permute-start.30 = (bf16[256,1024]{1,0:T(8,128)(2,1)S(1)}, bf16[256,1024]{1,0:T(8,128)(2,1)}, u32[]{:S(2)}, u32[]{:S(2)}) collective-permute-start(bf16[256,1024]{1,0:T(8,128)(2,1)S(1)} %get-tuple-element.65.refs_0_), channel_id=1, source_target_pairs={{0,1},{1,0},{2,3},{3,2},{4,5},{5,4},{6,7},{7,6},{8,9},{9,8},{10,11... | collective-permute-start | bytes 1572872 | tf_op jit(solution)/shard_map/ppermute | solution.py:407
  375.8 36.6 %collective-permute-start.32 = (bf16[256,1024]{1,0:T(8,128)(2,1)}, bf16[256,1024]{1,0:T(8,128)(2,1)}, u32[]{:S(2)}, u32[]{:S(2)}) collective-permute-start(bf16[256,1024]{1,0:T(8,128)(2,1)} %collective-permute-done.31.refs_2_), channel_id=1, source_target_pairs={{0,1},{1,0},{2,3},{3,2},{4,5},{5,4},{6,7},{7,6},{8,9},{9,8},{10,11... | collective-permute-start | bytes 1572872 | tf_op jit(solution)/shard_map/ppermute | solution.py:407
  407.4 58.4 %all-to-all-start.8 = ((bf16[4,288,1024]{2,1,0:T(8,128)(2,1)}), bf16[4,288,1024]{2,1,0:T(8,128)(2,1)}, u32[]{:S(2)}, u32[]{:S(2)}) async-start(bf16[4,288,1024]{2,1,0:T(8,128)(2,1)} %bitcast.189), calls=%async_computation.8 | async-start | bytes 4718592 | tf_op jit(solution)/shard_map/all_to_all | solution.py:492
  436.3 25.9 %collective-permute-start.36 = (bf16[4,128,1024]{2,1,0:T(8,128)(2,1)}, bf16[4,128,1024]{2,1,0:T(8,128)(2,1)}, u32[]{:S(2)}, u32[]{:S(2)}) collective-permute-start(bf16[4,128,1024]{2,1,0:T(8,128)(2,1)} %get-tuple-element.71), channel_id=1, source_target_pairs={{0,16},{1,17},{2,18},{3,19},{4,20},{5,21},{6,22},{7,23},{8,24},{9,... | collective-permute-start | bytes 3145736 | tf_op jit(solution)/shard_map/ppermute | solution.py:407
  442.4 22.4 %collective-permute-start.34 = (bf16[1,1,256,1024]{3,2,1,0:T(8,128)(2,1)}, bf16[1,1,256,1024]{3,2,1,0:T(8,128)(2,1)S(1)}, u32[]{:S(2)}, u32[]{:S(2)}) collective-permute-start(bf16[1,1,256,1024]{3,2,1,0:T(8,128)(2,1)} %fusion.28), channel_id=1, source_target_pairs={{0,2},{1,3},{2,0},{3,1},{4,6},{5,7},{6,4},{7,5},{8,10},{9,11},{10,... | collective-permute-start | bytes 1572872 | tf_op jit(solution)/shard_map/ppermute | solution.py:407
  468.9 31.5 %all-to-all-start.9 = ((bf16[4,128,1024]{2,1,0:T(8,128)(2,1)}), bf16[4,128,1024]{2,1,0:T(8,128)(2,1)S(1)}, u32[]{:S(2)}, u32[]{:S(2)}) async-start(bf16[4,128,1024]{2,1,0:T(8,128)(2,1)} %add_convert_fusion.1), calls=%async_computation.9 | async-start | bytes 2097152 | tf_op jit(solution)/shard_map/all_to_all | solution.py:492
  475.4 7.5 %collective-permute-start.27 = (bf16[2,1,72,1024]{3,2,0,1:T(8,128)(2,1)}, bf16[2,1,72,1024]{3,2,0,1:T(8,128)(2,1)}, u32[]{:S(2)}, u32[]{:S(2)}) collective-permute-start(bf16[2,1,72,1024]{3,2,0,1:T(8,128)(2,1)} %get-tuple-element.163), channel_id=1, source_target_pairs={{0,1},{1,0},{2,3},{3,2},{4,5},{5,4},{6,7},{7,6},{8,9},{9,8},{10,11... | collective-permute-start | bytes 884744 | tf_op jit(solution)/shard_map/ppermute | solution.py:407
  484.2 9.5 %collective-permute-start.28 = (bf16[1,2,72,1024]{3,2,1,0:T(8,128)(2,1)S(1)}, bf16[1,2,72,1024]{3,2,1,0:T(8,128)(2,1)S(1)}, u32[]{:S(2)}, u32[]{:S(2)}) collective-permute-start(bf16[1,2,72,1024]{3,2,1,0:T(8,128)(2,1)S(1)} %get-tuple-element.161), channel_id=1, source_target_pairs={{0,2},{1,3},{2,0},{3,1},{4,6},{5,7},{6,4},{7,5},{8,10},{9,11},{10,... | collective-permute-start | bytes 884744 | tf_op jit(solution)/shard_map/ppermute | solution.py:407
  488.0 62.3 %collective-permute-start.35 = (bf16[256,1024]{1,0:T(8,128)(2,1)}, bf16[256,1024]{1,0:T(8,128)(2,1)}, u32[]{:S(2)}, u32[]{:S(2)}) collective-permute-start(bf16[256,1024]{1,0:T(8,128)(2,1)} %fusion.15), channel_id=1, source_target_pairs={{0,0},{1,4},{2,8},{3,12},{4,2},{5,6},{6,10},{7,14},{8,1},{9,5},{10... | collective-permute-start | bytes 1572872 | tf_op jit(solution)/shard_map/ppermute | solution.py:407
  495.1 57.3 %collective-permute-start.29 = (bf16[256,1024]{1,0:T(8,128)(2,1)}, bf16[256,1024]{1,0:T(8,128)(2,1)S(1)}, u32[]{:S(2)}, u32[]{:S(2)}) collective-permute-start(bf16[256,1024]{1,0:T(8,128)(2,1)} %fusion.23), channel_id=1, source_target_pairs={{0,0},{1,4},{2,8},{3,12},{4,2},{5,6},{6,10},{7,14},{8,1},{9,5},{10... | collective-permute-start | bytes 1572872 | tf_op jit(solution)/shard_map/ppermute | solution.py:407
  501.3 44.9 %all-to-all-start.11 = ((f32[32,1,256]{2,1,0:T(1,128)}), f32[32,1,256]{2,1,0:T(1,128)S(1)}, u32[]{:S(2)}, u32[]{:S(2)}) async-start(f32[32,1,256]{2,1,0:T(1,128)} %copy.135), calls=%async_computation.11 | async-start | bytes 65536 | tf_op jit(solution)/shard_map/all_to_all | solution.py:667
  546.2 14.8 %all-to-all-start.10 = ((bf16[4,32,1792]{2,1,0:T(8,128)(2,1)}), bf16[4,32,1792]{2,1,0:T(8,128)(2,1)S(1)}, u32[]{:S(2)}, u32[]{:S(2)}) async-start(bf16[4,32,1792]{2,1,0:T(8,128)(2,1)} %pad_maximum_fusion.3), calls=%async_computation.10 | async-start | bytes 917504 | tf_op jit(solution)/shard_map/all_to_all | solution.py:658
  552.4 8.0 %collective-permute-start.37 = (bf16[32,1024]{1,0:T(8,128)(2,1)S(1)}, bf16[32,1024]{1,0:T(8,128)(2,1)S(1)}, u32[]{:S(2)}, u32[]{:S(2)}) collective-permute-start(bf16[32,1024]{1,0:T(8,128)(2,1)S(1)} %bitcast.219), channel_id=1, source_target_pairs={{0,0},{1,8},{2,16},{3,24},{4,1},{5,9},{6,17},{7,25},{8,2},{9,10},{... | collective-permute-start | bytes 196616 | tf_op jit(solution)/shard_map/ppermute | solution.py:407
  (65 other events, 1031.3 us)
